TPU v7x, 512 devices: a whole 4x4x16 slice. The times are simulated.
512 devices in a mesh: dp: 128 (over z_lo, x, y), layer: 4 (over z_hi, core).
Axes of the slice: x: 4, y: 4, z: 16 (z_hi: 2, z_lo: 8; z = z_hi * 8 + z_lo), core: 2. Of those that a mesh axis runs over, the one named last changes fastest.
Arguments:
- train_grads: bfloat16 [4, 65536, 4096], P('layer', 'dp'), may hold values from -0.079589844 to 0.079589844
- query_grads: bfloat16 [4, 1024, 4096], P('layer', 'dp'), may hold values from -6 to 6
- left_factor: float32 [4, 64, 64], P('layer'), may hold values from -0.12 to 2.12, as said below
- right_factor: float32 [4, 64, 64], P('layer'), may hold values from -0.12 to 2.12, as said below
Outputs:
- scores: float32 [1024, 65536], P(None, ('dp', 'layer'))
Inputs may be any that keep to these rules, and one draw needn't show every extreme that they name: `left_factor`: symmetric; diagonal entries between 0.88 and 2.12, off-diagonal entries between -0.12 and 0.12. `right_factor`: symmetric; diagonal entries between 0.88 and 2.12, off-diagonal entries between -0.12 and 0.12.
All inputs are finite; a program needn't handle non-finite values.
Results may differ from a plain program's by a relative error of at most 0.0029.
Values may be sent and summed in bfloat16 or wider, within the bound.
No kernel may reach another device: no remote copies, remote signals or barrier semaphores. Data moves between devices by JAX's collectives and lax.ppermute only.
A program may use at most 128 MiB of HBM per device.

v0:
```python
import jax
import jax.numpy as jnp
from jax import lax
from jax.sharding import PartitionSpec as P


def condition(block, left, right):
    rows = block.shape[0]
    side = left.shape[0]
    grid = block.astype(jnp.float32).reshape(rows, side, side)
    inner = jnp.einsum("ab,qbc->qac", left, grid, precision=lax.Precision.HIGHEST)
    outer = jnp.einsum("qac,cd->qad", inner, right, precision=lax.Precision.HIGHEST)
    return outer.reshape(rows, side * side).astype(jnp.bfloat16)


def on_device(train_grads, query_grads, left_factor, right_factor):
    resident = train_grads[0]
    left = left_factor[0]
    right = right_factor[0]
    own_queries = query_grads[0]
    conditioned = condition(own_queries, left, right)
    partial_scores = lax.dot_general(
        lax.all_gather(conditioned, "dp", axis=0, tiled=True),
        resident,
        (((1,), (1,)), ((), ())),
        preferred_element_type=jnp.float32,
    )
    summed = lax.psum(partial_scores, "layer")
    share_width = resident.shape[0] // lax.axis_size("layer")
    return lax.dynamic_slice_in_dim(summed, lax.axis_index("layer") * share_width, share_width, 1)


def solution(mesh):
    return jax.shard_map(
        on_device,
        mesh=mesh,
        in_specs=(
            P("layer", "dp", None),
            P("layer", "dp", None),
            P("layer", None, None),
            P("layer", None, None),
        ),
        out_specs=P(None, ("dp", "layer")),
        check_vma=False,
    )
```

profile of v0, /device:TPU:1, one launch (start us, length us, event | category | flops | bytes accessed | tf_op | source)
XLA Modules:
  0.0 1186.2 jit_solution(17568010315629157070)
XLA Ops:
  6.5 0.0 copy-start
  6.5 0.0 all-gather.2.cloned.1.call-start
  6.5 1.0 reshape.6
  7.6 0.0 copy-done
  7.6 0.2 convolution_bitcast_fusion
  7.8 1.1 convolution_convert_fusion
  9.0 0.8 convert_element_type.8
  9.8 0.0 all-gather.2.cloned.1.call-update
  9.8 0.0 all-reduce.2.cloned.1.call-start
  9.8 895.5 %all-gather.2.cloned.1.call-done = bf16[1024,4096]{1,0:T(8,128)(2,1)} async-done(((bf16[8,4096]{1,0:T(8,128)(2,1)}), bf16[1024,4096]{1,0:T(8,128)(2,1)}) %all-gather.2.cloned.1.call-update) | async-done | bytes 8388624 | tf_op jit(solution)/shard_map/all_gather | solution.py:23
  905.3 10.4 fusion
  915.8 0.0 all-reduce.2.cloned.1.call-update
  915.8 261.8 %all-reduce.2.cloned.1.call-done = f32[1024,512]{1,0:T(8,128)} async-done(((f32[1024,512]{1,0:T(8,128)}), f32[1024,512]{1,0:T(8,128)}) %all-reduce.2.cloned.1.call-update) | async-done | bytes 2097168 | tf_op jit(solution)/shard_map/psum | solution.py:28
  1177.5 1.9 constant_dynamic-slice_fusion
Async XLA Ops:
  6.5 1.1 copy-start
  6.5 898.8 %all-gather.2.cloned.1.call-start = ((), (), s32[]{:S(2)}) async-start(), calls=%async_computation | async-start | bytes 8454144 | tf_op jit(solution)/shard_map/all_gather | solution.py:23
  9.8 1167.7 %all-reduce.2.cloned.1.call-start = ((), (), s32[]{:S(2)}) async-start(), calls=%async_computation.1 | async-start | bytes 4194304 | tf_op jit(solution)/shard_map/psum | solution.py:28
Sparse Core Ops, SparseCore 0:
  9.9 895.3 all-gather.1
  915.9 261.5 all-reduce.1
where the time goes:
time: 1190 us
  waiting for transfers between devices  1160 us (97%)
  between operations  13.4 us (1%)
    all_gather x1, waiting for transfers between devices, on_device(): lax.all_gather(conditioned, 'dp', axis=0, tiled=True)  895 us
    psum x1, waiting for transfers between devices, on_device(): summed = lax.psum(partial_scores, 'layer')  262 us
  transfers between devices with their start and end apart: 2, of which 2 were waited for; matrix products, arithmetic and copies ran while one was open for 0% of the time, Pallas kernels for 0%

commit v1 on v0

v1 whole, which is shorter than its diff:
```python
import jax
import jax.numpy as jnp
from jax import lax
from jax.experimental import pallas as pl
from jax.experimental.pallas import tpu as pltpu
from jax.sharding import Mesh
from jax.sharding import PartitionSpec as P

AXES = ("z", "x", "y", "half", "core")
SIZES = (8, 4, 4, 2, 2)
RING = 4


def condition(block, left, right):
    rows = block.shape[0]
    side = left.shape[0]
    grid = block.astype(jnp.float32).reshape(rows, side, side)
    inner = jnp.einsum("ab,qbc->qac", left, grid, precision=lax.Precision.HIGHEST)
    outer = jnp.einsum("qac,cd->qad", inner, right, precision=lax.Precision.HIGHEST)
    return outer.reshape(rows, side * side).astype(jnp.bfloat16)


def moved(piece, axis, step):
    rows, owners = piece
    came = lax.ppermute(rows, axis, [(i, (i + step) % RING) for i in range(RING)])
    dx, dy = (-step, 0) if axis == "x" else (0, -step)
    return came, [(z, (x + dx) % RING, (y + dy) % RING) for z, x, y in owners]


def part(piece, start, stop):
    rows, owners = piece
    size = rows.shape[0] // len(owners)
    return rows[start * size : stop * size], owners[start:stop]


def joined(pieces):
    return jnp.concatenate([p[0] for p in pieces], 0), [o for p in pieces for o in p[1]]


def round_ring(piece, axis):
    half = len(piece[1]) // 2
    low = moved(piece, axis, 1)
    high = moved(piece, axis, -1)
    far_low = moved(part(low, 0, half), axis, 1)
    far_high = moved(part(high, half, 2 * half), axis, -1)
    return low, high, joined([far_low, far_high])


def over_plane(piece, first, second):
    low, high, far = round_ring(piece, first)
    line = joined([piece, low, high, far])
    return (line,) + round_ring(line, second)


def flipped(piece, bit):
    rows, owners = piece
    came = lax.ppermute(rows, "z", [(i, i ^ bit) for i in range(SIZES[0])])
    return came, [(z ^ bit, x, y) for z, x, y in owners]


def place_kernel(place_ref, *refs):
    count = (len(refs) - 2) // 2
    out_ref, total = refs[-2], refs[-1]
    first = 0
    for own_ref, came_ref in zip(refs[:count], refs[count : 2 * count]):
        rows = own_ref.shape[0]
        total[first : first + rows, :] = own_ref[...] + came_ref[...].astype(jnp.float32)
        first += rows
    group = out_ref.shape[0] // place_ref.shape[0]

    def step(k, carry):
        source = pl.ds(pl.multiple_of(k * group, group), group)
        target = pl.ds(pl.multiple_of(place_ref[k] * group, group), group)
        out_ref[target, :] = total[source, :]
        return carry

    lax.fori_loop(0, place_ref.shape[0], step, 0, unroll=8)


def place(own, came, places):
    rows = sum(a.shape[0] for a in own)
    shape = (rows, own[0].shape[1])
    vmem = pl.BlockSpec(memory_space=pltpu.VMEM)
    return pl.pallas_call(
        place_kernel,
        out_shape=jax.ShapeDtypeStruct(shape, jnp.float32),
        in_specs=[pl.BlockSpec(memory_space=pltpu.SMEM)] + [vmem] * (2 * len(own)),
        out_specs=vmem,
        scratch_shapes=[pltpu.VMEM(shape, jnp.float32)],
        compiler_params=pltpu.CompilerParams(vmem_limit_bytes=8 * 2**20),
    )(places, *own, *came)


def on_device(train_grads, query_grads, left_factor, right_factor):
    half, core = lax.axis_index("half"), lax.axis_index("core")
    width = train_grads.shape[1] // 4
    shares = train_grads[0].reshape(4, width, train_grads.shape[2])
    order = [2 * half + core, 2 * (1 - half) + core, 2 * half + 1 - core, 2 * (1 - half) + 1 - core]
    resident = jnp.concatenate([lax.dynamic_index_in_dim(shares, k, 0, False) for k in order], 0)

    own = condition(query_grads[0], left_factor[0], right_factor[0]), [(0, 0, 0)]
    four = flipped(own, 4)
    pair = joined([own, four])
    two = flipped(pair, 2)
    one = flipped(joined([pair, two]), 1)
    a = over_plane(pair, "y", "x")
    b = over_plane(two, "x", "y")
    c = over_plane(part(one, 0, 2), "y", "x")
    d = over_plane(part(one, 2, 4), "x", "y")
    groups = [joined([a[0], b[0], a[1], a[2]]), joined([b[1], b[2], a[3], b[3]])]
    groups += [joined([c[0], d[0], c[1], c[2]]), joined([d[1], d[2], c[3], d[3]])]

    kept, arrived, owners = [], [], []
    for rows, of in groups:
        partial_scores = lax.dot_general(
            rows, resident, (((1,), (1,)), ((), ())), preferred_element_type=jnp.float32
        )
        other = lax.ppermute(partial_scores[:, 2 * width :], "core", [(0, 1), (1, 0)])
        both = partial_scores[:, : 2 * width] + other
        kept.append(both[:, :width])
        arrived.append(lax.ppermute(both[:, width:].astype(jnp.bfloat16), "half", [(0, 1), (1, 0)]))
        owners += of
    z, x, y = (lax.axis_index(name) for name in "zxy")
    flips, dx, dy = (jnp.array([o[i] for o in owners], jnp.int32) for i in range(3))
    places = ((z ^ flips) * 4 + (x + dx) % 4) * 4 + (y + dy) % 4
    return place(kept, arrived, places.astype(jnp.int32))


def solution(mesh):
    fine = Mesh(mesh.devices.reshape(SIZES), AXES)
    dp, layer = ("z", "x", "y"), ("half", "core")
    return jax.shard_map(
        on_device,
        mesh=fine,
        in_specs=(P(layer, dp, None), P(layer, dp, None), P(layer, None, None), P(layer, None, None)),
        out_specs=P(None, dp + layer),
        check_vma=False,
    )
```

time: 1190 us -> 228 us (0.19)
  waiting for transfers between devices: 1160 us -> 41.1 us
  starting transfers between devices: 0.04 us -> 168 us
  between operations: 13.4 us -> 1.28 us
    all_gather x1 -> x0, waiting for transfers between devices: 895 us -> none  [on_device(): lax.all_gather(conditioned, 'dp', axis=0, tiled=True)]
    psum x1 -> x0, waiting for transfers between devices: 262 us -> none  [on_device(): summed = lax.psum(partial_scores, 'layer')]
    ppermute x0 -> x43, starting transfers between devices: none -> 168 us  [the longest x32 97.3 us: moved(): lax.ppermute(rows, axis, [(i, (i + step) % RING) for i in range(RING)])]
    ppermute x0 -> x43, waiting for transfers between devices: none -> 41.1 us  [the longest x32 28.9 us: moved(): lax.ppermute(rows, axis, [(i, (i + step) % RING) for i in range(RING)])]
  transfers between devices with their start and end apart: 2 -> 43, of which waited for: 2 -> 11; matrix products, arithmetic and copies ran while one was open for 0% -> 5% of each run, Pallas kernels for 0% -> 0%
where the time goes in v1:
time: 228 us; the launch traced here: 226 us
  starting transfers between devices  168 us (74%)
  waiting for transfers between devices  41.1 us (18%)
  matrix products  6.5 us (3%)
  local copies, waits for them, and re-layouts  5.08 us (2%)
  other arithmetic  2.53 us (1%)
    ppermute x32, starting transfers between devices, moved(): lax.ppermute(rows, axis, [(i, (i + step) % RING) for i in range(RING)])  97.3 us
    ppermute x32, waiting for transfers between devices, moved(): lax.ppermute(rows, axis, [(i, (i + step) % RING) for i in range(RING)])  28.9 us
    ppermute x4, starting transfers between devices, on_device(): lax.ppermute(both[:, width:].astype(jnp.bfloat16), 'half', [(0, 1), (1, 0)])  28 us
    ppermute x4, starting transfers between devices, on_device(): lax.ppermute(partial_scores[:, 2 * width:], 'core', [(0, 1), (1, 0)])  23.2 us
    ppermute x3, starting transfers between devices, flipped(): came = lax.ppermute(rows, 'z', [(i, i ^ bit) for i in range(SIZES[0])])  19.9 us
    ppermute x4, waiting for transfers between devices, on_device(): lax.ppermute(both[:, width:].astype(jnp.bfloat16), 'half', [(0, 1), (1, 0)])  11.1 us
    dot_general x4, matrix products, on_device(): lax.dot_general(rows, resident, (((1,), (1,)), ((), ())), preferred_eleme...  5.14 us
  transfers between devices with their start and end apart: 43, of which 11 were waited for; matrix products, arithmetic and copies ran while one was open for 5% of the time, Pallas kernels for 0%

profile of v1, /device:TPU:1, one launch (start us, length us, event | category | flops | bytes accessed | tf_op | source)
XLA Modules:
  0.0 226.4 jit_solution(17071072768905693097)
XLA Ops:
  2.6 9.6 %collective-permute-start = (bf16[8,4096]{1,0:T(8,128)(2,1)S(1)}, bf16[8,4096]{1,0:T(8,128)(2,1)S(1)}, u32[]{:S(2)}, u32[]{:S(2)}) collective-permute-start(bf16[8,4096]{1,0:T(8,128)(2,1)S(1)} %convert_element_type.12), channel_id=1, source_target_pairs={{0,256},{64,320},{128,384},{192,448},{256,0},{320,64},{384,128},{4... | collective-permute-start | bytes 196616 | tf_op jit(solution)/shard_map/ppermute | solution.py:57
  12.3 2.7 %dynamic-slice_bitcast_fusion.3 = (bf16[128,4096]{1,0:T(8,128)(2,1)S(1)}, bf16[128,4096]{1,0:T(8,128)(2,1)S(1)}, bf16[128,4096]{1,0:T(8,128)(2,1)S(1)}, bf16[128,4096]{1,0:T(8,128)(2,1)S(1)}) fusion(bf16[4,128,4096]{2,1,0:T(8,128)(2,1)} %bitcast.29, s32[]{:T(128)S(6)} %select_n.26, s32[]{:T(128)S(6)} %select_n.29, s32[]{:T(128)S(6)} %select_n.28, s32[]{:T(128)S(6)} %select_n.27), kind=kLoop, calls=%fused_computation.6 | loop fusion | bytes 8388624 | tf_op jit(solution)/shard_map/jit(dynamic_index_in_dim)/squeeze | solution.py:99
  15.0 5.9 %collective-permute-start.5 = (bf16[16,4096]{1,0:T(8,128)(2,1)S(1)}, bf16[16,4096]{1,0:T(8,128)(2,1)S(1)}, u32[]{:S(2)}, u32[]{:S(2)}) collective-permute-start(bf16[16,4096]{1,0:T(8,128)(2,1)S(1)} %get-tuple-element.50), channel_id=1, source_target_pairs={{0,128},{64,192},{128,0},{192,64},{256,384},{320,448},{384,256},{4... | collective-permute-start | bytes 393224 | tf_op jit(solution)/shard_map/ppermute | solution.py:57
  20.9 3.2 %collective-permute-start.1 = (bf16[16,4096]{1,0:T(8,128)(2,1)S(1)}, bf16[16,4096]{1,0:T(8,128)(2,1)S(1)}, u32[]{:S(2)}, u32[]{:S(2)}) collective-permute-start(bf16[16,4096]{1,0:T(8,128)(2,1)S(1)} %get-tuple-element.50), channel_id=1, source_target_pairs={{0,4},{4,8},{8,12},{12,0},{1,5},{5,9},{9,13},{13,1},{2,6},{6,10},{... | collective-permute-start | bytes 393224 | tf_op jit(solution)/shard_map/ppermute | solution.py:25
  24.1 3.4 %collective-permute-start.2 = (bf16[16,4096]{1,0:T(8,128)(2,1)S(1)}, bf16[16,4096]{1,0:T(8,128)(2,1)S(1)}, u32[]{:S(2)}, u32[]{:S(2)}) collective-permute-start(bf16[16,4096]{1,0:T(8,128)(2,1)S(1)} %get-tuple-element.50), channel_id=1, source_target_pairs={{0,12},{4,0},{8,4},{12,8},{1,13},{5,1},{9,5},{13,9},{2,14},{6,2},{... | collective-permute-start | bytes 393224 | tf_op jit(solution)/shard_map/ppermute | solution.py:25
  27.5 2.3 %pad_maximum_fusion = bf16[512,4096]{1,0:T(8,128)(2,1)} fusion(bf16[128,4096]{1,0:T(8,128)(2,1)S(1)} %get-tuple-element.6, bf16[128,4096]{1,0:T(8,128)(2,1)S(1)} %get-tuple-element.7, bf16[128,4096]{1,0:T(8,128)(2,1)S(1)} %get-tuple-element.8, bf16[128,4096]{1,0:T(8,128)(2,1)S(1)} %get-tuple-element.5), kind=kLoop, calls=%fused_computation | loop fusion | flops 16777216 | bytes 8388608 | tf_op jit(solution)/shard_map/concatenate | solution.py:99
  29.8 1.9 collective-permute-start.3
  31.8 4.6 %collective-permute-start.4 = (bf16[8,4096]{1,0:T(8,128)(2,1)S(1)}, bf16[8,4096]{1,0:T(8,128)(2,1)S(1)}, u32[]{:S(2)}, u32[]{:S(2)}) collective-permute-start(bf16[8,4096]{1,0:T(8,128)(2,1)S(1)} %slice.141), channel_id=1, source_target_pairs={{0,12},{4,0},{8,4},{12,8},{1,13},{5,1},{9,5},{13,9},{2,14},{6,2},{... | collective-permute-start | bytes 196616 | tf_op jit(solution)/shard_map/ppermute | solution.py:25
  36.4 4.3 %collective-permute-start.20 = (bf16[32,4096]{1,0:T(8,128)(2,1)S(1)}, bf16[32,4096]{1,0:T(8,128)(2,1)S(1)}, u32[]{:S(2)}, u32[]{:S(2)}) collective-permute-start(bf16[32,4096]{1,0:T(8,128)(2,1)S(1)} %pad_maximum_fusion.1), channel_id=1, source_target_pairs={{0,64},{64,0},{128,192},{192,128},{256,320},{320,256},{384,448},{4... | collective-permute-start | bytes 786440 | tf_op jit(solution)/shard_map/ppermute | solution.py:57
  40.7 3.1 %collective-permute-start.6 = (bf16[16,4096]{1,0:T(8,128)(2,1)S(1)}, bf16[16,4096]{1,0:T(8,128)(2,1)S(1)}, u32[]{:S(2)}, u32[]{:S(2)}) collective-permute-start(bf16[16,4096]{1,0:T(8,128)(2,1)S(1)} %collective-permute-done.5), channel_id=1, source_target_pairs={{0,16},{16,32},{32,48},{48,0},{1,17},{17,33},{33,49},{49,1},{2,18}... | collective-permute-start | bytes 393224 | tf_op jit(solution)/shard_map/ppermute | solution.py:25
  43.9 3.4 %collective-permute-start.7 = (bf16[16,4096]{1,0:T(8,128)(2,1)S(1)}, bf16[16,4096]{1,0:T(8,128)(2,1)S(1)}, u32[]{:S(2)}, u32[]{:S(2)}) collective-permute-start(bf16[16,4096]{1,0:T(8,128)(2,1)S(1)} %collective-permute-done.5), channel_id=1, source_target_pairs={{0,48},{16,0},{32,16},{48,32},{1,49},{17,1},{33,17},{49,33},{2,50}... | collective-permute-start | bytes 393224 | tf_op jit(solution)/shard_map/ppermute | solution.py:25
  47.4 1.9 collective-permute-start.10
  49.3 4.6 %collective-permute-start.11 = (bf16[64,4096]{1,0:T(8,128)(2,1)S(1)}, bf16[64,4096]{1,0:T(8,128)(2,1)S(1)}, u32[]{:S(2)}, u32[]{:S(2)}) collective-permute-start(bf16[64,4096]{1,0:T(8,128)(2,1)S(1)} %get-tuple-element.44), channel_id=1, source_target_pairs={{0,48},{16,0},{32,16},{48,32},{1,49},{17,1},{33,17},{49,33},{2,50}... | collective-permute-start | bytes 1572872 | tf_op jit(solution)/shard_map/ppermute | solution.py:25
  53.9 1.9 collective-permute-start.8
  55.9 4.6 %collective-permute-start.9 = (bf16[8,4096]{1,0:T(8,128)(2,1)S(1)}, bf16[8,4096]{1,0:T(8,128)(2,1)S(1)}, u32[]{:S(2)}, u32[]{:S(2)}) collective-permute-start(bf16[8,4096]{1,0:T(8,128)(2,1)S(1)} %slice.143), channel_id=1, source_target_pairs={{0,48},{16,0},{32,16},{48,32},{1,49},{17,1},{33,17},{49,33},{2,50}... | collective-permute-start | bytes 196616 | tf_op jit(solution)/shard_map/ppermute | solution.py:25
  60.5 2.0 collective-permute-done.8
  62.6 1.9 collective-permute-start.21
  64.5 4.6 %collective-permute-start.22 = (bf16[16,4096]{1,0:T(8,128)(2,1)S(1)}, bf16[16,4096]{1,0:T(8,128)(2,1)S(1)}, u32[]{:S(2)}, u32[]{:S(2)}) collective-permute-start(bf16[16,4096]{1,0:T(8,128)(2,1)S(1)} %get-tuple-element.13), channel_id=1, source_target_pairs={{0,12},{4,0},{8,4},{12,8},{1,13},{5,1},{9,5},{13,9},{2,14},{6,2},{... | collective-permute-start | bytes 393224 | tf_op jit(solution)/shard_map/ppermute | solution.py:25
  69.1 1.9 collective-permute-start.25
  71.0 4.6 %collective-permute-start.26 = (bf16[16,4096]{1,0:T(8,128)(2,1)S(1)}, bf16[16,4096]{1,0:T(8,128)(2,1)S(1)}, u32[]{:S(2)}, u32[]{:S(2)}) collective-permute-start(bf16[16,4096]{1,0:T(8,128)(2,1)S(1)} %get-tuple-element.12), channel_id=1, source_target_pairs={{0,48},{16,0},{32,16},{48,32},{1,49},{17,1},{33,17},{49,33},{2,50}... | collective-permute-start | bytes 393224 | tf_op jit(solution)/shard_map/ppermute | solution.py:25
  75.7 1.9 collective-permute-start.23
  77.7 2.2 collective-permute-start.13
  79.9 4.6 %collective-permute-start.14 = (bf16[64,4096]{1,0:T(8,128)(2,1)S(1)}, bf16[64,4096]{1,0:T(8,128)(2,1)S(1)}, u32[]{:S(2)}, u32[]{:S(2)}) collective-permute-start(bf16[64,4096]{1,0:T(8,128)(2,1)S(1)} %get-tuple-element.40), channel_id=1, source_target_pairs={{0,12},{4,0},{8,4},{12,8},{1,13},{5,1},{9,5},{13,9},{2,14},{6,2},{... | collective-permute-start | bytes 1572872 | tf_op jit(solution)/shard_map/ppermute | solution.py:25
  84.5 3.4 %collective-permute-start.24 = (bf16[8,4096]{1,0:T(8,128)(2,1)S(1)}, bf16[8,4096]{1,0:T(8,128)(2,1)S(1)}, u32[]{:S(2)}, u32[]{:S(2)}) collective-permute-start(bf16[8,4096]{1,0:T(8,128)(2,1)S(1)} %slice.156), channel_id=1, source_target_pairs={{0,12},{4,0},{8,4},{12,8},{1,13},{5,1},{9,5},{13,9},{2,14},{6,2},{... | collective-permute-start | bytes 196616 | tf_op jit(solution)/shard_map/ppermute | solution.py:25
  87.9 4.1 %collective-permute-done.24 = bf16[8,4096]{1,0:T(8,128)(2,1)S(1)} collective-permute-done((bf16[8,4096]{1,0:T(8,128)(2,1)S(1)}, bf16[8,4096]{1,0:T(8,128)(2,1)S(1)}, u32[]{:S(2)}, u32[]{:S(2)}) %collective-permute-start.24) | collective-permute-done | bytes 65568 | tf_op jit(solution)/shard_map/ppermute | solution.py:25
  93.9 4.2 %collective-permute-done.27 = bf16[8,4096]{1,0:T(8,128)(2,1)S(1)} collective-permute-done((bf16[8,4096]{1,0:T(8,128)(2,1)S(1)}, bf16[8,4096]{1,0:T(8,128)(2,1)S(1)}, u32[]{:S(2)}, u32[]{:S(2)}) %collective-permute-start.27) | collective-permute-done | bytes 65568 | tf_op jit(solution)/shard_map/ppermute | solution.py:25
  100.1 3.1 %collective-permute-done.28 = bf16[8,4096]{1,0:T(8,128)(2,1)S(1)} collective-permute-done((bf16[8,4096]{1,0:T(8,128)(2,1)S(1)}, bf16[8,4096]{1,0:T(8,128)(2,1)S(1)}, u32[]{:S(2)}, u32[]{:S(2)}) %collective-permute-start.28) | collective-permute-done | bytes 65568 | tf_op jit(solution)/shard_map/ppermute | solution.py:25
  105.1 4.6 %collective-permute-start.30 = (bf16[64,4096]{1,0:T(8,128)(2,1)S(1)}, bf16[64,4096]{1,0:T(8,128)(2,1)S(1)}, u32[]{:S(2)}, u32[]{:S(2)}) collective-permute-start(bf16[64,4096]{1,0:T(8,128)(2,1)S(1)} %get-tuple-element.36), channel_id=1, source_target_pairs={{0,48},{16,0},{32,16},{48,32},{1,49},{17,1},{33,17},{49,33},{2,50}... | collective-permute-start | bytes 1572872 | tf_op jit(solution)/shard_map/ppermute | solution.py:25
  109.7 3.5 %collective-permute-start.32 = (bf16[64,4096]{1,0:T(8,128)(2,1)S(1)}, bf16[64,4096]{1,0:T(8,128)(2,1)S(1)}, u32[]{:S(2)}, u32[]{:S(2)}) collective-permute-start(bf16[64,4096]{1,0:T(8,128)(2,1)S(1)} %get-tuple-element.32), channel_id=1, source_target_pairs={{0,4},{4,8},{8,12},{12,0},{1,5},{5,9},{9,13},{13,1},{2,6},{6,10},{... | collective-permute-start | bytes 1572872 | tf_op jit(solution)/shard_map/ppermute | solution.py:25
  114.7 3.7 %collective-permute-start.33 = (bf16[64,4096]{1,0:T(8,128)(2,1)S(1)}, bf16[64,4096]{1,0:T(8,128)(2,1)S(1)}, u32[]{:S(2)}, u32[]{:S(2)}) collective-permute-start(bf16[64,4096]{1,0:T(8,128)(2,1)S(1)} %get-tuple-element.32), channel_id=1, source_target_pairs={{0,12},{4,0},{8,4},{12,8},{1,13},{5,1},{9,5},{13,9},{2,14},{6,2},{... | collective-permute-start | bytes 1572872 | tf_op jit(solution)/shard_map/ppermute | solution.py:25
  118.5 1.9 collective-permute-start.15
  120.5 6.6 %collective-permute-done.15 = bf16[32,4096]{1,0:T(8,128)(2,1)S(1)} collective-permute-done((bf16[32,4096]{1,0:T(8,128)(2,1)S(1)}, bf16[32,4096]{1,0:T(8,128)(2,1)S(1)}, u32[]{:S(2)}, u32[]{:S(2)}) %collective-permute-start.15) | collective-permute-done | bytes 262176 | tf_op jit(solution)/shard_map/ppermute | solution.py:25
  129.1 5.5 %collective-permute-done.16 = bf16[32,4096]{1,0:T(8,128)(2,1)S(1)} collective-permute-done((bf16[32,4096]{1,0:T(8,128)(2,1)S(1)}, bf16[32,4096]{1,0:T(8,128)(2,1)S(1)}, u32[]{:S(2)}, u32[]{:S(2)}) %collective-permute-start.16) | collective-permute-done | bytes 262176 | tf_op jit(solution)/shard_map/ppermute | solution.py:25
  134.5 13.5 %collective-permute-start.12 = (f32[256,256]{1,0:T(8,128)S(1)}, f32[256,256]{1,0:T(8,128)S(1)}, u32[]{:S(2)}, u32[]{:S(2)}) collective-permute-start(f32[256,256]{1,0:T(8,128)S(1)} %slice.145), channel_id=1, source_target_pairs={{0,1},{1,0},{2,3},{3,2},{4,5},{5,4},{6,7},{7,6},{8,9},{9,8},{10,11... | collective-permute-start | bytes 786440 | tf_op jit(solution)/shard_map/ppermute | solution.py:118
  151.1 4.6 %collective-permute-start.18 = (bf16[32,4096]{1,0:T(8,128)(2,1)S(1)}, bf16[32,4096]{1,0:T(8,128)(2,1)S(1)}, u32[]{:S(2)}, u32[]{:S(2)}) collective-permute-start(bf16[32,4096]{1,0:T(8,128)(2,1)S(1)} %slice.150), channel_id=1, source_target_pairs={{0,12},{4,0},{8,4},{12,8},{1,13},{5,1},{9,5},{13,9},{2,14},{6,2},{... | collective-permute-start | bytes 786440 | tf_op jit(solution)/shard_map/ppermute | solution.py:25
  155.7 11.3 %collective-permute-start.39 = (bf16[256,128]{1,0:T(8,128)(2,1)S(1)}, bf16[256,128]{1,0:T(8,128)(2,1)S(1)}, u32[]{:S(2)}, u32[]{:S(2)}) collective-permute-start(bf16[256,128]{1,0:T(8,128)(2,1)S(1)} %slice.189), channel_id=1, source_target_pairs={{0,2},{2,0},{1,3},{3,1},{4,6},{6,4},{5,7},{7,5},{8,10},{10,8},{9,1... | collective-permute-start | bytes 196616 | tf_op jit(solution)/shard_map/ppermute | solution.py:121
  168.5 3.1 %collective-permute-start.31 = (f32[256,256]{1,0:T(8,128)S(1)}, f32[256,256]{1,0:T(8,128)S(1)}, u32[]{:S(2)}, u32[]{:S(2)}) collective-permute-start(f32[256,256]{1,0:T(8,128)S(1)} %slice.161), channel_id=1, source_target_pairs={{0,1},{1,0},{2,3},{3,2},{4,5},{5,4},{6,7},{7,6},{8,9},{9,8},{10,11... | collective-permute-start | bytes 786440 | tf_op jit(solution)/shard_map/ppermute | solution.py:118
  171.7 1.9 collective-permute-start.34
  173.7 4.6 %collective-permute-start.35 = (bf16[32,4096]{1,0:T(8,128)(2,1)S(1)}, bf16[32,4096]{1,0:T(8,128)(2,1)S(1)}, u32[]{:S(2)}, u32[]{:S(2)}) collective-permute-start(bf16[32,4096]{1,0:T(8,128)(2,1)S(1)} %slice.164), channel_id=1, source_target_pairs={{0,48},{16,0},{32,16},{48,32},{1,49},{17,1},{33,17},{49,33},{2,50}... | collective-permute-start | bytes 786440 | tf_op jit(solution)/shard_map/ppermute | solution.py:25
  182.7 3.5 %collective-permute-start.37 = (bf16[32,4096]{1,0:T(8,128)(2,1)S(1)}, bf16[32,4096]{1,0:T(8,128)(2,1)S(1)}, u32[]{:S(2)}, u32[]{:S(2)}) collective-permute-start(bf16[32,4096]{1,0:T(8,128)(2,1)S(1)} %slice.166), channel_id=1, source_target_pairs={{0,12},{4,0},{8,4},{12,8},{1,13},{5,1},{9,5},{13,9},{2,14},{6,2},{... | collective-permute-start | bytes 786440 | tf_op jit(solution)/shard_map/ppermute | solution.py:25
  186.2 3.0 %collective-permute-start.19 = (f32[256,256]{1,0:T(8,128)S(1)}, f32[256,256]{1,0:T(8,128)S(1)}, u32[]{:S(2)}, u32[]{:S(2)}) collective-permute-start(f32[256,256]{1,0:T(8,128)S(1)} %slice.152), channel_id=1, source_target_pairs={{0,1},{1,0},{2,3},{3,2},{4,5},{5,4},{6,7},{7,6},{8,9},{9,8},{10,11... | collective-permute-start | bytes 786440 | tf_op jit(solution)/shard_map/ppermute | solution.py:118
  189.3 2.3 %collective-permute-done.37 = bf16[32,4096]{1,0:T(8,128)(2,1)S(1)} collective-permute-done((bf16[32,4096]{1,0:T(8,128)(2,1)S(1)}, bf16[32,4096]{1,0:T(8,128)(2,1)S(1)}, u32[]{:S(2)}, u32[]{:S(2)}) %collective-permute-start.37) | collective-permute-done | bytes 262176 | tf_op jit(solution)/shard_map/ppermute | solution.py:25
  193.0 3.6 %collective-permute-start.38 = (f32[256,256]{1,0:T(8,128)S(1)}, f32[256,256]{1,0:T(8,128)S(1)}, u32[]{:S(2)}, u32[]{:S(2)}) collective-permute-start(f32[256,256]{1,0:T(8,128)S(1)} %slice.168), channel_id=1, source_target_pairs={{0,1},{1,0},{2,3},{3,2},{4,5},{5,4},{6,7},{7,6},{8,9},{9,8},{10,11... | collective-permute-start | bytes 786440 | tf_op jit(solution)/shard_map/ppermute | solution.py:118
  196.7 2.7 %collective-permute-start.41 = (bf16[256,128]{1,0:T(8,128)(2,1)S(1)}, bf16[256,128]{1,0:T(8,128)(2,1)S(1)}, u32[]{:S(2)}, u32[]{:S(2)}) collective-permute-start(bf16[256,128]{1,0:T(8,128)(2,1)S(1)} %slice.187), channel_id=1, source_target_pairs={{0,2},{2,0},{1,3},{3,1},{4,6},{6,4},{5,7},{7,5},{8,10},{10,8},{9,1... | collective-permute-start | bytes 196616 | tf_op jit(solution)/shard_map/ppermute | solution.py:121
  199.5 11.3 %collective-permute-start.40 = (bf16[256,128]{1,0:T(8,128)(2,1)S(1)}, bf16[256,128]{1,0:T(8,128)(2,1)S(1)}, u32[]{:S(2)}, u32[]{:S(2)}) collective-permute-start(bf16[256,128]{1,0:T(8,128)(2,1)S(1)} %slice.188), channel_id=1, source_target_pairs={{0,2},{2,0},{1,3},{3,1},{4,6},{6,4},{5,7},{7,5},{8,10},{10,8},{9,1... | collective-permute-start | bytes 196616 | tf_op jit(solution)/shard_map/ppermute | solution.py:121
  210.8 2.7 %collective-permute-start.42 = (bf16[256,128]{1,0:T(8,128)(2,1)S(1)}, bf16[256,128]{1,0:T(8,128)(2,1)S(1)}, u32[]{:S(2)}, u32[]{:S(2)}) collective-permute-start(bf16[256,128]{1,0:T(8,128)(2,1)S(1)} %slice.186), channel_id=1, source_target_pairs={{0,2},{2,0},{1,3},{3,1},{4,6},{6,4},{5,7},{7,5},{8,10},{10,8},{9,1... | collective-permute-start | bytes 196616 | tf_op jit(solution)/shard_map/ppermute | solution.py:121
  213.7 3.0 %collective-permute-done.40.refs_5_ = bf16[256,128]{1,0:T(8,128)(2,1)S(1)} collective-permute-done((bf16[256,128]{1,0:T(8,128)(2,1)S(1)}, bf16[256,128]{1,0:T(8,128)(2,1)S(1)}, u32[]{:S(2)}, u32[]{:S(2)}) %collective-permute-start.40) | collective-permute-done | bytes 65568 | tf_op jit(solution)/shard_map/ppermute | solution.py:121
  216.7 8.1 %collective-permute-done.42.refs_7_ = bf16[256,128]{1,0:T(8,128)(2,1)S(1)} collective-permute-done((bf16[256,128]{1,0:T(8,128)(2,1)S(1)}, bf16[256,128]{1,0:T(8,128)(2,1)S(1)}, u32[]{:S(2)}, u32[]{:S(2)}) %collective-permute-start.42) | collective-permute-done | bytes 65568 | tf_op jit(solution)/shard_map/ppermute | solution.py:121
  (130 shorter events, 24.5 us)
Async XLA Ops:
  0.0 1.0 copy-start
  2.6 12.4 %collective-permute-start = (bf16[8,4096]{1,0:T(8,128)(2,1)S(1)}, bf16[8,4096]{1,0:T(8,128)(2,1)S(1)}, u32[]{:S(2)}, u32[]{:S(2)}) collective-permute-start(bf16[8,4096]{1,0:T(8,128)(2,1)S(1)} %convert_element_type.12), channel_id=1, source_target_pairs={{0,256},{64,320},{128,384},{192,448},{256,0},{320,64},{384,128},{4... | collective-permute-start | bytes 196616 | tf_op jit(solution)/shard_map/ppermute | solution.py:57
  15.0 21.4 %collective-permute-start.5 = (bf16[16,4096]{1,0:T(8,128)(2,1)S(1)}, bf16[16,4096]{1,0:T(8,128)(2,1)S(1)}, u32[]{:S(2)}, u32[]{:S(2)}) collective-permute-start(bf16[16,4096]{1,0:T(8,128)(2,1)S(1)} %get-tuple-element.50), channel_id=1, source_target_pairs={{0,128},{64,192},{128,0},{192,64},{256,384},{320,448},{384,256},{4... | collective-permute-start | bytes 393224 | tf_op jit(solution)/shard_map/ppermute | solution.py:57
  20.9 8.9 %collective-permute-start.1 = (bf16[16,4096]{1,0:T(8,128)(2,1)S(1)}, bf16[16,4096]{1,0:T(8,128)(2,1)S(1)}, u32[]{:S(2)}, u32[]{:S(2)}) collective-permute-start(bf16[16,4096]{1,0:T(8,128)(2,1)S(1)} %get-tuple-element.50), channel_id=1, source_target_pairs={{0,4},{4,8},{8,12},{12,0},{1,5},{5,9},{9,13},{13,1},{2,6},{6,10},{... | collective-permute-start | bytes 393224 | tf_op jit(solution)/shard_map/ppermute | solution.py:25
  24.1 7.7 %collective-permute-start.2 = (bf16[16,4096]{1,0:T(8,128)(2,1)S(1)}, bf16[16,4096]{1,0:T(8,128)(2,1)S(1)}, u32[]{:S(2)}, u32[]{:S(2)}) collective-permute-start(bf16[16,4096]{1,0:T(8,128)(2,1)S(1)} %get-tuple-element.50), channel_id=1, source_target_pairs={{0,12},{4,0},{8,4},{12,8},{1,13},{5,1},{9,5},{13,9},{2,14},{6,2},{... | collective-permute-start | bytes 393224 | tf_op jit(solution)/shard_map/ppermute | solution.py:25
  29.8 17.5 %collective-permute-start.3 = (bf16[8,4096]{1,0:T(8,128)(2,1)S(1)}, bf16[8,4096]{1,0:T(8,128)(2,1)S(1)}, u32[]{:S(2)}, u32[]{:S(2)}) collective-permute-start(bf16[8,4096]{1,0:T(8,128)(2,1)S(1)} %slice.140), channel_id=1, source_target_pairs={{0,4},{4,8},{8,12},{12,0},{1,5},{5,9},{9,13},{13,1},{2,6},{6,10},{... | collective-permute-start | bytes 196616 | tf_op jit(solution)/shard_map/ppermute | solution.py:25
  31.8 15.5 %collective-permute-start.4 = (bf16[8,4096]{1,0:T(8,128)(2,1)S(1)}, bf16[8,4096]{1,0:T(8,128)(2,1)S(1)}, u32[]{:S(2)}, u32[]{:S(2)}) collective-permute-start(bf16[8,4096]{1,0:T(8,128)(2,1)S(1)} %slice.141), channel_id=1, source_target_pairs={{0,12},{4,0},{8,4},{12,8},{1,13},{5,1},{9,5},{13,9},{2,14},{6,2},{... | collective-permute-start | bytes 196616 | tf_op jit(solution)/shard_map/ppermute | solution.py:25
  36.4 26.1 %collective-permute-start.20 = (bf16[32,4096]{1,0:T(8,128)(2,1)S(1)}, bf16[32,4096]{1,0:T(8,128)(2,1)S(1)}, u32[]{:S(2)}, u32[]{:S(2)}) collective-permute-start(bf16[32,4096]{1,0:T(8,128)(2,1)S(1)} %pad_maximum_fusion.1), channel_id=1, source_target_pairs={{0,64},{64,0},{128,192},{192,128},{256,320},{320,256},{384,448},{4... | collective-permute-start | bytes 786440 | tf_op jit(solution)/shard_map/ppermute | solution.py:57
  40.7 13.2 %collective-permute-start.6 = (bf16[16,4096]{1,0:T(8,128)(2,1)S(1)}, bf16[16,4096]{1,0:T(8,128)(2,1)S(1)}, u32[]{:S(2)}, u32[]{:S(2)}) collective-permute-start(bf16[16,4096]{1,0:T(8,128)(2,1)S(1)} %collective-permute-done.5), channel_id=1, source_target_pairs={{0,16},{16,32},{32,48},{48,0},{1,17},{17,33},{33,49},{49,1},{2,18}... | collective-permute-start | bytes 393224 | tf_op jit(solution)/shard_map/ppermute | solution.py:25
  43.9 12.0 %collective-permute-start.7 = (bf16[16,4096]{1,0:T(8,128)(2,1)S(1)}, bf16[16,4096]{1,0:T(8,128)(2,1)S(1)}, u32[]{:S(2)}, u32[]{:S(2)}) collective-permute-start(bf16[16,4096]{1,0:T(8,128)(2,1)S(1)} %collective-permute-done.5), channel_id=1, source_target_pairs={{0,48},{16,0},{32,16},{48,32},{1,49},{17,1},{33,17},{49,33},{2,50}... | collective-permute-start | bytes 393224 | tf_op jit(solution)/shard_map/ppermute | solution.py:25
  47.4 57.7 %collective-permute-start.10 = (bf16[64,4096]{1,0:T(8,128)(2,1)S(1)}, bf16[64,4096]{1,0:T(8,128)(2,1)S(1)}, u32[]{:S(2)}, u32[]{:S(2)}) collective-permute-start(bf16[64,4096]{1,0:T(8,128)(2,1)S(1)} %get-tuple-element.44), channel_id=1, source_target_pairs={{0,16},{16,32},{32,48},{48,0},{1,17},{17,33},{33,49},{49,1},{2,18}... | collective-permute-start | bytes 1572872 | tf_op jit(solution)/shard_map/ppermute | solution.py:25
  49.3 60.4 %collective-permute-start.11 = (bf16[64,4096]{1,0:T(8,128)(2,1)S(1)}, bf16[64,4096]{1,0:T(8,128)(2,1)S(1)}, u32[]{:S(2)}, u32[]{:S(2)}) collective-permute-start(bf16[64,4096]{1,0:T(8,128)(2,1)S(1)} %get-tuple-element.44), channel_id=1, source_target_pairs={{0,48},{16,0},{32,16},{48,32},{1,49},{17,1},{33,17},{49,33},{2,50}... | collective-permute-start | bytes 1572872 | tf_op jit(solution)/shard_map/ppermute | solution.py:25
  53.9 8.6 %collective-permute-start.8 = (bf16[8,4096]{1,0:T(8,128)(2,1)S(1)}, bf16[8,4096]{1,0:T(8,128)(2,1)S(1)}, u32[]{:S(2)}, u32[]{:S(2)}) collective-permute-start(bf16[8,4096]{1,0:T(8,128)(2,1)S(1)} %slice.142), channel_id=1, source_target_pairs={{0,16},{16,32},{32,48},{48,0},{1,17},{17,33},{33,49},{49,1},{2,18}... | collective-permute-start | bytes 196616 | tf_op jit(solution)/shard_map/ppermute | solution.py:25
  55.9 8.6 %collective-permute-start.9 = (bf16[8,4096]{1,0:T(8,128)(2,1)S(1)}, bf16[8,4096]{1,0:T(8,128)(2,1)S(1)}, u32[]{:S(2)}, u32[]{:S(2)}) collective-permute-start(bf16[8,4096]{1,0:T(8,128)(2,1)S(1)} %slice.143), channel_id=1, source_target_pairs={{0,48},{16,0},{32,16},{48,32},{1,49},{17,1},{33,17},{49,33},{2,50}... | collective-permute-start | bytes 196616 | tf_op jit(solution)/shard_map/ppermute | solution.py:25
  62.6 8.5 %collective-permute-start.21 = (bf16[16,4096]{1,0:T(8,128)(2,1)S(1)}, bf16[16,4096]{1,0:T(8,128)(2,1)S(1)}, u32[]{:S(2)}, u32[]{:S(2)}) collective-permute-start(bf16[16,4096]{1,0:T(8,128)(2,1)S(1)} %get-tuple-element.13), channel_id=1, source_target_pairs={{0,4},{4,8},{8,12},{12,0},{1,5},{5,9},{9,13},{13,1},{2,6},{6,10},{... | collective-permute-start | bytes 393224 | tf_op jit(solution)/shard_map/ppermute | solution.py:25
  64.5 11.1 %collective-permute-start.22 = (bf16[16,4096]{1,0:T(8,128)(2,1)S(1)}, bf16[16,4096]{1,0:T(8,128)(2,1)S(1)}, u32[]{:S(2)}, u32[]{:S(2)}) collective-permute-start(bf16[16,4096]{1,0:T(8,128)(2,1)S(1)} %get-tuple-element.13), channel_id=1, source_target_pairs={{0,12},{4,0},{8,4},{12,8},{1,13},{5,1},{9,5},{13,9},{2,14},{6,2},{... | collective-permute-start | bytes 393224 | tf_op jit(solution)/shard_map/ppermute | solution.py:25
  69.1 8.5 %collective-permute-start.25 = (bf16[16,4096]{1,0:T(8,128)(2,1)S(1)}, bf16[16,4096]{1,0:T(8,128)(2,1)S(1)}, u32[]{:S(2)}, u32[]{:S(2)}) collective-permute-start(bf16[16,4096]{1,0:T(8,128)(2,1)S(1)} %get-tuple-element.12), channel_id=1, source_target_pairs={{0,16},{16,32},{32,48},{48,0},{1,17},{17,33},{33,49},{49,1},{2,18}... | collective-permute-start | bytes 393224 | tf_op jit(solution)/shard_map/ppermute | solution.py:25
  71.0 8.8 %collective-permute-start.26 = (bf16[16,4096]{1,0:T(8,128)(2,1)S(1)}, bf16[16,4096]{1,0:T(8,128)(2,1)S(1)}, u32[]{:S(2)}, u32[]{:S(2)}) collective-permute-start(bf16[16,4096]{1,0:T(8,128)(2,1)S(1)} %get-tuple-element.12), channel_id=1, source_target_pairs={{0,48},{16,0},{32,16},{48,32},{1,49},{17,1},{33,17},{49,33},{2,50}... | collective-permute-start | bytes 393224 | tf_op jit(solution)/shard_map/ppermute | solution.py:25
  75.7 8.8 %collective-permute-start.23 = (bf16[8,4096]{1,0:T(8,128)(2,1)S(1)}, bf16[8,4096]{1,0:T(8,128)(2,1)S(1)}, u32[]{:S(2)}, u32[]{:S(2)}) collective-permute-start(bf16[8,4096]{1,0:T(8,128)(2,1)S(1)} %slice.155), channel_id=1, source_target_pairs={{0,4},{4,8},{8,12},{12,0},{1,5},{5,9},{9,13},{13,1},{2,6},{6,10},{... | collective-permute-start | bytes 196616 | tf_op jit(solution)/shard_map/ppermute | solution.py:25
  77.7 35.6 %copy-start.1 = (bf16[512,4096]{1,0:T(8,128)(2,1)S(1)}, bf16[512,4096]{1,0:T(8,128)(2,1)}, u32[]{:S(2)}) copy-start(bf16[512,4096]{1,0:T(8,128)(2,1)} %pad_maximum_fusion) | copy-start | bytes 12582916
  77.7 37.0 %collective-permute-start.13 = (bf16[64,4096]{1,0:T(8,128)(2,1)S(1)}, bf16[64,4096]{1,0:T(8,128)(2,1)S(1)}, u32[]{:S(2)}, u32[]{:S(2)}) collective-permute-start(bf16[64,4096]{1,0:T(8,128)(2,1)S(1)} %get-tuple-element.40), channel_id=1, source_target_pairs={{0,4},{4,8},{8,12},{12,0},{1,5},{5,9},{9,13},{13,1},{2,6},{6,10},{... | collective-permute-start | bytes 1572872 | tf_op jit(solution)/shard_map/ppermute | solution.py:25
  79.9 38.6 %collective-permute-start.14 = (bf16[64,4096]{1,0:T(8,128)(2,1)S(1)}, bf16[64,4096]{1,0:T(8,128)(2,1)S(1)}, u32[]{:S(2)}, u32[]{:S(2)}) collective-permute-start(bf16[64,4096]{1,0:T(8,128)(2,1)S(1)} %get-tuple-element.40), channel_id=1, source_target_pairs={{0,12},{4,0},{8,4},{12,8},{1,13},{5,1},{9,5},{13,9},{2,14},{6,2},{... | collective-permute-start | bytes 1572872 | tf_op jit(solution)/shard_map/ppermute | solution.py:25
  84.5 7.4 %collective-permute-start.24 = (bf16[8,4096]{1,0:T(8,128)(2,1)S(1)}, bf16[8,4096]{1,0:T(8,128)(2,1)S(1)}, u32[]{:S(2)}, u32[]{:S(2)}) collective-permute-start(bf16[8,4096]{1,0:T(8,128)(2,1)S(1)} %slice.156), channel_id=1, source_target_pairs={{0,12},{4,0},{8,4},{12,8},{1,13},{5,1},{9,5},{13,9},{2,14},{6,2},{... | collective-permute-start | bytes 196616 | tf_op jit(solution)/shard_map/ppermute | solution.py:25
  91.9 6.2 %collective-permute-start.27 = (bf16[8,4096]{1,0:T(8,128)(2,1)S(1)}, bf16[8,4096]{1,0:T(8,128)(2,1)S(1)}, u32[]{:S(2)}, u32[]{:S(2)}) collective-permute-start(bf16[8,4096]{1,0:T(8,128)(2,1)S(1)} %slice.158), channel_id=1, source_target_pairs={{0,16},{16,32},{32,48},{48,0},{1,17},{17,33},{33,49},{49,1},{2,18}... | collective-permute-start | bytes 196616 | tf_op jit(solution)/shard_map/ppermute | solution.py:25
  98.1 5.0 %collective-permute-start.28 = (bf16[8,4096]{1,0:T(8,128)(2,1)S(1)}, bf16[8,4096]{1,0:T(8,128)(2,1)S(1)}, u32[]{:S(2)}, u32[]{:S(2)}) collective-permute-start(bf16[8,4096]{1,0:T(8,128)(2,1)S(1)} %slice.159), channel_id=1, source_target_pairs={{0,48},{16,0},{32,16},{48,32},{1,49},{17,1},{33,17},{49,33},{2,50}... | collective-permute-start | bytes 196616 | tf_op jit(solution)/shard_map/ppermute | solution.py:25
  103.1 48.0 %collective-permute-start.29 = (bf16[64,4096]{1,0:T(8,128)(2,1)S(1)}, bf16[64,4096]{1,0:T(8,128)(2,1)S(1)}, u32[]{:S(2)}, u32[]{:S(2)}) collective-permute-start(bf16[64,4096]{1,0:T(8,128)(2,1)S(1)} %get-tuple-element.36), channel_id=1, source_target_pairs={{0,16},{16,32},{32,48},{48,0},{1,17},{17,33},{33,49},{49,1},{2,18}... | collective-permute-start | bytes 1572872 | tf_op jit(solution)/shard_map/ppermute | solution.py:25
  105.1 50.6 %collective-permute-start.30 = (bf16[64,4096]{1,0:T(8,128)(2,1)S(1)}, bf16[64,4096]{1,0:T(8,128)(2,1)S(1)}, u32[]{:S(2)}, u32[]{:S(2)}) collective-permute-start(bf16[64,4096]{1,0:T(8,128)(2,1)S(1)} %get-tuple-element.36), channel_id=1, source_target_pairs={{0,48},{16,0},{32,16},{48,32},{1,49},{17,1},{33,17},{49,33},{2,50}... | collective-permute-start | bytes 1572872 | tf_op jit(solution)/shard_map/ppermute | solution.py:25
  109.7 58.7 %collective-permute-start.32 = (bf16[64,4096]{1,0:T(8,128)(2,1)S(1)}, bf16[64,4096]{1,0:T(8,128)(2,1)S(1)}, u32[]{:S(2)}, u32[]{:S(2)}) collective-permute-start(bf16[64,4096]{1,0:T(8,128)(2,1)S(1)} %get-tuple-element.32), channel_id=1, source_target_pairs={{0,4},{4,8},{8,12},{12,0},{1,5},{5,9},{9,13},{13,1},{2,6},{6,10},{... | collective-permute-start | bytes 1572872 | tf_op jit(solution)/shard_map/ppermute | solution.py:25
  114.7 57.0 %collective-permute-start.33 = (bf16[64,4096]{1,0:T(8,128)(2,1)S(1)}, bf16[64,4096]{1,0:T(8,128)(2,1)S(1)}, u32[]{:S(2)}, u32[]{:S(2)}) collective-permute-start(bf16[64,4096]{1,0:T(8,128)(2,1)S(1)} %get-tuple-element.32), channel_id=1, source_target_pairs={{0,12},{4,0},{8,4},{12,8},{1,13},{5,1},{9,5},{13,9},{2,14},{6,2},{... | collective-permute-start | bytes 1572872 | tf_op jit(solution)/shard_map/ppermute | solution.py:25
  118.5 8.6 %collective-permute-start.15 = (bf16[32,4096]{1,0:T(8,128)(2,1)S(1)}, bf16[32,4096]{1,0:T(8,128)(2,1)S(1)}, u32[]{:S(2)}, u32[]{:S(2)}) collective-permute-start(bf16[32,4096]{1,0:T(8,128)(2,1)S(1)} %slice.147), channel_id=1, source_target_pairs={{0,16},{16,32},{32,48},{48,0},{1,17},{17,33},{33,49},{49,1},{2,18}... | collective-permute-start | bytes 786440 | tf_op jit(solution)/shard_map/ppermute | solution.py:25
  127.1 7.4 %collective-permute-start.16 = (bf16[32,4096]{1,0:T(8,128)(2,1)S(1)}, bf16[32,4096]{1,0:T(8,128)(2,1)S(1)}, u32[]{:S(2)}, u32[]{:S(2)}) collective-permute-start(bf16[32,4096]{1,0:T(8,128)(2,1)S(1)} %slice.148), channel_id=1, source_target_pairs={{0,48},{16,0},{32,16},{48,32},{1,49},{17,1},{33,17},{49,33},{2,50}... | collective-permute-start | bytes 786440 | tf_op jit(solution)/shard_map/ppermute | solution.py:25
  134.5 14.6 %collective-permute-start.12 = (f32[256,256]{1,0:T(8,128)S(1)}, f32[256,256]{1,0:T(8,128)S(1)}, u32[]{:S(2)}, u32[]{:S(2)}) collective-permute-start(f32[256,256]{1,0:T(8,128)S(1)} %slice.145), channel_id=1, source_target_pairs={{0,1},{1,0},{2,3},{3,2},{4,5},{5,4},{6,7},{7,6},{8,9},{9,8},{10,11... | collective-permute-start | bytes 786440 | tf_op jit(solution)/shard_map/ppermute | solution.py:118
  149.1 24.6 %collective-permute-start.17 = (bf16[32,4096]{1,0:T(8,128)(2,1)S(1)}, bf16[32,4096]{1,0:T(8,128)(2,1)S(1)}, u32[]{:S(2)}, u32[]{:S(2)}) collective-permute-start(bf16[32,4096]{1,0:T(8,128)(2,1)S(1)} %slice.149), channel_id=1, source_target_pairs={{0,4},{4,8},{8,12},{12,0},{1,5},{5,9},{9,13},{13,1},{2,6},{6,10},{... | collective-permute-start | bytes 786440 | tf_op jit(solution)/shard_map/ppermute | solution.py:25
  151.1 27.2 %collective-permute-start.18 = (bf16[32,4096]{1,0:T(8,128)(2,1)S(1)}, bf16[32,4096]{1,0:T(8,128)(2,1)S(1)}, u32[]{:S(2)}, u32[]{:S(2)}) collective-permute-start(bf16[32,4096]{1,0:T(8,128)(2,1)S(1)} %slice.150), channel_id=1, source_target_pairs={{0,12},{4,0},{8,4},{12,8},{1,13},{5,1},{9,5},{13,9},{2,14},{6,2},{... | collective-permute-start | bytes 786440 | tf_op jit(solution)/shard_map/ppermute | solution.py:25
  155.7 57.9 %collective-permute-start.39 = (bf16[256,128]{1,0:T(8,128)(2,1)S(1)}, bf16[256,128]{1,0:T(8,128)(2,1)S(1)}, u32[]{:S(2)}, u32[]{:S(2)}) collective-permute-start(bf16[256,128]{1,0:T(8,128)(2,1)S(1)} %slice.189), channel_id=1, source_target_pairs={{0,2},{2,0},{1,3},{3,1},{4,6},{6,4},{5,7},{7,5},{8,10},{10,8},{9,1... | collective-permute-start | bytes 196616 | tf_op jit(solution)/shard_map/ppermute | solution.py:121
  168.5 28.1 %collective-permute-start.31 = (f32[256,256]{1,0:T(8,128)S(1)}, f32[256,256]{1,0:T(8,128)S(1)}, u32[]{:S(2)}, u32[]{:S(2)}) collective-permute-start(f32[256,256]{1,0:T(8,128)S(1)} %slice.161), channel_id=1, source_target_pairs={{0,1},{1,0},{2,3},{3,2},{4,5},{5,4},{6,7},{7,6},{8,9},{9,8},{10,11... | collective-permute-start | bytes 786440 | tf_op jit(solution)/shard_map/ppermute | solution.py:118
  171.7 11.0 %collective-permute-start.34 = (bf16[32,4096]{1,0:T(8,128)(2,1)S(1)}, bf16[32,4096]{1,0:T(8,128)(2,1)S(1)}, u32[]{:S(2)}, u32[]{:S(2)}) collective-permute-start(bf16[32,4096]{1,0:T(8,128)(2,1)S(1)} %slice.163), channel_id=1, source_target_pairs={{0,16},{16,32},{32,48},{48,0},{1,17},{17,33},{33,49},{49,1},{2,18}... | collective-permute-start | bytes 786440 | tf_op jit(solution)/shard_map/ppermute | solution.py:25
  173.7 12.5 %collective-permute-start.35 = (bf16[32,4096]{1,0:T(8,128)(2,1)S(1)}, bf16[32,4096]{1,0:T(8,128)(2,1)S(1)}, u32[]{:S(2)}, u32[]{:S(2)}) collective-permute-start(bf16[32,4096]{1,0:T(8,128)(2,1)S(1)} %slice.164), channel_id=1, source_target_pairs={{0,48},{16,0},{32,16},{48,32},{1,49},{17,1},{33,17},{49,33},{2,50}... | collective-permute-start | bytes 786440 | tf_op jit(solution)/shard_map/ppermute | solution.py:25
  178.3 11.0 %collective-permute-start.36 = (bf16[32,4096]{1,0:T(8,128)(2,1)S(1)}, bf16[32,4096]{1,0:T(8,128)(2,1)S(1)}, u32[]{:S(2)}, u32[]{:S(2)}) collective-permute-start(bf16[32,4096]{1,0:T(8,128)(2,1)S(1)} %slice.165), channel_id=1, source_target_pairs={{0,4},{4,8},{8,12},{12,0},{1,5},{5,9},{9,13},{13,1},{2,6},{6,10},{... | collective-permute-start | bytes 786440 | tf_op jit(solution)/shard_map/ppermute | solution.py:25
  182.7 8.9 %collective-permute-start.37 = (bf16[32,4096]{1,0:T(8,128)(2,1)S(1)}, bf16[32,4096]{1,0:T(8,128)(2,1)S(1)}, u32[]{:S(2)}, u32[]{:S(2)}) collective-permute-start(bf16[32,4096]{1,0:T(8,128)(2,1)S(1)} %slice.166), channel_id=1, source_target_pairs={{0,12},{4,0},{8,4},{12,8},{1,13},{5,1},{9,5},{13,9},{2,14},{6,2},{... | collective-permute-start | bytes 786440 | tf_op jit(solution)/shard_map/ppermute | solution.py:25
  186.2 13.2 %collective-permute-start.19 = (f32[256,256]{1,0:T(8,128)S(1)}, f32[256,256]{1,0:T(8,128)S(1)}, u32[]{:S(2)}, u32[]{:S(2)}) collective-permute-start(f32[256,256]{1,0:T(8,128)S(1)} %slice.152), channel_id=1, source_target_pairs={{0,1},{1,0},{2,3},{3,2},{4,5},{5,4},{6,7},{7,6},{8,9},{9,8},{10,11... | collective-permute-start | bytes 786440 | tf_op jit(solution)/shard_map/ppermute | solution.py:118
  192.9 20.6 %copy-start.2 = (s32[128]{0:T(128)S(1)}, s32[128]{0:T(128)}, u32[]{:S(2)}) copy-start(s32[128]{0:T(128)} %constant.64.clone) | copy-start | bytes 1540
  192.9 20.6 %copy-start.3 = (s32[128]{0:T(128)S(1)}, s32[128]{0:T(128)}, u32[]{:S(2)}) copy-start(s32[128]{0:T(128)} %constant.63.clone) | copy-start | bytes 1540
  193.0 20.6 %copy-start.4 = (s32[128]{0:T(128)S(1)}, s32[128]{0:T(128)}, u32[]{:S(2)}) copy-start(s32[128]{0:T(128)} %constant.62.clone) | copy-start | bytes 1540
  193.0 17.8 %collective-permute-start.38 = (f32[256,256]{1,0:T(8,128)S(1)}, f32[256,256]{1,0:T(8,128)S(1)}, u32[]{:S(2)}, u32[]{:S(2)}) collective-permute-start(f32[256,256]{1,0:T(8,128)S(1)} %slice.168), channel_id=1, source_target_pairs={{0,1},{1,0},{2,3},{3,2},{4,5},{5,4},{6,7},{7,6},{8,9},{9,8},{10,11... | collective-permute-start | bytes 786440 | tf_op jit(solution)/shard_map/ppermute | solution.py:118
  196.7 17.0 %collective-permute-start.41 = (bf16[256,128]{1,0:T(8,128)(2,1)S(1)}, bf16[256,128]{1,0:T(8,128)(2,1)S(1)}, u32[]{:S(2)}, u32[]{:S(2)}) collective-permute-start(bf16[256,128]{1,0:T(8,128)(2,1)S(1)} %slice.187), channel_id=1, source_target_pairs={{0,2},{2,0},{1,3},{3,1},{4,6},{6,4},{5,7},{7,5},{8,10},{10,8},{9,1... | collective-permute-start | bytes 196616 | tf_op jit(solution)/shard_map/ppermute | solution.py:121
  199.5 17.2 %collective-permute-start.40 = (bf16[256,128]{1,0:T(8,128)(2,1)S(1)}, bf16[256,128]{1,0:T(8,128)(2,1)S(1)}, u32[]{:S(2)}, u32[]{:S(2)}) collective-permute-start(bf16[256,128]{1,0:T(8,128)(2,1)S(1)} %slice.188), channel_id=1, source_target_pairs={{0,2},{2,0},{1,3},{3,1},{4,6},{6,4},{5,7},{7,5},{8,10},{10,8},{9,1... | collective-permute-start | bytes 196616 | tf_op jit(solution)/shard_map/ppermute | solution.py:121
  210.8 14.0 %collective-permute-start.42 = (bf16[256,128]{1,0:T(8,128)(2,1)S(1)}, bf16[256,128]{1,0:T(8,128)(2,1)S(1)}, u32[]{:S(2)}, u32[]{:S(2)}) collective-permute-start(bf16[256,128]{1,0:T(8,128)(2,1)S(1)} %slice.186), channel_id=1, source_target_pairs={{0,2},{2,0},{1,3},{3,1},{4,6},{6,4},{5,7},{7,5},{8,10},{10,8},{9,1... | collective-permute-start | bytes 196616 | tf_op jit(solution)/shard_map/ppermute | solution.py:121

commit v2 on v1

--- a/solution.py
+++ b/solution.py
@@ -8,7 +8,6 @@
 
 AXES = ("z", "x", "y", "half", "core")
 SIZES = (8, 4, 4, 2, 2)
-RING = 4
 
 
 def condition(block, left, right):
@@ -20,42 +19,14 @@
     return outer.reshape(rows, side * side).astype(jnp.bfloat16)
 
 
-def moved(piece, axis, step):
-    rows, owners = piece
-    came = lax.ppermute(rows, axis, [(i, (i + step) % RING) for i in range(RING)])
-    dx, dy = (-step, 0) if axis == "x" else (0, -step)
-    return came, [(z, (x + dx) % RING, (y + dy) % RING) for z, x, y in owners]
-
-
-def part(piece, start, stop):
-    rows, owners = piece
-    size = rows.shape[0] // len(owners)
-    return rows[start * size : stop * size], owners[start:stop]
-
-
 def joined(pieces):
     return jnp.concatenate([p[0] for p in pieces], 0), [o for p in pieces for o in p[1]]
-
-
-def round_ring(piece, axis):
-    half = len(piece[1]) // 2
-    low = moved(piece, axis, 1)
-    high = moved(piece, axis, -1)
-    far_low = moved(part(low, 0, half), axis, 1)
-    far_high = moved(part(high, half, 2 * half), axis, -1)
-    return low, high, joined([far_low, far_high])
-
-
-def over_plane(piece, first, second):
-    low, high, far = round_ring(piece, first)
-    line = joined([piece, low, high, far])
-    return (line,) + round_ring(line, second)
 
 
 def flipped(piece, bit):
     rows, owners = piece
     came = lax.ppermute(rows, "z", [(i, i ^ bit) for i in range(SIZES[0])])
-    return came, [(z ^ bit, x, y) for z, x, y in owners]
+    return came, [z ^ bit for z in owners]
 
 
 def place_kernel(place_ref, *refs):
@@ -98,20 +69,15 @@
     order = [2 * half + core, 2 * (1 - half) + core, 2 * half + 1 - core, 2 * (1 - half) + 1 - core]
     resident = jnp.concatenate([lax.dynamic_index_in_dim(shares, k, 0, False) for k in order], 0)
 
-    own = condition(query_grads[0], left_factor[0], right_factor[0]), [(0, 0, 0)]
-    four = flipped(own, 4)
-    pair = joined([own, four])
-    two = flipped(pair, 2)
-    one = flipped(joined([pair, two]), 1)
-    a = over_plane(pair, "y", "x")
-    b = over_plane(two, "x", "y")
-    c = over_plane(part(one, 0, 2), "y", "x")
-    d = over_plane(part(one, 2, 4), "x", "y")
-    groups = [joined([a[0], b[0], a[1], a[2]]), joined([b[1], b[2], a[3], b[3]])]
-    groups += [joined([c[0], d[0], c[1], c[2]]), joined([d[1], d[2], c[3], d[3]])]
+    own = condition(query_grads[0], left_factor[0], right_factor[0]), [0]
+    pair = joined([own, flipped(own, 4)])
+    four = joined([pair, flipped(pair, 2)])
+    column, flips = joined([four, flipped(four, 1)])
+    plane = lax.all_gather(column, ("x", "y"), axis=0, tiled=True)
+    groups = [plane[: plane.shape[0] // 4], plane[plane.shape[0] // 4 :]]
 
-    kept, arrived, owners = [], [], []
-    for rows, of in groups:
+    kept, arrived = [], []
+    for rows in groups:
         partial_scores = lax.dot_general(
             rows, resident, (((1,), (1,)), ((), ())), preferred_element_type=jnp.float32
         )
@@ -119,11 +85,10 @@
         both = partial_scores[:, : 2 * width] + other
         kept.append(both[:, :width])
         arrived.append(lax.ppermute(both[:, width:].astype(jnp.bfloat16), "half", [(0, 1), (1, 0)]))
-        owners += of
-    z, x, y = (lax.axis_index(name) for name in "zxy")
-    flips, dx, dy = (jnp.array([o[i] for o in owners], jnp.int32) for i in range(3))
-    places = ((z ^ flips) * 4 + (x + dx) % 4) * 4 + (y + dy) % 4
-    return place(kept, arrived, places.astype(jnp.int32))
+    z = lax.axis_index("z") ^ jnp.array(flips, jnp.int32)
+    in_plane = lax.broadcasted_iota(jnp.int32, (16, 1), 0)
+    places = (z[None, :] * 16 + in_plane).reshape(-1)
+    return place(kept, arrived, places)
 
 
 def solution(mesh):

time: 228 us -> 204 us (0.89)
  starting transfers between devices: 168 us -> 42.3 us
  waiting for transfers between devices: 41.1 us -> 124 us
  between operations: 1.28 us -> 13.6 us
  matrix products: 6.5 us -> 11.6 us
    ppermute x32 -> x0, starting transfers between devices: 97.3 us -> none  [moved(): lax.ppermute(rows, axis, [(i, (i + step) % RING) for i in range(RING)])]
    all_gather x0 -> x1, waiting for transfers between devices: none -> 88.6 us  [on_device(): plane = lax.all_gather(column, ('x', 'y'), axis=0, tiled=True)]
    ppermute x32 -> x0, waiting for transfers between devices: 28.9 us -> none  [moved(): lax.ppermute(rows, axis, [(i, (i + step) % RING) for i in range(RING)])]
    ppermute x4 -> x2, starting transfers between devices: 23.2 us -> 4.5 us  [on_device(): lax.ppermute(partial_scores[:, 2 * width:], 'core', [(0, 1), (1, 0)])]
    ppermute x4 -> x2, waiting for transfers between devices: 11.1 us -> 24.9 us  [on_device(): lax.ppermute(both[:, width:].astype(jnp.bfloat16), 'half', [(0, 1), (1, 0)])]
    ppermute x4 -> x2, starting transfers between devices: 28 us -> 14.4 us  [on_device(): lax.ppermute(both[:, width:].astype(jnp.bfloat16), 'half', [(0, 1), (1, 0)])]
    ppermute x3, waiting for transfers between devices: 0.01 us -> 9.1 us  [flipped(): came = lax.ppermute(rows, 'z', [(i, i ^ bit) for i in range(SIZES[0])])]
    dot_general x4 -> x2, matrix products: 5.14 us -> 10.3 us  [on_device(): lax.dot_general(rows, resident, (((1,), (1,)), ((), ())), preferred_eleme...]
  transfers between devices with their start and end apart: 43 -> 8, of which waited for: 11 -> 6; matrix products, arithmetic and copies ran while one was open for 5% -> 5% of each run, Pallas kernels for 0% -> 0%
where the time goes in v2:
time: 204 us; the launch traced here: 203 us
  waiting for transfers between devices  124 us (61%)
  starting transfers between devices  42.3 us (21%)
  between operations  13.6 us (7%)
  matrix products  11.6 us (6%)
  local copies, waits for them, and re-layouts  6.93 us (3%)
  other arithmetic  3.12 us (2%)
    all_gather x1, waiting for transfers between devices, on_device(): plane = lax.all_gather(column, ('x', 'y'), axis=0, tiled=True)  88.6 us
    ppermute x2, waiting for transfers between devices, on_device(): lax.ppermute(both[:, width:].astype(jnp.bfloat16), 'half', [(0, 1), (1, 0)])  24.9 us
    ppermute x3, starting transfers between devices, flipped(): came = lax.ppermute(rows, 'z', [(i, i ^ bit) for i in range(SIZES[0])])  23.4 us
    ppermute x2, starting transfers between devices, on_device(): lax.ppermute(both[:, width:].astype(jnp.bfloat16), 'half', [(0, 1), (1, 0)])  14.4 us
    dot_general x2, matrix products, on_device(): lax.dot_general(rows, resident, (((1,), (1,)), ((), ())), preferred_eleme...  10.3 us
    ppermute x3, waiting for transfers between devices, flipped(): came = lax.ppermute(rows, 'z', [(i, i ^ bit) for i in range(SIZES[0])])  9.1 us
    ppermute x2, starting transfers between devices, on_device(): lax.ppermute(partial_scores[:, 2 * width:], 'core', [(0, 1), (1, 0)])  4.5 us
  transfers between devices with their start and end apart: 8, of which 6 were waited for; matrix products, arithmetic and copies ran while one was open for 5% of the time, Pallas kernels for 0%

profile of v2, /device:TPU:1, one launch (start us, length us, event | category | flops | bytes accessed | tf_op | source)
XLA Modules:
  0.0 203.3 jit_solution(7078503112182067939)
XLA Ops:
  6.5 0.0 copy-start
  6.5 0.0 all-gather.2.cloned.1.call-start
  6.5 1.0 reshape.12
  7.6 0.0 copy-done
  7.6 0.2 convolution_bitcast_fusion
  7.8 1.1 convolution_convert_fusion
  9.0 0.2 convert_element_type.10
  9.1 9.6 %collective-permute-start = (bf16[8,4096]{1,0:T(8,128)(2,1)S(1)}, bf16[8,4096]{1,0:T(8,128)(2,1)S(1)}, u32[]{:S(2)}, u32[]{:S(2)}) collective-permute-start(bf16[8,4096]{1,0:T(8,128)(2,1)S(1)} %convert_element_type.10), channel_id=1, source_target_pairs={{0,256},{64,320},{128,384},{192,448},{256,0},{320,64},{384,128},{4... | collective-permute-start | bytes 196616 | tf_op jit(solution)/shard_map/ppermute | solution.py:28
  18.8 1.6 collective-permute-done
  20.5 7.0 %collective-permute-start.1 = (bf16[16,4096]{1,0:T(8,128)(2,1)S(1)}, bf16[16,4096]{1,0:T(8,128)(2,1)S(1)}, u32[]{:S(2)}, u32[]{:S(2)}) collective-permute-start(bf16[16,4096]{1,0:T(8,128)(2,1)S(1)} %pad_maximum_fusion.5), channel_id=1, source_target_pairs={{0,128},{64,192},{128,0},{192,64},{256,384},{320,448},{384,256},{4... | collective-permute-start | bytes 393224 | tf_op jit(solution)/shard_map/ppermute | solution.py:28
  27.5 2.3 %collective-permute-done.1 = bf16[16,4096]{1,0:T(8,128)(2,1)S(1)} collective-permute-done((bf16[16,4096]{1,0:T(8,128)(2,1)S(1)}, bf16[16,4096]{1,0:T(8,128)(2,1)S(1)}, u32[]{:S(2)}, u32[]{:S(2)}) %collective-permute-start.1) | collective-permute-done | bytes 131104 | tf_op jit(solution)/shard_map/ppermute | solution.py:28
  29.8 6.7 %collective-permute-start.2 = (bf16[32,4096]{1,0:T(8,128)(2,1)S(1)}, bf16[32,4096]{1,0:T(8,128)(2,1)S(1)}, u32[]{:S(2)}, u32[]{:S(2)}) collective-permute-start(bf16[32,4096]{1,0:T(8,128)(2,1)S(1)} %pad_maximum_fusion.4), channel_id=1, source_target_pairs={{0,64},{64,0},{128,192},{192,128},{256,320},{320,256},{384,448},{4... | collective-permute-start | bytes 786440 | tf_op jit(solution)/shard_map/ppermute | solution.py:28
  36.6 5.1 %collective-permute-done.2 = bf16[32,4096]{1,0:T(8,128)(2,1)S(1)} collective-permute-done((bf16[32,4096]{1,0:T(8,128)(2,1)S(1)}, bf16[32,4096]{1,0:T(8,128)(2,1)S(1)}, u32[]{:S(2)}, u32[]{:S(2)}) %collective-permute-start.2) | collective-permute-done | bytes 262176 | tf_op jit(solution)/shard_map/ppermute | solution.py:28
  41.7 0.8 pad_maximum_fusion.3
  42.5 0.0 all-gather.2.cloned.1.call-update
  42.5 4.0 %dynamic-slice_bitcast_fusion.3 = (bf16[128,4096]{1,0:T(8,128)(2,1)S(1)}, bf16[128,4096]{1,0:T(8,128)(2,1)}, bf16[128,4096]{1,0:T(8,128)(2,1)}, bf16[128,4096]{1,0:T(8,128)(2,1)}) fusion(bf16[4,128,4096]{2,1,0:T(8,128)(2,1)} %bitcast.21, s32[]{:T(128)S(6)} %select_n.13, s32[]{:T(128)S(6)} %select_n.16, s32[]{:T(128)S(6)} %select_n.15, s32[]{:T(128)S(6)} %select_n.14), kind=kLoop, calls=%fused_computation.10 | loop fusion | bytes 8388624 | tf_op jit(solution)/shard_map/jit(dynamic_index_in_dim)/squeeze | solution.py:70
  46.6 88.6 %all-gather.2.cloned.1.call-done = bf16[1024,4096]{1,0:T(8,128)(2,1)} async-done(((bf16[64,4096]{1,0:T(8,128)(2,1)}), bf16[1024,4096]{1,0:T(8,128)(2,1)}) %all-gather.2.cloned.1.call-update) | async-done | bytes 8388624 | tf_op jit(solution)/shard_map/all_gather | solution.py:76
  135.2 0.0 copy-start.1
  135.2 0.0 copy-start.2
  135.2 0.0 copy-start.3
  135.2 7.2 %fusion = f32[768,512]{1,0:T(8,128)S(1)} fusion(bf16[1024,4096]{1,0:T(8,128)(2,1)} %all-gather.2.cloned.1.call-done, bf16[128,4096]{1,0:T(8,128)(2,1)} %get-tuple-element.6, bf16[128,4096]{1,0:T(8,128)(2,1)} %get-tuple-element.7, bf16[128,4096]{1,0:T(8,128)(2,1)} %get-tuple-element.8, bf16[128,4096]{1,0:T(8,128)(2,1)S(1)} %get-tuple-element.5), kind=kOutput, calls=%fused_computation | convolution fusion | flops 3238002688 | bytes 12058624 | tf_op jit(solution)/shard_map/dot_general | solution.py:81
  142.4 0.1 slice.48
  142.5 0.0 copy-start.5
  142.5 2.6 %collective-permute-start.4 = (f32[768,256]{1,0:T(8,128)S(1)}, f32[768,256]{1,0:T(8,128)}, u32[]{:S(2)}, u32[]{:S(2)}) collective-permute-start(f32[768,256]{1,0:T(8,128)S(1)} %slice.48), channel_id=1, source_target_pairs={{0,1},{1,0},{2,3},{3,2},{4,5},{5,4},{6,7},{7,6},{8,9},{9,8},{10,11... | collective-permute-start | bytes 2359304 | tf_op jit(solution)/shard_map/ppermute | solution.py:84
  145.1 0.0 copy-done.1
  145.1 0.0 copy-done.2
  145.1 0.0 copy-done.3
  145.1 3.1 %fusion.2 = f32[256,512]{1,0:T(8,128)S(1)} fusion(bf16[1024,4096]{1,0:T(8,128)(2,1)} %all-gather.2.cloned.1.call-done, bf16[128,4096]{1,0:T(8,128)(2,1)S(1)} %copy-done.1, bf16[128,4096]{1,0:T(8,128)(2,1)S(1)} %copy-done.2, bf16[128,4096]{1,0:T(8,128)(2,1)S(1)} %copy-done.3, bf16[128,4096]{1,0:T(8,128)(2,1)S(1)} %get-tuple-element.5), kind=kOutput, calls=%fused_computation.3 | convolution fusion | flops 1090519040 | bytes 6815744 | tf_op jit(solution)/shard_map/dot_general | solution.py:81
  148.2 0.0 copy-start.4
  148.2 0.8 copy-done.4
  149.0 1.9 collective-permute-start.3
  150.9 0.0 copy-done.5
  150.9 1.5 collective-permute-done.3
  152.4 1.0 slice_add_fusion.1
  153.4 0.6 slice.61
  154.0 12.5 %collective-permute-start.5 = (bf16[256,128]{1,0:T(8,128)(2,1)}, bf16[256,128]{1,0:T(8,128)(2,1)S(1)}, u32[]{:S(2)}, u32[]{:S(2)}) collective-permute-start(bf16[256,128]{1,0:T(8,128)(2,1)} %slice.61), channel_id=1, source_target_pairs={{0,2},{2,0},{1,3},{3,1},{4,6},{6,4},{5,7},{7,5},{8,10},{10,8},{9,1... | collective-permute-start | bytes 196616 | tf_op jit(solution)/shard_map/ppermute | solution.py:87
  166.6 0.0 collective-permute-done.4
  166.6 1.3 slice_add_fusion
  167.9 1.9 collective-permute-start.6
  169.8 0.1 add.51.place_ref
  170.0 0.0 collective-permute-done.5.refs_2_
  170.0 24.9 %collective-permute-done.6.refs_3_ = bf16[768,128]{1,0:T(8,128)(2,1)S(1)} collective-permute-done((bf16[768,128]{1,0:T(8,128)(2,1)S(1)}, bf16[768,128]{1,0:T(8,128)(2,1)S(1)}, u32[]{:S(2)}, u32[]{:S(2)}) %collective-permute-start.6) | collective-permute-done | bytes 196640 | tf_op jit(solution)/shard_map/ppermute | solution.py:87
  194.9 1.6 shard_map.55
  (8 shorter events, 0.1 us)
Async XLA Ops:
  6.5 1.1 copy-start
  6.5 128.6 %all-gather.2.cloned.1.call-start = ((), (), s32[]{:S(2)}) async-start(), calls=%async_computation | async-start | bytes 8912896 | tf_op jit(solution)/shard_map/all_gather | solution.py:76
  9.1 11.3 %collective-permute-start = (bf16[8,4096]{1,0:T(8,128)(2,1)S(1)}, bf16[8,4096]{1,0:T(8,128)(2,1)S(1)}, u32[]{:S(2)}, u32[]{:S(2)}) collective-permute-start(bf16[8,4096]{1,0:T(8,128)(2,1)S(1)} %convert_element_type.10), channel_id=1, source_target_pairs={{0,256},{64,320},{128,384},{192,448},{256,0},{320,64},{384,128},{4... | collective-permute-start | bytes 196616 | tf_op jit(solution)/shard_map/ppermute | solution.py:28
  20.5 9.3 %collective-permute-start.1 = (bf16[16,4096]{1,0:T(8,128)(2,1)S(1)}, bf16[16,4096]{1,0:T(8,128)(2,1)S(1)}, u32[]{:S(2)}, u32[]{:S(2)}) collective-permute-start(bf16[16,4096]{1,0:T(8,128)(2,1)S(1)} %pad_maximum_fusion.5), channel_id=1, source_target_pairs={{0,128},{64,192},{128,0},{192,64},{256,384},{320,448},{384,256},{4... | collective-permute-start | bytes 393224 | tf_op jit(solution)/shard_map/ppermute | solution.py:28
  29.8 11.9 %collective-permute-start.2 = (bf16[32,4096]{1,0:T(8,128)(2,1)S(1)}, bf16[32,4096]{1,0:T(8,128)(2,1)S(1)}, u32[]{:S(2)}, u32[]{:S(2)}) collective-permute-start(bf16[32,4096]{1,0:T(8,128)(2,1)S(1)} %pad_maximum_fusion.4), channel_id=1, source_target_pairs={{0,64},{64,0},{128,192},{192,128},{256,320},{320,256},{384,448},{4... | collective-permute-start | bytes 786440 | tf_op jit(solution)/shard_map/ppermute | solution.py:28
  135.2 9.9 %copy-start.1 = (bf16[128,4096]{1,0:T(8,128)(2,1)S(1)}, bf16[128,4096]{1,0:T(8,128)(2,1)}, u32[]{:S(2)}) copy-start(bf16[128,4096]{1,0:T(8,128)(2,1)} %get-tuple-element.6) | copy-start | bytes 3145732
  135.2 9.9 %copy-start.2 = (bf16[128,4096]{1,0:T(8,128)(2,1)S(1)}, bf16[128,4096]{1,0:T(8,128)(2,1)}, u32[]{:S(2)}) copy-start(bf16[128,4096]{1,0:T(8,128)(2,1)} %get-tuple-element.7) | copy-start | bytes 3145732
  135.2 9.9 %copy-start.3 = (bf16[128,4096]{1,0:T(8,128)(2,1)S(1)}, bf16[128,4096]{1,0:T(8,128)(2,1)}, u32[]{:S(2)}) copy-start(bf16[128,4096]{1,0:T(8,128)(2,1)} %get-tuple-element.8) | copy-start | bytes 3145732
  142.5 8.5 %copy-start.5 = (s32[8]{0:T(128)S(1)}, s32[8]{0:T(128)}, u32[]{:S(2)}) copy-start(s32[8]{0:T(128)} %constant.32.clone) | copy-start | bytes 100
  142.5 24.1 %collective-permute-start.4 = (f32[768,256]{1,0:T(8,128)S(1)}, f32[768,256]{1,0:T(8,128)}, u32[]{:S(2)}, u32[]{:S(2)}) collective-permute-start(f32[768,256]{1,0:T(8,128)S(1)} %slice.48), channel_id=1, source_target_pairs={{0,1},{1,0},{2,3},{3,2},{4,5},{5,4},{6,7},{7,6},{8,9},{9,8},{10,11... | collective-permute-start | bytes 2359304 | tf_op jit(solution)/shard_map/ppermute | solution.py:84
  148.2 0.8 copy-start.4
  149.0 3.4 %collective-permute-start.3 = (f32[256,256]{1,0:T(8,128)S(1)}, f32[256,256]{1,0:T(8,128)S(1)}, u32[]{:S(2)}, u32[]{:S(2)}) collective-permute-start(f32[256,256]{1,0:T(8,128)S(1)} %slice.44), channel_id=1, source_target_pairs={{0,1},{1,0},{2,3},{3,2},{4,5},{5,4},{6,7},{7,6},{8,9},{9,8},{10,11... | collective-permute-start | bytes 786440 | tf_op jit(solution)/shard_map/ppermute | solution.py:84
  154.0 15.9 %collective-permute-start.5 = (bf16[256,128]{1,0:T(8,128)(2,1)}, bf16[256,128]{1,0:T(8,128)(2,1)S(1)}, u32[]{:S(2)}, u32[]{:S(2)}) collective-permute-start(bf16[256,128]{1,0:T(8,128)(2,1)} %slice.61), channel_id=1, source_target_pairs={{0,2},{2,0},{1,3},{3,1},{4,6},{6,4},{5,7},{7,5},{8,10},{10,8},{9,1... | collective-permute-start | bytes 196616 | tf_op jit(solution)/shard_map/ppermute | solution.py:87
  167.9 27.0 %collective-permute-start.6 = (bf16[768,128]{1,0:T(8,128)(2,1)S(1)}, bf16[768,128]{1,0:T(8,128)(2,1)S(1)}, u32[]{:S(2)}, u32[]{:S(2)}) collective-permute-start(bf16[768,128]{1,0:T(8,128)(2,1)S(1)} %slice.60), channel_id=1, source_target_pairs={{0,2},{2,0},{1,3},{3,1},{4,6},{6,4},{5,7},{7,5},{8,10},{10,8},{9,1... | collective-permute-start | bytes 589832 | tf_op jit(solution)/shard_map/ppermute | solution.py:87
Sparse Core Ops, SparseCore 0:
  42.7 92.4 all-gather.1

commit v3 on v2

--- a/solution.py
+++ b/solution.py
@@ -8,6 +8,7 @@
 
 AXES = ("z", "x", "y", "half", "core")
 SIZES = (8, 4, 4, 2, 2)
+TURNS = (("x", 1), ("y", 1), ("x", 3), ("y", 3))
 
 
 def condition(block, left, right):
@@ -20,13 +21,15 @@
 
 
 def joined(pieces):
-    return jnp.concatenate([p[0] for p in pieces], 0), [o for p in pieces for o in p[1]]
+    rows = lax.optimization_barrier(jnp.concatenate([p[0] for p in pieces], 0))
+    return rows, [o for p in pieces for o in p[1]]
 
 
-def flipped(piece, bit):
+def partner(piece, axis, bits):
     rows, owners = piece
-    came = lax.ppermute(rows, "z", [(i, i ^ bit) for i in range(SIZES[0])])
-    return came, [z ^ bit for z in owners]
+    came = lax.ppermute(rows, axis, [(i, i ^ bits) for i in range(SIZES[AXES.index(axis)])])
+    flip = [bits if name == axis else 0 for name in "zxy"]
+    return came, [tuple(a ^ b for a, b in zip(o, flip)) for o in owners]
 
 
 def place_kernel(place_ref, *refs):
@@ -65,29 +68,38 @@
 def on_device(train_grads, query_grads, left_factor, right_factor):
     half, core = lax.axis_index("half"), lax.axis_index("core")
     width = train_grads.shape[1] // 4
-    shares = train_grads[0].reshape(4, width, train_grads.shape[2])
-    order = [2 * half + core, 2 * (1 - half) + core, 2 * half + 1 - core, 2 * (1 - half) + 1 - core]
-    resident = jnp.concatenate([lax.dynamic_index_in_dim(shares, k, 0, False) for k in order], 0)
+    resident = train_grads[0]
 
-    own = condition(query_grads[0], left_factor[0], right_factor[0]), [0]
-    pair = joined([own, flipped(own, 4)])
-    four = joined([pair, flipped(pair, 2)])
-    column, flips = joined([four, flipped(four, 1)])
-    plane = lax.all_gather(column, ("x", "y"), axis=0, tiled=True)
-    groups = [plane[: plane.shape[0] // 4], plane[plane.shape[0] // 4 :]]
+    own = condition(query_grads[0], left_factor[0], right_factor[0]), [(0, 0, 0)]
+    pair = joined([own, partner(own, "z", 4)])
+    two = partner(pair, "z", 2)
+    one = partner(pair, "z", 1)
+    held = [pair, two, one, partner(two, "z", 1)]
+    for step in range(len(TURNS)):
+        came = [partner(p, *TURNS[(k + step) % len(TURNS)]) for k, p in enumerate(held)]
+        if step < len(TURNS) - 1:
+            held = [joined(pieces) for pieces in zip(held, came)]
 
-    kept, arrived = [], []
-    for rows in groups:
-        partial_scores = lax.dot_general(
-            rows, resident, (((1,), (1,)), ((), ())), preferred_element_type=jnp.float32
+    kept, arrived, owners = [], [], []
+    for pieces in (held[:2], held[2:] + came[:1], came[1:]):
+        partial_scores = jnp.concatenate(
+            [
+                lax.dot_general(rows, resident, (((1,), (1,)), ((), ())), preferred_element_type=jnp.float32)
+                for rows, _ in pieces
+            ],
+            0,
         )
-        other = lax.ppermute(partial_scores[:, 2 * width :], "core", [(0, 1), (1, 0)])
-        both = partial_scores[:, : 2 * width] + other
-        kept.append(both[:, :width])
-        arrived.append(lax.ppermute(both[:, width:].astype(jnp.bfloat16), "half", [(0, 1), (1, 0)]))
-    z = lax.axis_index("z") ^ jnp.array(flips, jnp.int32)
-    in_plane = lax.broadcasted_iota(jnp.int32, (16, 1), 0)
-    places = (z[None, :] * 16 + in_plane).reshape(-1)
+        shares = [partial_scores[:, k * width : (k + 1) * width] for k in range(4)]
+        away = [jnp.where(core == 0, shares[2 * k + 1], shares[2 * k]) for k in range(2)]
+        here = [jnp.where(core == 0, shares[2 * k], shares[2 * k + 1]) for k in range(2)]
+        other = lax.ppermute(jnp.concatenate(away, 1), "core", [(0, 1), (1, 0)])
+        both = [here[k] + other[:, k * width : (k + 1) * width] for k in range(2)]
+        kept.append(jnp.where(half == 0, both[0], both[1]))
+        cross = jnp.where(half == 0, both[1], both[0]).astype(jnp.bfloat16)
+        arrived.append(lax.ppermute(cross, "half", [(0, 1), (1, 0)]))
+        owners += [o for piece in pieces for o in piece[1]]
+    z, x, y = (lax.axis_index(n) ^ jnp.array([o[k] for o in owners], jnp.int32) for k, n in enumerate("zxy"))
+    places = (z * SIZES[1] + x) * SIZES[2] + y
     return place(kept, arrived, places)
 
 

time: 204 us -> 162 us (0.79)
  waiting for transfers between devices: 124 us -> 27.5 us
  starting transfers between devices: 42.3 us -> 114 us
  between operations: 13.6 us -> 0.66 us
  local copies, waits for them, and re-layouts: 6.93 us -> 1.22 us
    all_gather x1 -> x0, waiting for transfers between devices: 88.6 us -> none  [on_device(): plane = lax.all_gather(column, ('x', 'y'), axis=0, tiled=True)]
    ppermute x7 -> x26, starting transfers between devices: 42.3 us -> 114 us  [the longest x20 71.6 us: partner(): lax.ppermute(rows, axis, [(i, i ^ bits) for i in range(SIZES[AXES.index(a...]
    ppermute x7 -> x26, waiting for transfers between devices: 35.5 us -> 27.5 us  [the longest x3 20.9 us: on_device(): arrived.append(lax.ppermute(cross, 'half', [(0, 1), (1, 0)]))]
    squeeze x1 -> x0, local copies, waits for them, and re-layouts: 4.03 us -> none  [on_device(): lax.dynamic_index_in_dim(shares, k, 0, False)]
    dot_general x2 -> x8, matrix products: 10.3 us -> 12.2 us  [on_device(): lax.dot_general(rows, resident, (((1,), (1,)), ((), ())), preferred_eleme...]
  transfers between devices with their start and end apart: 8 -> 26, of which waited for: 6 -> 7; matrix products, arithmetic and copies ran while one was open for 5% -> 9% of each run, Pallas kernels for 0% -> 0%
where the time goes in v3:
time: 162 us; the launch traced here: 161 us
  starting transfers between devices  114 us (70%)
  waiting for transfers between devices  27.5 us (17%)
  matrix products  13.6 us (8%)
  other arithmetic  1.84 us (1%)
    ppermute x20, starting transfers between devices, partner(): lax.ppermute(rows, axis, [(i, i ^ bits) for i in range(SIZES[AXES.index(a...  71.6 us
    ppermute x3, starting transfers between devices, on_device(): arrived.append(lax.ppermute(cross, 'half', [(0, 1), (1, 0)]))  27.3 us
    ppermute x3, waiting for transfers between devices, on_device(): arrived.append(lax.ppermute(cross, 'half', [(0, 1), (1, 0)]))  20.9 us
    ppermute x3, starting transfers between devices, on_device(): other = lax.ppermute(jnp.concatenate(away, 1), 'core', [(0, 1), (1, 0)])  15.5 us
    dot_general x8, matrix products, on_device(): lax.dot_general(rows, resident, (((1,), (1,)), ((), ())), preferred_eleme...  12.2 us
    ppermute x20, waiting for transfers between devices, partner(): lax.ppermute(rows, axis, [(i, i ^ bits) for i in range(SIZES[AXES.index(a...  6.61 us
  transfers between devices with their start and end apart: 26, of which 7 were waited for; matrix products, arithmetic and copies ran while one was open for 9% of the time, Pallas kernels for 0%

profile of v3, /device:TPU:1, one launch (start us, length us, event | category | flops | bytes accessed | tf_op | source)
XLA Modules:
  0.0 160.8 jit_solution(17600583037427689788)
XLA Ops:
  0.0 1.0 reshape.6
  1.1 0.2 convolution_bitcast_fusion
  1.3 1.1 convolution_convert_fusion
  2.4 0.2 convert_element_type.17
  2.6 9.6 %collective-permute-start = (bf16[8,4096]{1,0:T(8,128)(2,1)S(1)}, bf16[8,4096]{1,0:T(8,128)(2,1)S(1)}, u32[]{:S(2)}, u32[]{:S(2)}) collective-permute-start(bf16[8,4096]{1,0:T(8,128)(2,1)S(1)} %convert_element_type.17), channel_id=1, source_target_pairs={{0,256},{64,320},{128,384},{192,448},{256,0},{320,64},{384,128},{4... | collective-permute-start | bytes 196616 | tf_op jit(solution)/shard_map/ppermute | solution.py:30
  12.3 1.6 %collective-permute-done = bf16[8,4096]{1,0:T(8,128)(2,1)S(1)} collective-permute-done((bf16[8,4096]{1,0:T(8,128)(2,1)S(1)}, bf16[8,4096]{1,0:T(8,128)(2,1)S(1)}, u32[]{:S(2)}, u32[]{:S(2)}) %collective-permute-start) | collective-permute-done | bytes 65568 | tf_op jit(solution)/shard_map/ppermute | solution.py:30
  13.9 7.0 %collective-permute-start.4 = (bf16[16,4096]{1,0:T(8,128)(2,1)S(1)}, bf16[16,4096]{1,0:T(8,128)(2,1)S(1)}, u32[]{:S(2)}, u32[]{:S(2)}) collective-permute-start(bf16[16,4096]{1,0:T(8,128)(2,1)S(1)} %pad_maximum_fusion.18), channel_id=1, source_target_pairs={{0,128},{64,192},{128,0},{192,64},{256,384},{320,448},{384,256},{4... | collective-permute-start | bytes 393224 | tf_op jit(solution)/shard_map/ppermute | solution.py:30
  20.9 3.1 %collective-permute-start.1 = (bf16[16,4096]{1,0:T(8,128)(2,1)S(1)}, bf16[16,4096]{1,0:T(8,128)(2,1)S(1)}, u32[]{:S(2)}, u32[]{:S(2)}) collective-permute-start(bf16[16,4096]{1,0:T(8,128)(2,1)S(1)} %pad_maximum_fusion.18), channel_id=1, source_target_pairs={{0,16},{16,0},{32,48},{48,32},{1,17},{17,1},{33,49},{49,33},{2,18}... | collective-permute-start | bytes 393224 | tf_op jit(solution)/shard_map/ppermute | solution.py:30
  24.0 0.7 xor_add_fusion.place_ref
  24.7 4.6 %collective-permute-start.9 = (bf16[16,4096]{1,0:T(8,128)(2,1)S(1)}, bf16[16,4096]{1,0:T(8,128)(2,1)S(1)}, u32[]{:S(2)}, u32[]{:S(2)}) collective-permute-start(bf16[16,4096]{1,0:T(8,128)(2,1)S(1)} %pad_maximum_fusion.18), channel_id=1, source_target_pairs={{0,64},{64,0},{128,192},{192,128},{256,320},{320,256},{384,448},{4... | collective-permute-start | bytes 393224 | tf_op jit(solution)/shard_map/ppermute | solution.py:30
  29.3 3.2 %collective-permute-start.5 = (bf16[16,4096]{1,0:T(8,128)(2,1)S(1)}, bf16[16,4096]{1,0:T(8,128)(2,1)S(1)}, u32[]{:S(2)}, u32[]{:S(2)}) collective-permute-start(bf16[16,4096]{1,0:T(8,128)(2,1)S(1)} %collective-permute-done.4), channel_id=1, source_target_pairs={{0,4},{4,0},{8,12},{12,8},{1,5},{5,1},{9,13},{13,9},{2,6},{6,2},{1... | collective-permute-start | bytes 393224 | tf_op jit(solution)/shard_map/ppermute | solution.py:30
  32.6 2.1 %collective-permute-start.2 = (bf16[32,4096]{1,0:T(8,128)(2,1)S(1)}, bf16[32,4096]{1,0:T(8,128)(2,1)S(1)}, u32[]{:S(2)}, u32[]{:S(2)}) collective-permute-start(bf16[32,4096]{1,0:T(8,128)(2,1)S(1)} %pad_maximum_fusion.12), channel_id=1, source_target_pairs={{0,4},{4,0},{8,12},{12,8},{1,5},{5,1},{9,13},{13,9},{2,6},{6,2},{1... | collective-permute-start | bytes 786440 | tf_op jit(solution)/shard_map/ppermute | solution.py:30
  34.7 1.9 %collective-permute-start.13 = (bf16[16,4096]{1,0:T(8,128)(2,1)S(1)}, bf16[16,4096]{1,0:T(8,128)(2,1)S(1)}, u32[]{:S(2)}, u32[]{:S(2)}) collective-permute-start(bf16[16,4096]{1,0:T(8,128)(2,1)S(1)} %collective-permute-done.4), channel_id=1, source_target_pairs={{0,64},{64,0},{128,192},{192,128},{256,320},{320,256},{384,448},{4... | collective-permute-start | bytes 393224 | tf_op jit(solution)/shard_map/ppermute | solution.py:30
  36.6 3.7 %collective-permute-start.10 = (bf16[16,4096]{1,0:T(8,128)(2,1)S(1)}, bf16[16,4096]{1,0:T(8,128)(2,1)S(1)}, u32[]{:S(2)}, u32[]{:S(2)}) collective-permute-start(bf16[16,4096]{1,0:T(8,128)(2,1)S(1)} %collective-permute-done.9), channel_id=1, source_target_pairs={{0,48},{16,32},{32,16},{48,0},{1,49},{17,33},{33,17},{49,1},{2,50}... | collective-permute-start | bytes 393224 | tf_op jit(solution)/shard_map/ppermute | solution.py:30
  40.4 2.8 %collective-permute-start.6 = (bf16[32,4096]{1,0:T(8,128)(2,1)S(1)}, bf16[32,4096]{1,0:T(8,128)(2,1)S(1)}, u32[]{:S(2)}, u32[]{:S(2)}) collective-permute-start(bf16[32,4096]{1,0:T(8,128)(2,1)S(1)} %pad_maximum_fusion.13), channel_id=1, source_target_pairs={{0,48},{16,32},{32,16},{48,0},{1,49},{17,33},{33,17},{49,1},{2,50}... | collective-permute-start | bytes 786440 | tf_op jit(solution)/shard_map/ppermute | solution.py:30
  43.1 0.4 collective-permute-done.10
  43.5 4.6 %collective-permute-start.11 = (bf16[32,4096]{1,0:T(8,128)(2,1)S(1)}, bf16[32,4096]{1,0:T(8,128)(2,1)S(1)}, u32[]{:S(2)}, u32[]{:S(2)}) collective-permute-start(bf16[32,4096]{1,0:T(8,128)(2,1)S(1)} %pad_maximum_fusion.15), channel_id=1, source_target_pairs={{0,12},{4,8},{8,4},{12,0},{1,13},{5,9},{9,5},{13,1},{2,14},{6,10},... | collective-permute-start | bytes 786440 | tf_op jit(solution)/shard_map/ppermute | solution.py:30
  48.2 1.9 %collective-permute-start.14 = (bf16[16,4096]{1,0:T(8,128)(2,1)S(1)}, bf16[16,4096]{1,0:T(8,128)(2,1)S(1)}, u32[]{:S(2)}, u32[]{:S(2)}) collective-permute-start(bf16[16,4096]{1,0:T(8,128)(2,1)S(1)} %collective-permute-done.13), channel_id=1, source_target_pairs={{0,12},{4,8},{8,4},{12,0},{1,13},{5,9},{9,5},{13,1},{2,14},{6,10},... | collective-permute-start | bytes 393224 | tf_op jit(solution)/shard_map/ppermute | solution.py:30
  50.2 3.7 %collective-permute-start.3 = (bf16[64,4096]{1,0:T(8,128)(2,1)S(1)}, bf16[64,4096]{1,0:T(8,128)(2,1)S(1)}, u32[]{:S(2)}, u32[]{:S(2)}) collective-permute-start(bf16[64,4096]{1,0:T(8,128)(2,1)S(1)} %pad_maximum_fusion.6), channel_id=1, source_target_pairs={{0,48},{16,32},{32,16},{48,0},{1,49},{17,33},{33,17},{49,1},{2,50}... | collective-permute-start | bytes 1572872 | tf_op jit(solution)/shard_map/ppermute | solution.py:30
  53.9 2.9 %collective-permute-done.14 = bf16[16,4096]{1,0:T(8,128)(2,1)S(1)} collective-permute-done((bf16[16,4096]{1,0:T(8,128)(2,1)S(1)}, bf16[16,4096]{1,0:T(8,128)(2,1)S(1)}, u32[]{:S(2)}, u32[]{:S(2)}) %collective-permute-start.14) | collective-permute-done | bytes 131104 | tf_op jit(solution)/shard_map/ppermute | solution.py:30
  56.8 1.9 %collective-permute-start.15 = (bf16[32,4096]{1,0:T(8,128)(2,1)S(1)}, bf16[32,4096]{1,0:T(8,128)(2,1)S(1)}, u32[]{:S(2)}, u32[]{:S(2)}) collective-permute-start(bf16[32,4096]{1,0:T(8,128)(2,1)S(1)} %pad_maximum_fusion.16), channel_id=1, source_target_pairs={{0,16},{16,0},{32,48},{48,32},{1,17},{17,1},{33,49},{49,33},{2,18}... | collective-permute-start | bytes 786440 | tf_op jit(solution)/shard_map/ppermute | solution.py:30
  58.8 1.9 %collective-permute-start.7 = (bf16[64,4096]{1,0:T(8,128)(2,1)S(1)}, bf16[64,4096]{1,0:T(8,128)(2,1)S(1)}, u32[]{:S(2)}, u32[]{:S(2)}) collective-permute-start(bf16[64,4096]{1,0:T(8,128)(2,1)S(1)} %pad_maximum_fusion.7), channel_id=1, source_target_pairs={{0,12},{4,8},{8,4},{12,0},{1,13},{5,9},{9,5},{13,1},{2,14},{6,10},... | collective-permute-start | bytes 1572872 | tf_op jit(solution)/shard_map/ppermute | solution.py:30
  60.8 3.4 %collective-permute-start.12 = (bf16[64,4096]{1,0:T(8,128)(2,1)S(1)}, bf16[64,4096]{1,0:T(8,128)(2,1)S(1)}, u32[]{:S(2)}, u32[]{:S(2)}) collective-permute-start(bf16[64,4096]{1,0:T(8,128)(2,1)S(1)} %pad_maximum_fusion.8), channel_id=1, source_target_pairs={{0,16},{16,0},{32,48},{48,32},{1,17},{17,1},{33,49},{49,33},{2,18}... | collective-permute-start | bytes 1572872 | tf_op jit(solution)/shard_map/ppermute | solution.py:30
  64.3 1.9 %collective-permute-start.16 = (bf16[64,4096]{1,0:T(8,128)(2,1)S(1)}, bf16[64,4096]{1,0:T(8,128)(2,1)S(1)}, u32[]{:S(2)}, u32[]{:S(2)}) collective-permute-start(bf16[64,4096]{1,0:T(8,128)(2,1)S(1)} %pad_maximum_fusion.9), channel_id=1, source_target_pairs={{0,4},{4,0},{8,12},{12,8},{1,5},{5,1},{9,13},{13,9},{2,6},{6,2},{1... | collective-permute-start | bytes 1572872 | tf_op jit(solution)/shard_map/ppermute | solution.py:30
  66.2 0.1 pad_maximum_fusion
  66.3 4.5 %collective-permute-start.17 = (bf16[128,4096]{1,0:T(8,128)(2,1)S(1)}, bf16[128,4096]{1,0:T(8,128)(2,1)S(1)}, u32[]{:S(2)}, u32[]{:S(2)}) collective-permute-start(bf16[128,4096]{1,0:T(8,128)(2,1)S(1)} %pad_maximum_fusion), channel_id=1, source_target_pairs={{0,12},{4,8},{8,4},{12,0},{1,13},{5,9},{9,5},{13,1},{2,14},{6,10},... | collective-permute-start | bytes 3145736 | tf_op jit(solution)/shard_map/ppermute | solution.py:30
  70.9 1.5 fusion.14
  72.5 3.0 %collective-permute-start.19 = (bf16[128,4096]{1,0:T(8,128)(2,1)S(1)}, bf16[128,4096]{1,0:T(8,128)(2,1)S(1)}, u32[]{:S(2)}, u32[]{:S(2)}) collective-permute-start(bf16[128,4096]{1,0:T(8,128)(2,1)S(1)} %pad_maximum_fusion.1), channel_id=1, source_target_pairs={{0,16},{16,0},{32,48},{48,32},{1,17},{17,1},{33,49},{49,33},{2,18}... | collective-permute-start | bytes 3145736 | tf_op jit(solution)/shard_map/ppermute | solution.py:30
  75.5 1.5 fusion.12
  77.1 10.2 %collective-permute-start.8 = (f32[256,256]{1,0:T(8,128)S(1)}, f32[256,256]{1,0:T(8,128)S(1)}, u32[]{:S(2)}, u32[]{:S(2)}) collective-permute-start(f32[256,256]{1,0:T(8,128)S(1)} %pad_maximum_fusion.14), channel_id=1, source_target_pairs={{0,1},{1,0},{2,3},{3,2},{4,5},{5,4},{6,7},{7,6},{8,9},{9,8},{10,11... | collective-permute-start | bytes 786440 | tf_op jit(solution)/shard_map/ppermute | solution.py:95
  87.4 0.1 pad_maximum_fusion.2
  87.5 1.9 %collective-permute-start.20 = (bf16[128,4096]{1,0:T(8,128)(2,1)S(1)}, bf16[128,4096]{1,0:T(8,128)(2,1)S(1)}, u32[]{:S(2)}, u32[]{:S(2)}) collective-permute-start(bf16[128,4096]{1,0:T(8,128)(2,1)S(1)} %pad_maximum_fusion.2), channel_id=1, source_target_pairs={{0,4},{4,0},{8,12},{12,8},{1,5},{5,1},{9,13},{13,9},{2,6},{6,2},{1... | collective-permute-start | bytes 3145736 | tf_op jit(solution)/shard_map/ppermute | solution.py:30
  89.4 1.5 fusion.10
  91.0 4.7 %collective-permute-start.21 = (bf16[128,4096]{1,0:T(8,128)(2,1)S(1)}, bf16[128,4096]{1,0:T(8,128)(2,1)S(1)}, u32[]{:S(2)}, u32[]{:S(2)}) collective-permute-start(bf16[128,4096]{1,0:T(8,128)(2,1)S(1)} %pad_maximum_fusion.3), channel_id=1, source_target_pairs={{0,48},{16,32},{32,16},{48,0},{1,49},{17,33},{33,17},{49,1},{2,50}... | collective-permute-start | bytes 3145736 | tf_op jit(solution)/shard_map/ppermute | solution.py:30
  95.8 1.5 fusion.8
  97.4 12.7 %collective-permute-start.23 = (bf16[256,128]{1,0:T(8,128)(2,1)S(1)}, bf16[256,128]{1,0:T(8,128)(2,1)S(1)}, u32[]{:S(2)}, u32[]{:S(2)}) collective-permute-start(bf16[256,128]{1,0:T(8,128)(2,1)S(1)} %get-tuple-element.11), channel_id=1, source_target_pairs={{0,2},{2,0},{1,3},{3,1},{4,6},{6,4},{5,7},{7,5},{8,10},{10,8},{9,1... | collective-permute-start | bytes 196616 | tf_op jit(solution)/shard_map/ppermute | solution.py:99
  110.1 1.5 fusion.6
  111.8 2.7 %collective-permute-start.18 = (f32[384,256]{1,0:T(8,128)S(1)}, f32[384,256]{1,0:T(8,128)S(1)}, u32[]{:S(2)}, u32[]{:S(2)}) collective-permute-start(f32[384,256]{1,0:T(8,128)S(1)} %pad_maximum_fusion.10), channel_id=1, source_target_pairs={{0,1},{1,0},{2,3},{3,2},{4,5},{5,4},{6,7},{7,6},{8,9},{9,8},{10,11... | collective-permute-start | bytes 1179656 | tf_op jit(solution)/shard_map/ppermute | solution.py:95
  114.5 1.5 fusion.2
  116.0 1.5 fusion.4
  117.5 1.6 collective-permute-done.21
  119.1 1.5 fusion
  120.8 2.6 %collective-permute-start.22 = (f32[384,256]{1,0:T(8,128)S(1)}, f32[384,256]{1,0:T(8,128)S(1)}, u32[]{:S(2)}, u32[]{:S(2)}) collective-permute-start(f32[384,256]{1,0:T(8,128)S(1)} %pad_maximum_fusion.11), channel_id=1, source_target_pairs={{0,1},{1,0},{2,3},{3,2},{4,5},{5,4},{6,7},{7,6},{8,9},{9,8},{10,11... | collective-permute-start | bytes 1179656 | tf_op jit(solution)/shard_map/ppermute | solution.py:95
  123.5 12.7 %collective-permute-start.24 = (bf16[384,128]{1,0:T(8,128)(2,1)S(1)}, bf16[384,128]{1,0:T(8,128)(2,1)S(1)}, u32[]{:S(2)}, u32[]{:S(2)}) collective-permute-start(bf16[384,128]{1,0:T(8,128)(2,1)S(1)} %get-tuple-element.8), channel_id=1, source_target_pairs={{0,2},{2,0},{1,3},{3,1},{4,6},{6,4},{5,7},{7,5},{8,10},{10,8},{9,1... | collective-permute-start | bytes 294920 | tf_op jit(solution)/shard_map/ppermute | solution.py:99
  136.3 1.9 %collective-permute-start.25 = (bf16[384,128]{1,0:T(8,128)(2,1)S(1)}, bf16[384,128]{1,0:T(8,128)(2,1)S(1)}, u32[]{:S(2)}, u32[]{:S(2)}) collective-permute-start(bf16[384,128]{1,0:T(8,128)(2,1)S(1)} %get-tuple-element.5), channel_id=1, source_target_pairs={{0,2},{2,0},{1,3},{3,1},{4,6},{6,4},{5,7},{7,5},{8,10},{10,8},{9,1... | collective-permute-start | bytes 294920 | tf_op jit(solution)/shard_map/ppermute | solution.py:99
  138.3 1.1 collective-permute-done.24.refs_4_
  139.4 19.8 %collective-permute-done.25.refs_5_ = bf16[384,128]{1,0:T(8,128)(2,1)S(1)} collective-permute-done((bf16[384,128]{1,0:T(8,128)(2,1)S(1)}, bf16[384,128]{1,0:T(8,128)(2,1)S(1)}, u32[]{:S(2)}, u32[]{:S(2)}) %collective-permute-start.25) | collective-permute-done | bytes 98336 | tf_op jit(solution)/shard_map/ppermute | solution.py:99
  159.2 1.6 shard_map.73
  (49 shorter events, 1.1 us)
Async XLA Ops:
  0.0 1.0 copy-start
  2.6 11.3 %collective-permute-start = (bf16[8,4096]{1,0:T(8,128)(2,1)S(1)}, bf16[8,4096]{1,0:T(8,128)(2,1)S(1)}, u32[]{:S(2)}, u32[]{:S(2)}) collective-permute-start(bf16[8,4096]{1,0:T(8,128)(2,1)S(1)} %convert_element_type.17), channel_id=1, source_target_pairs={{0,256},{64,320},{128,384},{192,448},{256,0},{320,64},{384,128},{4... | collective-permute-start | bytes 196616 | tf_op jit(solution)/shard_map/ppermute | solution.py:30
  13.9 15.4 %collective-permute-start.4 = (bf16[16,4096]{1,0:T(8,128)(2,1)S(1)}, bf16[16,4096]{1,0:T(8,128)(2,1)S(1)}, u32[]{:S(2)}, u32[]{:S(2)}) collective-permute-start(bf16[16,4096]{1,0:T(8,128)(2,1)S(1)} %pad_maximum_fusion.18), channel_id=1, source_target_pairs={{0,128},{64,192},{128,0},{192,64},{256,384},{320,448},{384,256},{4... | collective-permute-start | bytes 393224 | tf_op jit(solution)/shard_map/ppermute | solution.py:30
  20.9 11.6 %collective-permute-start.1 = (bf16[16,4096]{1,0:T(8,128)(2,1)S(1)}, bf16[16,4096]{1,0:T(8,128)(2,1)S(1)}, u32[]{:S(2)}, u32[]{:S(2)}) collective-permute-start(bf16[16,4096]{1,0:T(8,128)(2,1)S(1)} %pad_maximum_fusion.18), channel_id=1, source_target_pairs={{0,16},{16,0},{32,48},{48,32},{1,17},{17,1},{33,49},{49,33},{2,18}... | collective-permute-start | bytes 393224 | tf_op jit(solution)/shard_map/ppermute | solution.py:30
  24.7 46.1 %copy-start.1 = (bf16[1,512,4096]{2,1,0:T(8,128)(2,1)S(1)}, bf16[1,512,4096]{2,1,0:T(8,128)(2,1)}, u32[]{:S(2)}) copy-start(bf16[1,512,4096]{2,1,0:T(8,128)(2,1)} %param.7) | copy-start | bytes 12582916
  24.7 11.8 %collective-permute-start.9 = (bf16[16,4096]{1,0:T(8,128)(2,1)S(1)}, bf16[16,4096]{1,0:T(8,128)(2,1)S(1)}, u32[]{:S(2)}, u32[]{:S(2)}) collective-permute-start(bf16[16,4096]{1,0:T(8,128)(2,1)S(1)} %pad_maximum_fusion.18), channel_id=1, source_target_pairs={{0,64},{64,0},{128,192},{192,128},{256,320},{320,256},{384,448},{4... | collective-permute-start | bytes 393224 | tf_op jit(solution)/shard_map/ppermute | solution.py:30
  29.3 11.0 %collective-permute-start.5 = (bf16[16,4096]{1,0:T(8,128)(2,1)S(1)}, bf16[16,4096]{1,0:T(8,128)(2,1)S(1)}, u32[]{:S(2)}, u32[]{:S(2)}) collective-permute-start(bf16[16,4096]{1,0:T(8,128)(2,1)S(1)} %collective-permute-done.4), channel_id=1, source_target_pairs={{0,4},{4,0},{8,12},{12,8},{1,5},{5,1},{9,13},{13,9},{2,6},{6,2},{1... | collective-permute-start | bytes 393224 | tf_op jit(solution)/shard_map/ppermute | solution.py:30
  32.6 17.6 %collective-permute-start.2 = (bf16[32,4096]{1,0:T(8,128)(2,1)S(1)}, bf16[32,4096]{1,0:T(8,128)(2,1)S(1)}, u32[]{:S(2)}, u32[]{:S(2)}) collective-permute-start(bf16[32,4096]{1,0:T(8,128)(2,1)S(1)} %pad_maximum_fusion.12), channel_id=1, source_target_pairs={{0,4},{4,0},{8,12},{12,8},{1,5},{5,1},{9,13},{13,9},{2,6},{6,2},{1... | collective-permute-start | bytes 786440 | tf_op jit(solution)/shard_map/ppermute | solution.py:30
  34.7 13.5 %collective-permute-start.13 = (bf16[16,4096]{1,0:T(8,128)(2,1)S(1)}, bf16[16,4096]{1,0:T(8,128)(2,1)S(1)}, u32[]{:S(2)}, u32[]{:S(2)}) collective-permute-start(bf16[16,4096]{1,0:T(8,128)(2,1)S(1)} %collective-permute-done.4), channel_id=1, source_target_pairs={{0,64},{64,0},{128,192},{192,128},{256,320},{320,256},{384,448},{4... | collective-permute-start | bytes 393224 | tf_op jit(solution)/shard_map/ppermute | solution.py:30
  36.6 6.9 %collective-permute-start.10 = (bf16[16,4096]{1,0:T(8,128)(2,1)S(1)}, bf16[16,4096]{1,0:T(8,128)(2,1)S(1)}, u32[]{:S(2)}, u32[]{:S(2)}) collective-permute-start(bf16[16,4096]{1,0:T(8,128)(2,1)S(1)} %collective-permute-done.9), channel_id=1, source_target_pairs={{0,48},{16,32},{32,16},{48,0},{1,49},{17,33},{33,17},{49,1},{2,50}... | collective-permute-start | bytes 393224 | tf_op jit(solution)/shard_map/ppermute | solution.py:30
  40.4 18.4 %collective-permute-start.6 = (bf16[32,4096]{1,0:T(8,128)(2,1)S(1)}, bf16[32,4096]{1,0:T(8,128)(2,1)S(1)}, u32[]{:S(2)}, u32[]{:S(2)}) collective-permute-start(bf16[32,4096]{1,0:T(8,128)(2,1)S(1)} %pad_maximum_fusion.13), channel_id=1, source_target_pairs={{0,48},{16,32},{32,16},{48,0},{1,49},{17,33},{33,17},{49,1},{2,50}... | collective-permute-start | bytes 786440 | tf_op jit(solution)/shard_map/ppermute | solution.py:30
  43.5 17.2 %collective-permute-start.11 = (bf16[32,4096]{1,0:T(8,128)(2,1)S(1)}, bf16[32,4096]{1,0:T(8,128)(2,1)S(1)}, u32[]{:S(2)}, u32[]{:S(2)}) collective-permute-start(bf16[32,4096]{1,0:T(8,128)(2,1)S(1)} %pad_maximum_fusion.15), channel_id=1, source_target_pairs={{0,12},{4,8},{8,4},{12,0},{1,13},{5,9},{9,5},{13,1},{2,14},{6,10},... | collective-permute-start | bytes 786440 | tf_op jit(solution)/shard_map/ppermute | solution.py:30
  48.2 8.6 %collective-permute-start.14 = (bf16[16,4096]{1,0:T(8,128)(2,1)S(1)}, bf16[16,4096]{1,0:T(8,128)(2,1)S(1)}, u32[]{:S(2)}, u32[]{:S(2)}) collective-permute-start(bf16[16,4096]{1,0:T(8,128)(2,1)S(1)} %collective-permute-done.13), channel_id=1, source_target_pairs={{0,12},{4,8},{8,4},{12,0},{1,13},{5,9},{9,5},{13,1},{2,14},{6,10},... | collective-permute-start | bytes 393224 | tf_op jit(solution)/shard_map/ppermute | solution.py:30
  50.2 16.0 %collective-permute-start.3 = (bf16[64,4096]{1,0:T(8,128)(2,1)S(1)}, bf16[64,4096]{1,0:T(8,128)(2,1)S(1)}, u32[]{:S(2)}, u32[]{:S(2)}) collective-permute-start(bf16[64,4096]{1,0:T(8,128)(2,1)S(1)} %pad_maximum_fusion.6), channel_id=1, source_target_pairs={{0,48},{16,32},{32,16},{48,0},{1,49},{17,33},{33,17},{49,1},{2,50}... | collective-permute-start | bytes 1572872 | tf_op jit(solution)/shard_map/ppermute | solution.py:30
  56.8 7.4 %collective-permute-start.15 = (bf16[32,4096]{1,0:T(8,128)(2,1)S(1)}, bf16[32,4096]{1,0:T(8,128)(2,1)S(1)}, u32[]{:S(2)}, u32[]{:S(2)}) collective-permute-start(bf16[32,4096]{1,0:T(8,128)(2,1)S(1)} %pad_maximum_fusion.16), channel_id=1, source_target_pairs={{0,16},{16,0},{32,48},{48,32},{1,17},{17,1},{33,49},{49,33},{2,18}... | collective-permute-start | bytes 786440 | tf_op jit(solution)/shard_map/ppermute | solution.py:30
  58.8 13.6 %collective-permute-start.7 = (bf16[64,4096]{1,0:T(8,128)(2,1)S(1)}, bf16[64,4096]{1,0:T(8,128)(2,1)S(1)}, u32[]{:S(2)}, u32[]{:S(2)}) collective-permute-start(bf16[64,4096]{1,0:T(8,128)(2,1)S(1)} %pad_maximum_fusion.7), channel_id=1, source_target_pairs={{0,12},{4,8},{8,4},{12,0},{1,13},{5,9},{9,5},{13,1},{2,14},{6,10},... | collective-permute-start | bytes 1572872 | tf_op jit(solution)/shard_map/ppermute | solution.py:30
  60.8 26.5 %collective-permute-start.12 = (bf16[64,4096]{1,0:T(8,128)(2,1)S(1)}, bf16[64,4096]{1,0:T(8,128)(2,1)S(1)}, u32[]{:S(2)}, u32[]{:S(2)}) collective-permute-start(bf16[64,4096]{1,0:T(8,128)(2,1)S(1)} %pad_maximum_fusion.8), channel_id=1, source_target_pairs={{0,16},{16,0},{32,48},{48,32},{1,17},{17,1},{33,49},{49,33},{2,18}... | collective-permute-start | bytes 1572872 | tf_op jit(solution)/shard_map/ppermute | solution.py:30
  64.3 26.6 %collective-permute-start.16 = (bf16[64,4096]{1,0:T(8,128)(2,1)S(1)}, bf16[64,4096]{1,0:T(8,128)(2,1)S(1)}, u32[]{:S(2)}, u32[]{:S(2)}) collective-permute-start(bf16[64,4096]{1,0:T(8,128)(2,1)S(1)} %pad_maximum_fusion.9), channel_id=1, source_target_pairs={{0,4},{4,0},{8,12},{12,8},{1,5},{5,1},{9,13},{13,9},{2,6},{6,2},{1... | collective-permute-start | bytes 1572872 | tf_op jit(solution)/shard_map/ppermute | solution.py:30
  66.3 43.8 %collective-permute-start.17 = (bf16[128,4096]{1,0:T(8,128)(2,1)S(1)}, bf16[128,4096]{1,0:T(8,128)(2,1)S(1)}, u32[]{:S(2)}, u32[]{:S(2)}) collective-permute-start(bf16[128,4096]{1,0:T(8,128)(2,1)S(1)} %pad_maximum_fusion), channel_id=1, source_target_pairs={{0,12},{4,8},{8,4},{12,0},{1,13},{5,9},{9,5},{13,1},{2,14},{6,10},... | collective-permute-start | bytes 3145736 | tf_op jit(solution)/shard_map/ppermute | solution.py:30
  72.5 43.5 %collective-permute-start.19 = (bf16[128,4096]{1,0:T(8,128)(2,1)S(1)}, bf16[128,4096]{1,0:T(8,128)(2,1)S(1)}, u32[]{:S(2)}, u32[]{:S(2)}) collective-permute-start(bf16[128,4096]{1,0:T(8,128)(2,1)S(1)} %pad_maximum_fusion.1), channel_id=1, source_target_pairs={{0,16},{16,0},{32,48},{48,32},{1,17},{17,1},{33,49},{49,33},{2,18}... | collective-permute-start | bytes 3145736 | tf_op jit(solution)/shard_map/ppermute | solution.py:30
  77.1 20.2 %collective-permute-start.8 = (f32[256,256]{1,0:T(8,128)S(1)}, f32[256,256]{1,0:T(8,128)S(1)}, u32[]{:S(2)}, u32[]{:S(2)}) collective-permute-start(f32[256,256]{1,0:T(8,128)S(1)} %pad_maximum_fusion.14), channel_id=1, source_target_pairs={{0,1},{1,0},{2,3},{3,2},{4,5},{5,4},{6,7},{7,6},{8,9},{9,8},{10,11... | collective-permute-start | bytes 786440 | tf_op jit(solution)/shard_map/ppermute | solution.py:95
  87.5 27.0 %collective-permute-start.20 = (bf16[128,4096]{1,0:T(8,128)(2,1)S(1)}, bf16[128,4096]{1,0:T(8,128)(2,1)S(1)}, u32[]{:S(2)}, u32[]{:S(2)}) collective-permute-start(bf16[128,4096]{1,0:T(8,128)(2,1)S(1)} %pad_maximum_fusion.2), channel_id=1, source_target_pairs={{0,4},{4,0},{8,12},{12,8},{1,5},{5,1},{9,13},{13,9},{2,6},{6,2},{1... | collective-permute-start | bytes 3145736 | tf_op jit(solution)/shard_map/ppermute | solution.py:30
  91.0 28.1 %collective-permute-start.21 = (bf16[128,4096]{1,0:T(8,128)(2,1)S(1)}, bf16[128,4096]{1,0:T(8,128)(2,1)S(1)}, u32[]{:S(2)}, u32[]{:S(2)}) collective-permute-start(bf16[128,4096]{1,0:T(8,128)(2,1)S(1)} %pad_maximum_fusion.3), channel_id=1, source_target_pairs={{0,48},{16,32},{32,16},{48,0},{1,49},{17,33},{33,17},{49,1},{2,50}... | collective-permute-start | bytes 3145736 | tf_op jit(solution)/shard_map/ppermute | solution.py:30
  97.4 40.9 %collective-permute-start.23 = (bf16[256,128]{1,0:T(8,128)(2,1)S(1)}, bf16[256,128]{1,0:T(8,128)(2,1)S(1)}, u32[]{:S(2)}, u32[]{:S(2)}) collective-permute-start(bf16[256,128]{1,0:T(8,128)(2,1)S(1)} %get-tuple-element.11), channel_id=1, source_target_pairs={{0,2},{2,0},{1,3},{3,1},{4,6},{6,4},{5,7},{7,5},{8,10},{10,8},{9,1... | collective-permute-start | bytes 196616 | tf_op jit(solution)/shard_map/ppermute | solution.py:99
  111.8 11.7 %collective-permute-start.18 = (f32[384,256]{1,0:T(8,128)S(1)}, f32[384,256]{1,0:T(8,128)S(1)}, u32[]{:S(2)}, u32[]{:S(2)}) collective-permute-start(f32[384,256]{1,0:T(8,128)S(1)} %pad_maximum_fusion.10), channel_id=1, source_target_pairs={{0,1},{1,0},{2,3},{3,2},{4,5},{5,4},{6,7},{7,6},{8,9},{9,8},{10,11... | collective-permute-start | bytes 1179656 | tf_op jit(solution)/shard_map/ppermute | solution.py:95
  120.8 15.4 %collective-permute-start.22 = (f32[384,256]{1,0:T(8,128)S(1)}, f32[384,256]{1,0:T(8,128)S(1)}, u32[]{:S(2)}, u32[]{:S(2)}) collective-permute-start(f32[384,256]{1,0:T(8,128)S(1)} %pad_maximum_fusion.11), channel_id=1, source_target_pairs={{0,1},{1,0},{2,3},{3,2},{4,5},{5,4},{6,7},{7,6},{8,9},{9,8},{10,11... | collective-permute-start | bytes 1179656 | tf_op jit(solution)/shard_map/ppermute | solution.py:95
  123.5 15.8 %collective-permute-start.24 = (bf16[384,128]{1,0:T(8,128)(2,1)S(1)}, bf16[384,128]{1,0:T(8,128)(2,1)S(1)}, u32[]{:S(2)}, u32[]{:S(2)}) collective-permute-start(bf16[384,128]{1,0:T(8,128)(2,1)S(1)} %get-tuple-element.8), channel_id=1, source_target_pairs={{0,2},{2,0},{1,3},{3,1},{4,6},{6,4},{5,7},{7,5},{8,10},{10,8},{9,1... | collective-permute-start | bytes 294920 | tf_op jit(solution)/shard_map/ppermute | solution.py:99
  136.3 22.9 %collective-permute-start.25 = (bf16[384,128]{1,0:T(8,128)(2,1)S(1)}, bf16[384,128]{1,0:T(8,128)(2,1)S(1)}, u32[]{:S(2)}, u32[]{:S(2)}) collective-permute-start(bf16[384,128]{1,0:T(8,128)(2,1)S(1)} %get-tuple-element.5), channel_id=1, source_target_pairs={{0,2},{2,0},{1,3},{3,1},{4,6},{6,4},{5,7},{7,5},{8,10},{10,8},{9,1... | collective-permute-start | bytes 294920 | tf_op jit(solution)/shard_map/ppermute | solution.py:99

commit v4 on v3

v4 whole, which is shorter than its diff:
```python
import itertools
import math

import jax
import jax.numpy as jnp
from jax import lax
from jax.experimental import pallas as pl
from jax.experimental.pallas import tpu as pltpu
from jax.sharding import Mesh
from jax.sharding import PartitionSpec as P

AXES = ("z", "x", "y", "half", "core")
SIZES = (8, 4, 4, 2, 2)
TURNS = ((0, 1, 0), (0, 0, 1), (0, 3, 0), (0, 0, 3))


def condition(block, left, right):
    rows = block.shape[0]
    side = left.shape[0]
    grid = block.astype(jnp.float32).reshape(rows, side, side)
    inner = jnp.einsum("ab,qbc->qac", left, grid, precision=lax.Precision.HIGHEST)
    outer = jnp.einsum("qac,cd->qad", inner, right, precision=lax.Precision.HIGHEST)
    return outer.reshape(rows, side * side).astype(jnp.bfloat16)


def flipped(owners, flip):
    return [tuple(a ^ b for a, b in zip(o, flip)) for o in owners]


def sent(rows, flips):
    names = ("z", "x", "y", "core")
    sizes = tuple(SIZES[AXES.index(n)] for n in names)
    pairs = []
    for source in itertools.product(*map(range, sizes)):
        if flips[source[3]] is not None:
            target = tuple(a ^ b for a, b in zip(source, flips[source[3]] + (0,)))
            pairs.append(tuple(sum(p * math.prod(sizes[k + 1 :]) for k, p in enumerate(at)) for at in (source, target)))
    return lax.ppermute(rows, names, pairs)


def partner(piece, flips):
    return (sent(piece[0], flips),) + tuple(flipped(piece[1 + c], flips[c]) for c in range(2))


def joined(one, two):
    return lax.optimization_barrier(jnp.concatenate([one[0], two[0]], 1)), one[1] + two[1], one[2] + two[2]


def place_kernel(place_ref, *refs):
    count = (len(refs) - 2) // 2
    out_ref, total = refs[-2], refs[-1]
    first = 0
    for own_ref, came_ref in zip(refs[:count], refs[count : 2 * count]):
        rows = own_ref.shape[0]
        total[first : first + rows, :] = own_ref[...] + came_ref[...].astype(jnp.float32)
        first += rows
    group = out_ref.shape[0] // place_ref.shape[0]

    def step(k, carry):
        source = pl.ds(pl.multiple_of(k * group, group), group)
        target = pl.ds(pl.multiple_of(place_ref[k] * group, group), group)
        out_ref[target, :] = total[source, :]
        return carry

    lax.fori_loop(0, place_ref.shape[0], step, 0, unroll=8)


def place(own, came, places):
    rows = sum(a.shape[0] for a in own)
    shape = (rows, own[0].shape[1])
    vmem = pl.BlockSpec(memory_space=pltpu.VMEM)
    return pl.pallas_call(
        place_kernel,
        out_shape=jax.ShapeDtypeStruct(shape, jnp.float32),
        in_specs=[pl.BlockSpec(memory_space=pltpu.SMEM)] + [vmem] * (2 * len(own)),
        out_specs=vmem,
        scratch_shapes=[pltpu.VMEM(shape, jnp.float32)],
        compiler_params=pltpu.CompilerParams(vmem_limit_bytes=8 * 2**20),
    )(places, *own, *came)


def on_device(train_grads, query_grads, left_factor, right_factor):
    half, core = lax.axis_index("half"), lax.axis_index("core")
    width = train_grads.shape[1] // 4
    swap = [(0, 1), (1, 0)]

    own = condition(query_grads[0], left_factor[0], right_factor[0])
    pair = jnp.concatenate([own, sent(own, [(4, 0, 0)] * 2)], 0)
    both = lax.optimization_barrier(jnp.stack([pair, lax.ppermute(pair, "core", swap)]))
    first = sent(both, [(2, 0, 0), (1, 0, 0)])
    second = sent(both, [None, (3, 0, 0)])
    trains = (train_grads[0], lax.ppermute(train_grads[0], "core", swap))
    near = [(0, 0, 0), (4, 0, 0)]
    held = [
        (jnp.where(core == 0, both, first), near, flipped(near, (1, 0, 0))),
        (jnp.where(core == 0, first, second), flipped(near, (2, 0, 0)), flipped(near, (3, 0, 0))),
    ]
    for step in range(len(TURNS)):
        turn = [TURNS[(k + step) % len(TURNS)] for k in range(4)]
        came = [partner(p, turn[2 * k : 2 * k + 2]) for k, p in enumerate(held)]
        if step < len(TURNS) - 1:
            held = [joined(*pieces) for pieces in zip(held, came)]

    kept, arrived, owners = [], [], ([], [])
    for last in (False, True):
        pieces = held[1:] + came if last else held[:1]
        scores = jnp.concatenate(
            [
                sum(
                    lax.dot_general(r, t, (((1,), (1,)), ((), ())), preferred_element_type=jnp.float32)
                    for r, t in zip(rows, trains)
                )
                for rows, _, _ in pieces
            ],
            0,
        )
        shares = [scores[:, k * width : (k + 1) * width] for k in range(4)]
        away = [jnp.where(core == 0, shares[2 * k + 1], shares[2 * k]) for k in range(2)]
        here = [jnp.where(core == 0, shares[2 * k], shares[2 * k + 1]) for k in range(2)]
        other = lax.ppermute(jnp.concatenate(away, 1), "core", swap)
        whole = [jnp.concatenate([here[k], other[:, k * width : (k + 1) * width]], 0) for k in range(2)]
        kept.append(jnp.where(half == 0, whole[0], whole[1]))
        cross = jnp.where(half == 0, whole[1], whole[0]).astype(jnp.bfloat16)
        arrived.append(lax.ppermute(cross, "half", swap))
        if not last:
            arrived[0], rows = lax.optimization_barrier((arrived[0], came[0][0]))
            came[0] = (rows,) + came[0][1:]
        for c in range(2):
            owners[c].extend(o for k in (1 + c, 2 - c) for piece in pieces for o in piece[k])
    flips = jnp.where(core == 0, jnp.array(owners[0], jnp.int32).T, jnp.array(owners[1], jnp.int32).T)
    z, x, y = (lax.axis_index(n) ^ flips[k] for k, n in enumerate("zxy"))
    places = (z * SIZES[1] + x) * SIZES[2] + y
    return place(kept, arrived, places)


def solution(mesh):
    fine = Mesh(mesh.devices.reshape(SIZES), AXES)
    dp, layer = ("z", "x", "y"), ("half", "core")
    return jax.shard_map(
        on_device,
        mesh=fine,
        in_specs=(P(layer, dp, None), P(layer, dp, None), P(layer, None, None), P(layer, None, None)),
        out_specs=P(None, dp + layer),
        check_vma=False,
    )
```

time: 162 us -> 166 us (1.025)
  starting transfers between devices: 114 us -> 98.5 us
  waiting for transfers between devices: 27.5 us -> 38.7 us
  matrix products: 13.6 us -> 22.6 us
    ppermute x26 -> x17, starting transfers between devices: 114 us -> 98.5 us  [the longest x11 41 us: sent(): return lax.ppermute(rows, names, pairs)]
    ppermute x26 -> x17, waiting for transfers between devices: 27.5 us -> 38.7 us  [the longest x11 27.8 us: sent(): return lax.ppermute(rows, names, pairs)]
    dot_general x8, matrix products: 12.2 us -> 21.2 us  [on_device(): lax.dot_general(r, t, (((1,), (1,)), ((), ())), preferred_element_type=jn...]
  transfers between devices with their start and end apart: 26 -> 17, of which waited for: 7 -> 11; matrix products, arithmetic and copies ran while one was open for 9% -> 11% of each run, Pallas kernels for 0% -> 0%
where the time goes in v4:
time: 166 us; the launch traced here: 165 us
  starting transfers between devices  98.5 us (59%)
  waiting for transfers between devices  38.7 us (23%)
  matrix products  22.6 us (14%)
  other arithmetic  2.28 us (1%)
    ppermute x11, starting transfers between devices, sent(): return lax.ppermute(rows, names, pairs)  41 us
    ppermute x2, starting transfers between devices, on_device(): arrived.append(lax.ppermute(cross, 'half', swap))  28.1 us
    ppermute x11, waiting for transfers between devices, sent(): return lax.ppermute(rows, names, pairs)  27.8 us
    dot_general x8, matrix products, on_device(): lax.dot_general(r, t, (((1,), (1,)), ((), ())), preferred_element_type=jn...  21.2 us
    ppermute x2, starting transfers between devices, on_device(): other = lax.ppermute(jnp.concatenate(away, 1), 'core', swap)  19.2 us
    ppermute x2, waiting for transfers between devices, on_device(): arrived.append(lax.ppermute(cross, 'half', swap))  8.61 us
    ppermute x1, starting transfers between devices, on_device(): lax.ppermute(pair, 'core', swap)  8.31 us
  transfers between devices with their start and end apart: 17, of which 11 were waited for; matrix products, arithmetic and copies ran while one was open for 11% of the time, Pallas kernels for 0%

profile of v4, /device:TPU:1, one launch (start us, length us, event | category | flops | bytes accessed | tf_op | source)
XLA Modules:
  0.0 165.5 jit_solution(2839060112145321756)
XLA Ops:
  0.0 1.0 reshape.17
  1.1 0.2 convolution_bitcast_fusion
  1.3 1.1 convolution_convert_fusion
  2.4 0.2 convert_element_type.14
  2.6 9.6 %collective-permute-start = (bf16[8,4096]{1,0:T(8,128)(2,1)S(1)}, bf16[8,4096]{1,0:T(8,128)(2,1)S(1)}, u32[]{:S(2)}, u32[]{:S(2)}) collective-permute-start(bf16[8,4096]{1,0:T(8,128)(2,1)S(1)} %convert_element_type.14), channel_id=1, source_target_pairs={{0,256},{1,257},{4,260},{5,261},{8,264},{9,265},{12,268},{13,269},... | collective-permute-start | bytes 196616 | tf_op jit(solution)/shard_map/ppermute | solution.py:38
  12.3 1.6 collective-permute-done
  13.9 8.3 %collective-permute-start.1 = (bf16[16,4096]{1,0:T(8,128)(2,1)S(1)}, bf16[16,4096]{1,0:T(8,128)(2,1)S(1)}, u32[]{:S(2)}, u32[]{:S(2)}) collective-permute-start(bf16[16,4096]{1,0:T(8,128)(2,1)S(1)} %constant_dynamic-update-slice_fusion), channel_id=1, source_target_pairs={{0,1},{1,0},{2,3},{3,2},{4,5},{5,4},{6,7},{7,6},{8,9},{9,8},{10,11... | collective-permute-start | bytes 393224 | tf_op jit(solution)/shard_map/ppermute | solution.py:89
  22.2 1.0 collective-permute-done.1
  23.2 1.9 %collective-permute-start.2 = (bf16[2,16,4096]{2,1,0:T(8,128)(2,1)S(1)}, bf16[2,16,4096]{2,1,0:T(8,128)(2,1)S(1)}, u32[]{:S(2)}, u32[]{:S(2)}) collective-permute-start(bf16[2,16,4096]{2,1,0:T(8,128)(2,1)S(1)} %pad_maximum_fusion.10), channel_id=1, source_target_pairs={{0,128},{1,65},{4,132},{5,69},{8,136},{9,73},{12,140},{13,77},{16,... | collective-permute-start | bytes 786440 | tf_op jit(solution)/shard_map/ppermute | solution.py:38
  25.1 3.3 %collective-permute-start.8 = (bf16[2,16,4096]{2,1,0:T(8,128)(2,1)S(1)}, bf16[2,16,4096]{2,1,0:T(8,128)(2,1)S(1)}, u32[]{:S(2)}, u32[]{:S(2)}) collective-permute-start(bf16[2,16,4096]{2,1,0:T(8,128)(2,1)S(1)} %pad_maximum_fusion.10), channel_id=1, source_target_pairs={{1,193},{5,197},{9,201},{13,205},{17,209},{21,213},{25,217},{29,22... | collective-permute-start | bytes 786440 | tf_op jit(solution)/shard_map/ppermute | solution.py:38
  28.5 1.9 %collective-permute-start.6 = (bf16[512,4096]{1,0:T(8,128)(2,1)}, bf16[512,4096]{1,0:T(8,128)(2,1)}, u32[]{:S(2)}, u32[]{:S(2)}) collective-permute-start(bf16[512,4096]{1,0:T(8,128)(2,1)} %bitcast.59), channel_id=1, source_target_pairs={{0,1},{1,0},{2,3},{3,2},{4,5},{5,4},{6,7},{7,6},{8,9},{9,8},{10,11... | collective-permute-start | bytes 12582920 | tf_op jit(solution)/shard_map/ppermute | solution.py:92
  30.4 1.1 collective-permute-done.2
  31.5 4.5 %collective-permute-done.8 = bf16[2,16,4096]{2,1,0:T(8,128)(2,1)S(1)} collective-permute-done((bf16[2,16,4096]{2,1,0:T(8,128)(2,1)S(1)}, bf16[2,16,4096]{2,1,0:T(8,128)(2,1)S(1)}, u32[]{:S(2)}, u32[]{:S(2)}) %collective-permute-start.8) | collective-permute-done | bytes 262176 | tf_op jit(solution)/shard_map/ppermute | solution.py:38
  36.1 4.6 %collective-permute-start.9 = (bf16[2,16,4096]{2,1,0:T(8,128)(2,1)S(1)}, bf16[2,16,4096]{2,1,0:T(8,128)(2,1)S(1)}, u32[]{:S(2)}, u32[]{:S(2)}) collective-permute-start(bf16[2,16,4096]{2,1,0:T(8,128)(2,1)S(1)} %get-tuple-element.15), channel_id=1, source_target_pairs={{0,48},{1,13},{4,52},{5,9},{8,56},{9,5},{12,60},{13,1},{16,32},{17... | collective-permute-start | bytes 786440 | tf_op jit(solution)/shard_map/ppermute | solution.py:38
  40.7 1.9 %collective-permute-start.3 = (bf16[2,16,4096]{2,1,0:T(8,128)(2,1)S(1)}, bf16[2,16,4096]{2,1,0:T(8,128)(2,1)S(1)}, u32[]{:S(2)}, u32[]{:S(2)}) collective-permute-start(bf16[2,16,4096]{2,1,0:T(8,128)(2,1)S(1)} %get-tuple-element.16), channel_id=1, source_target_pairs={{0,16},{1,5},{4,20},{5,1},{8,24},{9,13},{12,28},{13,9},{16,0},{17,... | collective-permute-start | bytes 786440 | tf_op jit(solution)/shard_map/ppermute | solution.py:38
  42.6 1.8 %collective-permute-done.9 = bf16[2,16,4096]{2,1,0:T(8,128)(2,1)S(1)} collective-permute-done((bf16[2,16,4096]{2,1,0:T(8,128)(2,1)S(1)}, bf16[2,16,4096]{2,1,0:T(8,128)(2,1)S(1)}, u32[]{:S(2)}, u32[]{:S(2)}) %collective-permute-start.9) | collective-permute-done | bytes 262176 | tf_op jit(solution)/shard_map/ppermute | solution.py:38
  44.5 3.1 %collective-permute-start.10 = (bf16[2,32,4096]{2,1,0:T(8,128)(2,1)S(1)}, bf16[2,32,4096]{2,1,0:T(8,128)(2,1)S(1)}, u32[]{:S(2)}, u32[]{:S(2)}) collective-permute-start(bf16[2,32,4096]{2,1,0:T(8,128)(2,1)S(1)} %pad_maximum_fusion.6), channel_id=1, source_target_pairs={{0,12},{1,17},{4,8},{5,21},{8,4},{9,25},{12,0},{13,29},{16,28},{17... | collective-permute-start | bytes 1572872 | tf_op jit(solution)/shard_map/ppermute | solution.py:38
  47.6 0.5 collective-permute-done.3
  48.2 4.4 %collective-permute-start.4 = (bf16[2,32,4096]{2,1,0:T(8,128)(2,1)S(1)}, bf16[2,32,4096]{2,1,0:T(8,128)(2,1)S(1)}, u32[]{:S(2)}, u32[]{:S(2)}) collective-permute-start(bf16[2,32,4096]{2,1,0:T(8,128)(2,1)S(1)} %pad_maximum_fusion.5), channel_id=1, source_target_pairs={{0,4},{1,49},{4,0},{5,53},{8,12},{9,57},{12,8},{13,61},{16,20},{17... | collective-permute-start | bytes 1572872 | tf_op jit(solution)/shard_map/ppermute | solution.py:38
  52.6 5.0 %collective-permute-done.10 = bf16[2,32,4096]{2,1,0:T(8,128)(2,1)S(1)} collective-permute-done((bf16[2,32,4096]{2,1,0:T(8,128)(2,1)S(1)}, bf16[2,32,4096]{2,1,0:T(8,128)(2,1)S(1)}, u32[]{:S(2)}, u32[]{:S(2)}) %collective-permute-start.10) | collective-permute-done | bytes 524320 | tf_op jit(solution)/shard_map/ppermute | solution.py:38
  57.5 0.1 pad_maximum_fusion.3
  57.6 1.9 %collective-permute-start.11 = (bf16[2,64,4096]{2,1,0:T(8,128)(2,1)S(1)}, bf16[2,64,4096]{2,1,0:T(8,128)(2,1)S(1)}, u32[]{:S(2)}, u32[]{:S(2)}) collective-permute-start(bf16[2,64,4096]{2,1,0:T(8,128)(2,1)S(1)} %pad_maximum_fusion.3), channel_id=1, source_target_pairs={{0,16},{1,5},{4,20},{5,1},{8,24},{9,13},{12,28},{13,9},{16,0},{17,... | collective-permute-start | bytes 3145736 | tf_op jit(solution)/shard_map/ppermute | solution.py:38
  59.5 0.1 collective-permute-done.4
  59.6 0.1 pad_maximum_fusion.2
  59.7 4.5 %collective-permute-start.5 = (bf16[2,64,4096]{2,1,0:T(8,128)(2,1)S(1)}, bf16[2,64,4096]{2,1,0:T(8,128)(2,1)}, u32[]{:S(2)}, u32[]{:S(2)}) collective-permute-start(bf16[2,64,4096]{2,1,0:T(8,128)(2,1)S(1)} %pad_maximum_fusion.2), channel_id=1, source_target_pairs={{0,48},{1,13},{4,52},{5,9},{8,56},{9,5},{12,60},{13,1},{16,32},{17... | collective-permute-start | bytes 3145736 | tf_op jit(solution)/shard_map/ppermute | solution.py:38
  64.2 13.2 %collective-permute-done.11 = bf16[2,64,4096]{2,1,0:T(8,128)(2,1)S(1)} collective-permute-done((bf16[2,64,4096]{2,1,0:T(8,128)(2,1)S(1)}, bf16[2,64,4096]{2,1,0:T(8,128)(2,1)S(1)}, u32[]{:S(2)}, u32[]{:S(2)}) %collective-permute-start.11) | collective-permute-done | bytes 1048608 | tf_op jit(solution)/shard_map/ppermute | solution.py:38
  77.4 0.1 pad_maximum_fusion.1
  77.6 1.6 pad_maximum_fusion
  79.2 2.1 %collective-permute-start.13 = (bf16[2,128,4096]{2,1,0:T(8,128)(2,1)S(1)}, bf16[2,128,4096]{2,1,0:T(8,128)(2,1)S(1)}, u32[]{:S(2)}, u32[]{:S(2)}) collective-permute-start(bf16[2,128,4096]{2,1,0:T(8,128)(2,1)S(1)} %pad_maximum_fusion), channel_id=1, source_target_pairs={{0,12},{1,17},{4,8},{5,21},{8,4},{9,25},{12,0},{13,29},{16,28},{17... | collective-permute-start | bytes 6291464 | tf_op jit(solution)/shard_map/ppermute | solution.py:38
  81.3 3.5 %collective-permute-start.14 = (bf16[2,128,4096]{2,1,0:T(8,128)(2,1)S(1)}, bf16[2,128,4096]{2,1,0:T(8,128)(2,1)S(1)}, u32[]{:S(2)}, u32[]{:S(2)}) collective-permute-start(bf16[2,128,4096]{2,1,0:T(8,128)(2,1)S(1)} %pad_maximum_fusion.1), channel_id=1, source_target_pairs={{0,4},{1,49},{4,0},{5,53},{8,12},{9,57},{12,8},{13,61},{16,20},{17... | collective-permute-start | bytes 6291464 | tf_op jit(solution)/shard_map/ppermute | solution.py:38
  84.8 3.8 %fusion.4 = f32[128,512]{1,0:T(8,128)S(1)} fusion(bf16[512,4096]{1,0:T(8,128)(2,1)} %collective-permute-done.6, bf16[2,128,4096]{2,1,0:T(8,128)(2,1)S(1)} %pad_maximum_fusion), kind=kOutput, calls=%fused_computation.15 | convolution fusion | flops 536870912 | bytes 5505024 | tf_op jit(solution)/shard_map/dot_general | solution.py:110
  88.5 1.5 fusion.6
  90.1 17.0 %collective-permute-start.7 = (f32[128,256]{1,0:T(8,128)S(1)}, f32[128,256]{1,0:T(8,128)S(1)}, u32[]{:S(2)}, u32[]{:S(2)}) collective-permute-start(f32[128,256]{1,0:T(8,128)S(1)} %pad_maximum_fusion.11), channel_id=1, source_target_pairs={{0,1},{1,0},{2,3},{3,2},{4,5},{5,4},{6,7},{7,6},{8,9},{9,8},{10,11... | collective-permute-start | bytes 393224 | tf_op jit(solution)/shard_map/ppermute | solution.py:120
  107.1 3.8 %fusion.1 = f32[128,512]{1,0:T(8,128)S(1)} fusion(bf16[512,4096]{1,0:T(8,128)(2,1)} %collective-permute-done.6, bf16[2,128,4096]{2,1,0:T(8,128)(2,1)S(1)} %pad_maximum_fusion.1), kind=kOutput, calls=%fused_computation.10 | convolution fusion | flops 536870912 | bytes 5505024 | tf_op jit(solution)/shard_map/dot_general | solution.py:110
  110.9 1.5 fusion.3
  112.5 15.2 %collective-permute-start.12 = (bf16[256,128]{1,0:T(8,128)(2,1)S(1)}, bf16[256,128]{1,0:T(8,128)(2,1)S(1)}, u32[]{:S(2)}, u32[]{:S(2)}) collective-permute-start(bf16[256,128]{1,0:T(8,128)(2,1)S(1)} %select_convert_fusion.1), channel_id=1, source_target_pairs={{0,2},{2,0},{1,3},{3,1},{4,6},{6,4},{5,7},{7,5},{8,10},{10,8},{9,1... | collective-permute-start | bytes 196616 | tf_op jit(solution)/shard_map/ppermute | solution.py:124
  127.7 3.8 %fusion = f32[128,512]{1,0:T(8,128)S(1)} fusion(bf16[512,4096]{1,0:T(8,128)(2,1)} %collective-permute-done.6, bf16[2,128,4096]{2,1,0:T(8,128)(2,1)S(1)} %collective-permute-done.14), kind=kOutput, calls=%fused_computation.7 | convolution fusion | flops 536870912 | bytes 5505024 | tf_op jit(solution)/shard_map/dot_general | solution.py:110
  131.5 1.5 convolution_add_fusion
  133.0 1.5 fusion.8
  134.6 0.0 copy-start.2
  134.6 3.8 %convolution_add_fusion.1 = f32[128,512]{1,0:T(8,128)S(1)} fusion(f32[128,512]{1,0:T(8,128)S(1)} %fusion.8, bf16[512,4096]{1,0:T(8,128)(2,1)} %collective-permute-done.6, bf16[2,128,4096]{2,1,0:T(8,128)(2,1)S(1)} %collective-permute-done.13), kind=kOutput, calls=%fused_computation.4 | convolution fusion | flops 536936448 | bytes 5767168 | tf_op jit(solution)/shard_map/dot_general | solution.py:110
  138.4 0.1 pad_maximum_fusion.4
  138.4 0.1 slice_select_fusion.3
  138.5 2.2 %collective-permute-start.15 = (f32[384,256]{1,0:T(8,128)S(1)}, f32[384,256]{1,0:T(8,128)S(1)}, u32[]{:S(2)}, u32[]{:S(2)}) collective-permute-start(f32[384,256]{1,0:T(8,128)S(1)} %pad_maximum_fusion.7), channel_id=1, source_target_pairs={{0,1},{1,0},{2,3},{3,2},{4,5},{5,4},{6,7},{7,6},{8,9},{9,8},{10,11... | collective-permute-start | bytes 1179656 | tf_op jit(solution)/shard_map/ppermute | solution.py:120
  140.8 1.4 collective-permute-done.15
  142.2 12.9 %collective-permute-start.16 = (bf16[768,128]{1,0:T(8,128)(2,1)S(1)}, bf16[768,128]{1,0:T(8,128)(2,1)S(1)}, u32[]{:S(2)}, u32[]{:S(2)}) collective-permute-start(bf16[768,128]{1,0:T(8,128)(2,1)S(1)} %select_convert_fusion), channel_id=1, source_target_pairs={{0,2},{2,0},{1,3},{3,1},{4,6},{6,4},{5,7},{7,5},{8,10},{10,8},{9,1... | collective-permute-start | bytes 589832 | tf_op jit(solution)/shard_map/ppermute | solution.py:124
  155.3 8.6 %collective-permute-done.16.refs_3_ = bf16[768,128]{1,0:T(8,128)(2,1)S(1)} collective-permute-done((bf16[768,128]{1,0:T(8,128)(2,1)S(1)}, bf16[768,128]{1,0:T(8,128)(2,1)S(1)}, u32[]{:S(2)}, u32[]{:S(2)}) %collective-permute-start.16) | collective-permute-done | bytes 196640 | tf_op jit(solution)/shard_map/ppermute | solution.py:124
  163.9 1.6 shard_map.64
  (30 shorter events, 0.4 us)
Async XLA Ops:
  0.0 1.0 copy-start
  2.6 11.3 %collective-permute-start = (bf16[8,4096]{1,0:T(8,128)(2,1)S(1)}, bf16[8,4096]{1,0:T(8,128)(2,1)S(1)}, u32[]{:S(2)}, u32[]{:S(2)}) collective-permute-start(bf16[8,4096]{1,0:T(8,128)(2,1)S(1)} %convert_element_type.14), channel_id=1, source_target_pairs={{0,256},{1,257},{4,260},{5,261},{8,264},{9,265},{12,268},{13,269},... | collective-permute-start | bytes 196616 | tf_op jit(solution)/shard_map/ppermute | solution.py:38
  13.9 9.3 %collective-permute-start.1 = (bf16[16,4096]{1,0:T(8,128)(2,1)S(1)}, bf16[16,4096]{1,0:T(8,128)(2,1)S(1)}, u32[]{:S(2)}, u32[]{:S(2)}) collective-permute-start(bf16[16,4096]{1,0:T(8,128)(2,1)S(1)} %constant_dynamic-update-slice_fusion), channel_id=1, source_target_pairs={{0,1},{1,0},{2,3},{3,2},{4,5},{5,4},{6,7},{7,6},{8,9},{9,8},{10,11... | collective-permute-start | bytes 393224 | tf_op jit(solution)/shard_map/ppermute | solution.py:89
  23.2 8.3 %collective-permute-start.2 = (bf16[2,16,4096]{2,1,0:T(8,128)(2,1)S(1)}, bf16[2,16,4096]{2,1,0:T(8,128)(2,1)S(1)}, u32[]{:S(2)}, u32[]{:S(2)}) collective-permute-start(bf16[2,16,4096]{2,1,0:T(8,128)(2,1)S(1)} %pad_maximum_fusion.10), channel_id=1, source_target_pairs={{0,128},{1,65},{4,132},{5,69},{8,136},{9,73},{12,140},{13,77},{16,... | collective-permute-start | bytes 786440 | tf_op jit(solution)/shard_map/ppermute | solution.py:38
  25.1 10.9 %collective-permute-start.8 = (bf16[2,16,4096]{2,1,0:T(8,128)(2,1)S(1)}, bf16[2,16,4096]{2,1,0:T(8,128)(2,1)S(1)}, u32[]{:S(2)}, u32[]{:S(2)}) collective-permute-start(bf16[2,16,4096]{2,1,0:T(8,128)(2,1)S(1)} %pad_maximum_fusion.10), channel_id=1, source_target_pairs={{1,193},{5,197},{9,201},{13,205},{17,209},{21,213},{25,217},{29,22... | collective-permute-start | bytes 786440 | tf_op jit(solution)/shard_map/ppermute | solution.py:38
  28.5 56.3 %collective-permute-start.6 = (bf16[512,4096]{1,0:T(8,128)(2,1)}, bf16[512,4096]{1,0:T(8,128)(2,1)}, u32[]{:S(2)}, u32[]{:S(2)}) collective-permute-start(bf16[512,4096]{1,0:T(8,128)(2,1)} %bitcast.59), channel_id=1, source_target_pairs={{0,1},{1,0},{2,3},{3,2},{4,5},{5,4},{6,7},{7,6},{8,9},{9,8},{10,11... | collective-permute-start | bytes 12582920 | tf_op jit(solution)/shard_map/ppermute | solution.py:92
  36.1 8.4 %collective-permute-start.9 = (bf16[2,16,4096]{2,1,0:T(8,128)(2,1)S(1)}, bf16[2,16,4096]{2,1,0:T(8,128)(2,1)S(1)}, u32[]{:S(2)}, u32[]{:S(2)}) collective-permute-start(bf16[2,16,4096]{2,1,0:T(8,128)(2,1)S(1)} %get-tuple-element.15), channel_id=1, source_target_pairs={{0,48},{1,13},{4,52},{5,9},{8,56},{9,5},{12,60},{13,1},{16,32},{17... | collective-permute-start | bytes 786440 | tf_op jit(solution)/shard_map/ppermute | solution.py:38
  40.7 7.4 %collective-permute-start.3 = (bf16[2,16,4096]{2,1,0:T(8,128)(2,1)S(1)}, bf16[2,16,4096]{2,1,0:T(8,128)(2,1)S(1)}, u32[]{:S(2)}, u32[]{:S(2)}) collective-permute-start(bf16[2,16,4096]{2,1,0:T(8,128)(2,1)S(1)} %get-tuple-element.16), channel_id=1, source_target_pairs={{0,16},{1,5},{4,20},{5,1},{8,24},{9,13},{12,28},{13,9},{16,0},{17,... | collective-permute-start | bytes 786440 | tf_op jit(solution)/shard_map/ppermute | solution.py:38
  44.5 13.0 %collective-permute-start.10 = (bf16[2,32,4096]{2,1,0:T(8,128)(2,1)S(1)}, bf16[2,32,4096]{2,1,0:T(8,128)(2,1)S(1)}, u32[]{:S(2)}, u32[]{:S(2)}) collective-permute-start(bf16[2,32,4096]{2,1,0:T(8,128)(2,1)S(1)} %pad_maximum_fusion.6), channel_id=1, source_target_pairs={{0,12},{1,17},{4,8},{5,21},{8,4},{9,25},{12,0},{13,29},{16,28},{17... | collective-permute-start | bytes 1572872 | tf_op jit(solution)/shard_map/ppermute | solution.py:38
  48.2 11.4 %collective-permute-start.4 = (bf16[2,32,4096]{2,1,0:T(8,128)(2,1)S(1)}, bf16[2,32,4096]{2,1,0:T(8,128)(2,1)S(1)}, u32[]{:S(2)}, u32[]{:S(2)}) collective-permute-start(bf16[2,32,4096]{2,1,0:T(8,128)(2,1)S(1)} %pad_maximum_fusion.5), channel_id=1, source_target_pairs={{0,4},{1,49},{4,0},{5,53},{8,12},{9,57},{12,8},{13,61},{16,20},{17... | collective-permute-start | bytes 1572872 | tf_op jit(solution)/shard_map/ppermute | solution.py:38
  57.6 19.8 %collective-permute-start.11 = (bf16[2,64,4096]{2,1,0:T(8,128)(2,1)S(1)}, bf16[2,64,4096]{2,1,0:T(8,128)(2,1)S(1)}, u32[]{:S(2)}, u32[]{:S(2)}) collective-permute-start(bf16[2,64,4096]{2,1,0:T(8,128)(2,1)S(1)} %pad_maximum_fusion.3), channel_id=1, source_target_pairs={{0,16},{1,5},{4,20},{5,1},{8,24},{9,13},{12,28},{13,9},{16,0},{17,... | collective-permute-start | bytes 3145736 | tf_op jit(solution)/shard_map/ppermute | solution.py:38
  59.7 17.9 %collective-permute-start.5 = (bf16[2,64,4096]{2,1,0:T(8,128)(2,1)S(1)}, bf16[2,64,4096]{2,1,0:T(8,128)(2,1)}, u32[]{:S(2)}, u32[]{:S(2)}) collective-permute-start(bf16[2,64,4096]{2,1,0:T(8,128)(2,1)S(1)} %pad_maximum_fusion.2), channel_id=1, source_target_pairs={{0,48},{1,13},{4,52},{5,9},{8,56},{9,5},{12,60},{13,1},{16,32},{17... | collective-permute-start | bytes 3145736 | tf_op jit(solution)/shard_map/ppermute | solution.py:38
  77.6 11.0 %copy-start.1 = (bf16[1,512,4096]{2,1,0:T(8,128)(2,1)S(1)}, bf16[1,512,4096]{2,1,0:T(8,128)(2,1)}, u32[]{:S(2)}) copy-start(bf16[1,512,4096]{2,1,0:T(8,128)(2,1)} %param.6) | copy-start | bytes 12582916
  79.2 53.8 %collective-permute-start.13 = (bf16[2,128,4096]{2,1,0:T(8,128)(2,1)S(1)}, bf16[2,128,4096]{2,1,0:T(8,128)(2,1)S(1)}, u32[]{:S(2)}, u32[]{:S(2)}) collective-permute-start(bf16[2,128,4096]{2,1,0:T(8,128)(2,1)S(1)} %pad_maximum_fusion), channel_id=1, source_target_pairs={{0,12},{1,17},{4,8},{5,21},{8,4},{9,25},{12,0},{13,29},{16,28},{17... | collective-permute-start | bytes 6291464 | tf_op jit(solution)/shard_map/ppermute | solution.py:38
  81.3 46.4 %collective-permute-start.14 = (bf16[2,128,4096]{2,1,0:T(8,128)(2,1)S(1)}, bf16[2,128,4096]{2,1,0:T(8,128)(2,1)S(1)}, u32[]{:S(2)}, u32[]{:S(2)}) collective-permute-start(bf16[2,128,4096]{2,1,0:T(8,128)(2,1)S(1)} %pad_maximum_fusion.1), channel_id=1, source_target_pairs={{0,4},{1,49},{4,0},{5,53},{8,12},{9,57},{12,8},{13,61},{16,20},{17... | collective-permute-start | bytes 6291464 | tf_op jit(solution)/shard_map/ppermute | solution.py:38
  90.1 22.3 %collective-permute-start.7 = (f32[128,256]{1,0:T(8,128)S(1)}, f32[128,256]{1,0:T(8,128)S(1)}, u32[]{:S(2)}, u32[]{:S(2)}) collective-permute-start(f32[128,256]{1,0:T(8,128)S(1)} %pad_maximum_fusion.11), channel_id=1, source_target_pairs={{0,1},{1,0},{2,3},{3,2},{4,5},{5,4},{6,7},{7,6},{8,9},{9,8},{10,11... | collective-permute-start | bytes 393224 | tf_op jit(solution)/shard_map/ppermute | solution.py:120
  112.5 20.5 %collective-permute-start.12 = (bf16[256,128]{1,0:T(8,128)(2,1)S(1)}, bf16[256,128]{1,0:T(8,128)(2,1)S(1)}, u32[]{:S(2)}, u32[]{:S(2)}) collective-permute-start(bf16[256,128]{1,0:T(8,128)(2,1)S(1)} %select_convert_fusion.1), channel_id=1, source_target_pairs={{0,2},{2,0},{1,3},{3,1},{4,6},{6,4},{5,7},{7,5},{8,10},{10,8},{9,1... | collective-permute-start | bytes 196616 | tf_op jit(solution)/shard_map/ppermute | solution.py:124
  134.6 6.2 %copy-start.2 = (s32[128,3]{0,1:T(4,128)S(1)}, s32[128,3]{0,1:T(4,128)}, u32[]{:S(2)}) copy-start(s32[128,3]{0,1:T(4,128)} %constant.29.clone) | copy-start | bytes 4612
  134.6 6.2 %copy-start.3 = (s32[128,3]{0,1:T(4,128)S(1)}, s32[128,3]{0,1:T(4,128)}, u32[]{:S(2)}) copy-start(s32[128,3]{0,1:T(4,128)} %constant.30.clone) | copy-start | bytes 4612
  138.5 3.6 %collective-permute-start.15 = (f32[384,256]{1,0:T(8,128)S(1)}, f32[384,256]{1,0:T(8,128)S(1)}, u32[]{:S(2)}, u32[]{:S(2)}) collective-permute-start(f32[384,256]{1,0:T(8,128)S(1)} %pad_maximum_fusion.7), channel_id=1, source_target_pairs={{0,1},{1,0},{2,3},{3,2},{4,5},{5,4},{6,7},{7,6},{8,9},{9,8},{10,11... | collective-permute-start | bytes 1179656 | tf_op jit(solution)/shard_map/ppermute | solution.py:120
  142.2 21.6 %collective-permute-start.16 = (bf16[768,128]{1,0:T(8,128)(2,1)S(1)}, bf16[768,128]{1,0:T(8,128)(2,1)S(1)}, u32[]{:S(2)}, u32[]{:S(2)}) collective-permute-start(bf16[768,128]{1,0:T(8,128)(2,1)S(1)} %select_convert_fusion), channel_id=1, source_target_pairs={{0,2},{2,0},{1,3},{3,1},{4,6},{6,4},{5,7},{7,5},{8,10},{10,8},{9,1... | collective-permute-start | bytes 589832 | tf_op jit(solution)/shard_map/ppermute | solution.py:124

commit v5 on v4

--- a/solution.py
+++ b/solution.py
@@ -84,17 +84,22 @@
     width = train_grads.shape[1] // 4
     swap = [(0, 1), (1, 0)]
 
+    trains = [train_grads[0], lax.ppermute(train_grads[0], "core", swap)]
     own = condition(query_grads[0], left_factor[0], right_factor[0])
-    pair = jnp.concatenate([own, sent(own, [(4, 0, 0)] * 2)], 0)
-    both = lax.optimization_barrier(jnp.stack([pair, lax.ppermute(pair, "core", swap)]))
-    first = sent(both, [(2, 0, 0), (1, 0, 0)])
-    second = sent(both, [None, (3, 0, 0)])
-    trains = (train_grads[0], lax.ppermute(train_grads[0], "core", swap))
-    near = [(0, 0, 0), (4, 0, 0)]
+    both = lax.optimization_barrier(jnp.stack([own, lax.ppermute(own, "core", swap)]))
+    rows = both.shape[1]
+    pair = lax.optimization_barrier(jnp.concatenate([both, sent(both, [(4, 0, 0), (1, 0, 0)])], 1))
+    pair, trains[1] = lax.optimization_barrier((pair, trains[1]))
+    more = sent(pair, [(2, 0, 0), (4, 0, 0)])
+    first = jnp.where(core == 0, pair, jnp.concatenate([pair[:, rows:], more[:, rows:]], 1))
+    first = lax.optimization_barrier(first)
+    second = jnp.where(core == 0, more, sent(first, [None, (2, 0, 0)]))
     held = [
-        (jnp.where(core == 0, both, first), near, flipped(near, (1, 0, 0))),
-        (jnp.where(core == 0, first, second), flipped(near, (2, 0, 0)), flipped(near, (3, 0, 0))),
+        (first, [(0, 0, 0), (4, 0, 0)], [(1, 0, 0), (5, 0, 0)]),
+        (second, [(2, 0, 0), (6, 0, 0)], [(3, 0, 0), (7, 0, 0)]),
     ]
+    sibling = jnp.where(core < 2, trains[1], jnp.zeros_like(trains[1]))
+    trains[1] = lax.optimization_barrier(sibling)
     for step in range(len(TURNS)):
         turn = [TURNS[(k + step) % len(TURNS)] for k in range(4)]
         came = [partner(p, turn[2 * k : 2 * k + 2]) for k, p in enumerate(held)]

time: 166 us -> 181 us (1.090)
  waiting for transfers between devices: 38.7 us -> 58.2 us
  starting transfers between devices: 98.5 us -> 90.7 us
  other arithmetic: 2.28 us -> 4.83 us
    ppermute x2, starting transfers between devices: 19.2 us -> 5.8 us  [on_device(): other = lax.ppermute(jnp.concatenate(away, 1), 'core', swap)]
    ppermute x2, starting transfers between devices: 28.1 us -> 39.8 us  [on_device(): arrived.append(lax.ppermute(cross, 'half', swap))]
    ppermute x2, waiting for transfers between devices: 8.61 us -> 18.7 us  [on_device(): arrived.append(lax.ppermute(cross, 'half', swap))]
    ppermute x11, waiting for transfers between devices: 27.8 us -> 35.2 us  [sent(): return lax.ppermute(rows, names, pairs)]
    ppermute x11, starting transfers between devices: 41 us -> 34.3 us  [sent(): return lax.ppermute(rows, names, pairs)]
    select_n x1 -> x3, other arithmetic: 0.05 us -> 2.57 us  [the longest x1 2.47 us: on_device(): sibling = jnp.where(core < 2, trains[1], jnp.zeros_like(trains[1]))]
  transfers between devices with their start and end apart: 17 -> 17, of which waited for: 11 -> 11; matrix products, arithmetic and copies ran while one was open for 11% -> 13% of each run, Pallas kernels for 0% -> 0%
where the time goes in v5:
time: 181 us; the launch traced here: 180 us
  starting transfers between devices  90.7 us (50%)
  waiting for transfers between devices  58.2 us (32%)
  matrix products  22.4 us (12%)
  other arithmetic  4.83 us (3%)
    ppermute x2, starting transfers between devices, on_device(): arrived.append(lax.ppermute(cross, 'half', swap))  39.8 us
    ppermute x11, waiting for transfers between devices, sent(): return lax.ppermute(rows, names, pairs)  35.2 us
    ppermute x11, starting transfers between devices, sent(): return lax.ppermute(rows, names, pairs)  34.3 us
    dot_general x8, matrix products, on_device(): lax.dot_general(r, t, (((1,), (1,)), ((), ())), preferred_element_type=jn...  21 us
    ppermute x2, waiting for transfers between devices, on_device(): arrived.append(lax.ppermute(cross, 'half', swap))  18.7 us
    ppermute x1, starting transfers between devices, on_device(): trains = [train_grads[0], lax.ppermute(train_grads[0], 'core', swap)]  8.91 us
    ppermute x2, starting transfers between devices, on_device(): other = lax.ppermute(jnp.concatenate(away, 1), 'core', swap)  5.8 us
  transfers between devices with their start and end apart: 17, of which 11 were waited for; matrix products, arithmetic and copies ran while one was open for 13% of the time, Pallas kernels for 0%

profile of v5, /device:TPU:1, one launch (start us, length us, event | category | flops | bytes accessed | tf_op | source)
XLA Modules:
  0.0 179.7 jit_solution(9206316990678459440)
XLA Ops:
  0.0 8.9 %collective-permute-start.2 = (bf16[512,4096]{1,0:T(8,128)(2,1)}, bf16[512,4096]{1,0:T(8,128)(2,1)}, u32[]{:S(2)}, u32[]{:S(2)}) collective-permute-start(bf16[512,4096]{1,0:T(8,128)(2,1)} %bitcast.54), channel_id=1, source_target_pairs={{0,1},{1,0},{2,3},{3,2},{4,5},{5,4},{6,7},{7,6},{8,9},{9,8},{10,11... | collective-permute-start | bytes 12582920 | tf_op jit(solution)/shard_map/ppermute | solution.py:87
  8.9 1.0 reshape.28
  10.0 0.2 convolution_bitcast_fusion
  10.2 1.1 convolution_convert_fusion
  11.3 0.2 convert_element_type.25
  11.5 1.9 %collective-permute-start = (bf16[8,4096]{1,0:T(8,128)(2,1)S(1)}, bf16[8,4096]{1,0:T(8,128)(2,1)S(1)}, u32[]{:S(2)}, u32[]{:S(2)}) collective-permute-start(bf16[8,4096]{1,0:T(8,128)(2,1)S(1)} %convert_element_type.25), channel_id=1, source_target_pairs={{0,1},{1,0},{2,3},{3,2},{4,5},{5,4},{6,7},{7,6},{8,9},{9,8},{10,11... | collective-permute-start | bytes 196616 | tf_op jit(solution)/shard_map/ppermute | solution.py:89
  13.4 0.2 convert_element_type.24
  13.6 2.1 %collective-permute-done = bf16[8,4096]{1,0:T(8,128)(2,1)S(1)} collective-permute-done((bf16[8,4096]{1,0:T(8,128)(2,1)S(1)}, bf16[8,4096]{1,0:T(8,128)(2,1)S(1)}, u32[]{:S(2)}, u32[]{:S(2)}) %collective-permute-start) | collective-permute-done | bytes 65568 | tf_op jit(solution)/shard_map/ppermute | solution.py:89
  15.8 1.9 %collective-permute-start.1 = (bf16[2,8,4096]{2,1,0:T(8,128)(2,1)S(1)}, bf16[2,8,4096]{2,1,0:T(8,128)(2,1)S(1)}, u32[]{:S(2)}, u32[]{:S(2)}) collective-permute-start(bf16[2,8,4096]{2,1,0:T(8,128)(2,1)S(1)} %pad_maximum_fusion.11), channel_id=1, source_target_pairs={{0,256},{1,65},{4,260},{5,69},{8,264},{9,73},{12,268},{13,77},{16,... | collective-permute-start | bytes 393224 | tf_op jit(solution)/shard_map/ppermute | solution.py:38
  17.7 3.8 %collective-permute-done.1 = bf16[2,8,4096]{2,1,0:T(8,128)(2,1)S(1)} collective-permute-done((bf16[2,8,4096]{2,1,0:T(8,128)(2,1)S(1)}, bf16[2,8,4096]{2,1,0:T(8,128)(2,1)S(1)}, u32[]{:S(2)}, u32[]{:S(2)}) %collective-permute-start.1) | collective-permute-done | bytes 131104 | tf_op jit(solution)/shard_map/ppermute | solution.py:38
  21.5 6.8 %collective-permute-start.3 = (bf16[2,16,4096]{2,1,0:T(8,128)(2,1)S(1)}, bf16[2,16,4096]{2,1,0:T(8,128)(2,1)S(1)}, u32[]{:S(2)}, u32[]{:S(2)}) collective-permute-start(bf16[2,16,4096]{2,1,0:T(8,128)(2,1)S(1)} %pad_maximum_fusion.10), channel_id=1, source_target_pairs={{0,128},{1,257},{4,132},{5,261},{8,136},{9,265},{12,140},{13,269},... | collective-permute-start | bytes 786440 | tf_op jit(solution)/shard_map/ppermute | solution.py:38
  28.3 11.0 %collective-permute-done.3 = bf16[2,16,4096]{2,1,0:T(8,128)(2,1)S(1)} collective-permute-done((bf16[2,16,4096]{2,1,0:T(8,128)(2,1)S(1)}, bf16[2,16,4096]{2,1,0:T(8,128)(2,1)S(1)}, u32[]{:S(2)}, u32[]{:S(2)}) %collective-permute-start.3) | collective-permute-done | bytes 262176 | tf_op jit(solution)/shard_map/ppermute | solution.py:38
  39.3 0.1 maximum_select_fusion
  39.4 1.9 %collective-permute-start.8 = (bf16[2,16,4096]{2,1,0:T(8,128)(2,1)S(1)}, bf16[2,16,4096]{2,1,0:T(8,128)(2,1)S(1)}, u32[]{:S(2)}, u32[]{:S(2)}) collective-permute-start(bf16[2,16,4096]{2,1,0:T(8,128)(2,1)S(1)} %maximum_select_fusion), channel_id=1, source_target_pairs={{1,129},{5,133},{9,137},{13,141},{17,145},{21,149},{25,153},{29,15... | collective-permute-start | bytes 786440 | tf_op jit(solution)/shard_map/ppermute | solution.py:38
  41.3 2.5 %collective-permute-start.4 = (bf16[2,16,4096]{2,1,0:T(8,128)(2,1)S(1)}, bf16[2,16,4096]{2,1,0:T(8,128)(2,1)S(1)}, u32[]{:S(2)}, u32[]{:S(2)}) collective-permute-start(bf16[2,16,4096]{2,1,0:T(8,128)(2,1)S(1)} %maximum_select_fusion), channel_id=1, source_target_pairs={{0,16},{1,5},{4,20},{5,1},{8,24},{9,13},{12,28},{13,9},{16,0},{17,... | collective-permute-start | bytes 786440 | tf_op jit(solution)/shard_map/ppermute | solution.py:38
  43.8 7.2 %collective-permute-done.8 = bf16[2,16,4096]{2,1,0:T(8,128)(2,1)S(1)} collective-permute-done((bf16[2,16,4096]{2,1,0:T(8,128)(2,1)S(1)}, bf16[2,16,4096]{2,1,0:T(8,128)(2,1)S(1)}, u32[]{:S(2)}, u32[]{:S(2)}) %collective-permute-start.8) | collective-permute-done | bytes 262176 | tf_op jit(solution)/shard_map/ppermute | solution.py:38
  51.1 2.5 %collective-permute-start.9 = (bf16[2,16,4096]{2,1,0:T(8,128)(2,1)S(1)}, bf16[2,16,4096]{2,1,0:T(8,128)(2,1)S(1)}, u32[]{:S(2)}, u32[]{:S(2)}) collective-permute-start(bf16[2,16,4096]{2,1,0:T(8,128)(2,1)S(1)} %broadcast_select_fusion.1), channel_id=1, source_target_pairs={{0,48},{1,13},{4,52},{5,9},{8,56},{9,5},{12,60},{13,1},{16,32},{17... | collective-permute-start | bytes 786440 | tf_op jit(solution)/shard_map/ppermute | solution.py:38
  53.7 4.4 %collective-permute-start.5 = (bf16[2,32,4096]{2,1,0:T(8,128)(2,1)S(1)}, bf16[2,32,4096]{2,1,0:T(8,128)(2,1)S(1)}, u32[]{:S(2)}, u32[]{:S(2)}) collective-permute-start(bf16[2,32,4096]{2,1,0:T(8,128)(2,1)S(1)} %pad_maximum_fusion.5), channel_id=1, source_target_pairs={{0,4},{1,49},{4,0},{5,53},{8,12},{9,57},{12,8},{13,61},{16,20},{17... | collective-permute-start | bytes 1572872 | tf_op jit(solution)/shard_map/ppermute | solution.py:38
  58.1 1.4 collective-permute-done.9
  59.5 1.9 %collective-permute-start.10 = (bf16[2,32,4096]{2,1,0:T(8,128)(2,1)S(1)}, bf16[2,32,4096]{2,1,0:T(8,128)(2,1)S(1)}, u32[]{:S(2)}, u32[]{:S(2)}) collective-permute-start(bf16[2,32,4096]{2,1,0:T(8,128)(2,1)S(1)} %pad_maximum_fusion.6), channel_id=1, source_target_pairs={{0,12},{1,17},{4,8},{5,21},{8,4},{9,25},{12,0},{13,29},{16,28},{17... | collective-permute-start | bytes 1572872 | tf_op jit(solution)/shard_map/ppermute | solution.py:38
  61.4 3.4 %collective-permute-done.5 = bf16[2,32,4096]{2,1,0:T(8,128)(2,1)S(1)} collective-permute-done((bf16[2,32,4096]{2,1,0:T(8,128)(2,1)S(1)}, bf16[2,32,4096]{2,1,0:T(8,128)(2,1)S(1)}, u32[]{:S(2)}, u32[]{:S(2)}) %collective-permute-start.5) | collective-permute-done | bytes 524320 | tf_op jit(solution)/shard_map/ppermute | solution.py:38
  64.8 0.1 pad_maximum_fusion.2
  64.9 4.3 %collective-permute-start.6 = (bf16[2,64,4096]{2,1,0:T(8,128)(2,1)S(1)}, bf16[2,64,4096]{2,1,0:T(8,128)(2,1)S(1)}, u32[]{:S(2)}, u32[]{:S(2)}) collective-permute-start(bf16[2,64,4096]{2,1,0:T(8,128)(2,1)S(1)} %pad_maximum_fusion.2), channel_id=1, source_target_pairs={{0,48},{1,13},{4,52},{5,9},{8,56},{9,5},{12,60},{13,1},{16,32},{17... | collective-permute-start | bytes 3145736 | tf_op jit(solution)/shard_map/ppermute | solution.py:38
  69.2 2.5 %broadcast_select_fusion = bf16[512,4096]{1,0:T(8,128)(2,1)S(1)} fusion(bf16[512,4096]{1,0:T(8,128)(2,1)} %collective-permute-done.2, pred[]{:T(512)S(6)} %lt.3), kind=kLoop, calls=%fused_computation | loop fusion | flops 2097152 | bytes 8388609 | tf_op jit(solution)/shard_map/jit(_where)/select_n | solution.py:101
  71.7 0.1 pad_maximum_fusion.3
  71.8 2.3 %collective-permute-start.11 = (bf16[2,64,4096]{2,1,0:T(8,128)(2,1)S(1)}, bf16[2,64,4096]{2,1,0:T(8,128)(2,1)S(1)}, u32[]{:S(2)}, u32[]{:S(2)}) collective-permute-start(bf16[2,64,4096]{2,1,0:T(8,128)(2,1)S(1)} %pad_maximum_fusion.3), channel_id=1, source_target_pairs={{0,16},{1,5},{4,20},{5,1},{8,24},{9,13},{12,28},{13,9},{16,0},{17,... | collective-permute-start | bytes 3145736 | tf_op jit(solution)/shard_map/ppermute | solution.py:38
  74.1 8.2 %collective-permute-done.6 = bf16[2,64,4096]{2,1,0:T(8,128)(2,1)S(1)} collective-permute-done((bf16[2,64,4096]{2,1,0:T(8,128)(2,1)S(1)}, bf16[2,64,4096]{2,1,0:T(8,128)(2,1)S(1)}, u32[]{:S(2)}, u32[]{:S(2)}) %collective-permute-start.6) | collective-permute-done | bytes 1048608 | tf_op jit(solution)/shard_map/ppermute | solution.py:38
  82.4 0.1 pad_maximum_fusion
  82.5 2.1 %collective-permute-start.13 = (bf16[2,128,4096]{2,1,0:T(8,128)(2,1)S(1)}, bf16[2,128,4096]{2,1,0:T(8,128)(2,1)}, u32[]{:S(2)}, u32[]{:S(2)}) collective-permute-start(bf16[2,128,4096]{2,1,0:T(8,128)(2,1)S(1)} %pad_maximum_fusion), channel_id=1, source_target_pairs={{0,12},{1,17},{4,8},{5,21},{8,4},{9,25},{12,0},{13,29},{16,28},{17... | collective-permute-start | bytes 6291464 | tf_op jit(solution)/shard_map/ppermute | solution.py:38
  84.6 1.5 fusion.2
  86.2 1.5 convolution_add_fusion.3
  87.8 0.1 collective-permute-done.11
  87.9 1.6 pad_maximum_fusion.1
  89.5 3.7 %collective-permute-start.14 = (bf16[2,128,4096]{2,1,0:T(8,128)(2,1)}, bf16[2,128,4096]{2,1,0:T(8,128)(2,1)}, u32[]{:S(2)}, u32[]{:S(2)}) collective-permute-start(bf16[2,128,4096]{2,1,0:T(8,128)(2,1)} %pad_maximum_fusion.1), channel_id=1, source_target_pairs={{0,4},{1,49},{4,0},{5,53},{8,12},{9,57},{12,8},{13,61},{16,20},{17... | collective-permute-start | bytes 6291464 | tf_op jit(solution)/shard_map/ppermute | solution.py:38
  93.1 3.4 %collective-permute-start.7 = (f32[128,256]{1,0:T(8,128)S(1)}, f32[128,256]{1,0:T(8,128)S(1)}, u32[]{:S(2)}, u32[]{:S(2)}) collective-permute-start(f32[128,256]{1,0:T(8,128)S(1)} %pad_maximum_fusion.12), channel_id=1, source_target_pairs={{0,1},{1,0},{2,3},{3,2},{4,5},{5,4},{6,7},{7,6},{8,9},{9,8},{10,11... | collective-permute-start | bytes 393224 | tf_op jit(solution)/shard_map/ppermute | solution.py:125
  96.6 0.9 collective-permute-done.7
  97.5 31.6 %collective-permute-start.12 = (bf16[256,128]{1,0:T(8,128)(2,1)S(1)}, bf16[256,128]{1,0:T(8,128)(2,1)S(1)}, u32[]{:S(2)}, u32[]{:S(2)}) collective-permute-start(bf16[256,128]{1,0:T(8,128)(2,1)S(1)} %select_convert_fusion.1), channel_id=1, source_target_pairs={{0,2},{2,0},{1,3},{3,1},{4,6},{6,4},{5,7},{7,5},{8,10},{10,8},{9,1... | collective-permute-start | bytes 196616 | tf_op jit(solution)/shard_map/ppermute | solution.py:129
  129.1 4.0 %fusion.1 = f32[128,512]{1,0:T(8,128)S(1)} fusion(bf16[512,4096]{1,0:T(8,128)(2,1)} %copy-done.1, bf16[2,128,4096]{2,1,0:T(8,128)(2,1)} %pad_maximum_fusion.1), kind=kOutput, calls=%fused_computation.13 | convolution fusion | flops 536870912 | bytes 5505024 | tf_op jit(solution)/shard_map/dot_general | solution.py:115
  133.2 2.8 %convolution_add_fusion.2 = f32[128,512]{1,0:T(8,128)S(1)} fusion(f32[128,512]{1,0:T(8,128)S(1)} %fusion.1, bf16[2,128,4096]{2,1,0:T(8,128)(2,1)} %pad_maximum_fusion.1, bf16[1,512,4096]{2,1,0:T(8,128)(2,1)S(1)} %copy-done.4), kind=kOutput, calls=%fused_computation.6 | convolution fusion | flops 536936448 | bytes 5767168 | tf_op jit(solution)/shard_map/dot_general | solution.py:115
  136.0 2.9 %fusion.4 = f32[128,512]{1,0:T(8,128)S(1)} fusion(bf16[2,128,4096]{2,1,0:T(8,128)(2,1)} %collective-permute-done.13, bf16[1,512,4096]{2,1,0:T(8,128)(2,1)S(1)} %copy-done.4), kind=kOutput, calls=%fused_computation.21 | convolution fusion | flops 536870912 | bytes 5505024 | tf_op jit(solution)/shard_map/dot_general | solution.py:115
  138.9 2.8 %convolution_add_fusion.1 = f32[128,512]{1,0:T(8,128)S(1)} fusion(f32[128,512]{1,0:T(8,128)S(1)} %fusion.4, bf16[512,4096]{1,0:T(8,128)(2,1)S(1)} %copy-done.2, bf16[2,128,4096]{2,1,0:T(8,128)(2,1)} %collective-permute-done.13), kind=kOutput, calls=%fused_computation.5 | convolution fusion | flops 536936448 | bytes 5767168 | tf_op jit(solution)/shard_map/dot_general | solution.py:115
  141.7 2.7 %fusion = f32[128,512]{1,0:T(8,128)S(1)} fusion(bf16[512,4096]{1,0:T(8,128)(2,1)S(1)} %copy-done.2, bf16[2,128,4096]{2,1,0:T(8,128)(2,1)} %collective-permute-done.14), kind=kOutput, calls=%fused_computation.10 | convolution fusion | flops 536870912 | bytes 5505024 | tf_op jit(solution)/shard_map/dot_general | solution.py:115
  144.4 2.8 %convolution_add_fusion = f32[128,512]{1,0:T(8,128)S(1)} fusion(f32[128,512]{1,0:T(8,128)S(1)} %fusion, bf16[2,128,4096]{2,1,0:T(8,128)(2,1)} %collective-permute-done.14, bf16[1,512,4096]{2,1,0:T(8,128)(2,1)S(1)} %copy-done.4), kind=kOutput, calls=%fused_computation.4 | convolution fusion | flops 536936448 | bytes 5767168 | tf_op jit(solution)/shard_map/dot_general | solution.py:115
  147.4 2.4 %collective-permute-start.15 = (f32[384,256]{1,0:T(8,128)S(1)}, f32[384,256]{1,0:T(8,128)S(1)}, u32[]{:S(2)}, u32[]{:S(2)}) collective-permute-start(f32[384,256]{1,0:T(8,128)S(1)} %pad_maximum_fusion.7), channel_id=1, source_target_pairs={{0,1},{1,0},{2,3},{3,2},{4,5},{5,4},{6,7},{7,6},{8,9},{9,8},{10,11... | collective-permute-start | bytes 1179656 | tf_op jit(solution)/shard_map/ppermute | solution.py:125
  149.9 1.3 collective-permute-done.15
  151.2 8.2 %collective-permute-start.16 = (bf16[768,128]{1,0:T(8,128)(2,1)S(1)}, bf16[768,128]{1,0:T(8,128)(2,1)S(1)}, u32[]{:S(2)}, u32[]{:S(2)}) collective-permute-start(bf16[768,128]{1,0:T(8,128)(2,1)S(1)} %select_convert_fusion), channel_id=1, source_target_pairs={{0,2},{2,0},{1,3},{3,1},{4,6},{6,4},{5,7},{7,5},{8,10},{10,8},{9,1... | collective-permute-start | bytes 589832 | tf_op jit(solution)/shard_map/ppermute | solution.py:129
  159.5 18.7 %collective-permute-done.16.refs_3_ = bf16[768,128]{1,0:T(8,128)(2,1)S(1)} collective-permute-done((bf16[768,128]{1,0:T(8,128)(2,1)S(1)}, bf16[768,128]{1,0:T(8,128)(2,1)S(1)}, u32[]{:S(2)}, u32[]{:S(2)}) %collective-permute-start.16) | collective-permute-done | bytes 196640 | tf_op jit(solution)/shard_map/ppermute | solution.py:129
  178.1 1.6 shard_map.64
  (40 shorter events, 0.6 us)
Async XLA Ops:
  0.0 10.0 %copy-start = (f32[1,64,64]{2,1,0:T(8,128)S(1)}, f32[1,64,64]{2,1,0:T(8,128)}, u32[]{:S(2)}) copy-start(f32[1,64,64]{2,1,0:T(8,128)} %param.8) | copy-start | bytes 49156
  0.0 21.5 %collective-permute-start.2 = (bf16[512,4096]{1,0:T(8,128)(2,1)}, bf16[512,4096]{1,0:T(8,128)(2,1)}, u32[]{:S(2)}, u32[]{:S(2)}) collective-permute-start(bf16[512,4096]{1,0:T(8,128)(2,1)} %bitcast.54), channel_id=1, source_target_pairs={{0,1},{1,0},{2,3},{3,2},{4,5},{5,4},{6,7},{7,6},{8,9},{9,8},{10,11... | collective-permute-start | bytes 12582920 | tf_op jit(solution)/shard_map/ppermute | solution.py:87
  11.5 4.3 %collective-permute-start = (bf16[8,4096]{1,0:T(8,128)(2,1)S(1)}, bf16[8,4096]{1,0:T(8,128)(2,1)S(1)}, u32[]{:S(2)}, u32[]{:S(2)}) collective-permute-start(bf16[8,4096]{1,0:T(8,128)(2,1)S(1)} %convert_element_type.25), channel_id=1, source_target_pairs={{0,1},{1,0},{2,3},{3,2},{4,5},{5,4},{6,7},{7,6},{8,9},{9,8},{10,11... | collective-permute-start | bytes 196616 | tf_op jit(solution)/shard_map/ppermute | solution.py:89
  15.8 5.7 %collective-permute-start.1 = (bf16[2,8,4096]{2,1,0:T(8,128)(2,1)S(1)}, bf16[2,8,4096]{2,1,0:T(8,128)(2,1)S(1)}, u32[]{:S(2)}, u32[]{:S(2)}) collective-permute-start(bf16[2,8,4096]{2,1,0:T(8,128)(2,1)S(1)} %pad_maximum_fusion.11), channel_id=1, source_target_pairs={{0,256},{1,65},{4,260},{5,69},{8,264},{9,73},{12,268},{13,77},{16,... | collective-permute-start | bytes 393224 | tf_op jit(solution)/shard_map/ppermute | solution.py:38
  21.5 17.8 %collective-permute-start.3 = (bf16[2,16,4096]{2,1,0:T(8,128)(2,1)S(1)}, bf16[2,16,4096]{2,1,0:T(8,128)(2,1)S(1)}, u32[]{:S(2)}, u32[]{:S(2)}) collective-permute-start(bf16[2,16,4096]{2,1,0:T(8,128)(2,1)S(1)} %pad_maximum_fusion.10), channel_id=1, source_target_pairs={{0,128},{1,257},{4,132},{5,261},{8,136},{9,265},{12,140},{13,269},... | collective-permute-start | bytes 786440 | tf_op jit(solution)/shard_map/ppermute | solution.py:38
  39.4 11.7 %collective-permute-start.8 = (bf16[2,16,4096]{2,1,0:T(8,128)(2,1)S(1)}, bf16[2,16,4096]{2,1,0:T(8,128)(2,1)S(1)}, u32[]{:S(2)}, u32[]{:S(2)}) collective-permute-start(bf16[2,16,4096]{2,1,0:T(8,128)(2,1)S(1)} %maximum_select_fusion), channel_id=1, source_target_pairs={{1,129},{5,133},{9,137},{13,141},{17,145},{21,149},{25,153},{29,15... | collective-permute-start | bytes 786440 | tf_op jit(solution)/shard_map/ppermute | solution.py:38
  41.3 12.3 %collective-permute-start.4 = (bf16[2,16,4096]{2,1,0:T(8,128)(2,1)S(1)}, bf16[2,16,4096]{2,1,0:T(8,128)(2,1)S(1)}, u32[]{:S(2)}, u32[]{:S(2)}) collective-permute-start(bf16[2,16,4096]{2,1,0:T(8,128)(2,1)S(1)} %maximum_select_fusion), channel_id=1, source_target_pairs={{0,16},{1,5},{4,20},{5,1},{8,24},{9,13},{12,28},{13,9},{16,0},{17,... | collective-permute-start | bytes 786440 | tf_op jit(solution)/shard_map/ppermute | solution.py:38
  51.1 8.3 %collective-permute-start.9 = (bf16[2,16,4096]{2,1,0:T(8,128)(2,1)S(1)}, bf16[2,16,4096]{2,1,0:T(8,128)(2,1)S(1)}, u32[]{:S(2)}, u32[]{:S(2)}) collective-permute-start(bf16[2,16,4096]{2,1,0:T(8,128)(2,1)S(1)} %broadcast_select_fusion.1), channel_id=1, source_target_pairs={{0,48},{1,13},{4,52},{5,9},{8,56},{9,5},{12,60},{13,1},{16,32},{17... | collective-permute-start | bytes 786440 | tf_op jit(solution)/shard_map/ppermute | solution.py:38
  53.7 11.1 %collective-permute-start.5 = (bf16[2,32,4096]{2,1,0:T(8,128)(2,1)S(1)}, bf16[2,32,4096]{2,1,0:T(8,128)(2,1)S(1)}, u32[]{:S(2)}, u32[]{:S(2)}) collective-permute-start(bf16[2,32,4096]{2,1,0:T(8,128)(2,1)S(1)} %pad_maximum_fusion.5), channel_id=1, source_target_pairs={{0,4},{1,49},{4,0},{5,53},{8,12},{9,57},{12,8},{13,61},{16,20},{17... | collective-permute-start | bytes 1572872 | tf_op jit(solution)/shard_map/ppermute | solution.py:38
  59.5 12.2 %collective-permute-start.10 = (bf16[2,32,4096]{2,1,0:T(8,128)(2,1)S(1)}, bf16[2,32,4096]{2,1,0:T(8,128)(2,1)S(1)}, u32[]{:S(2)}, u32[]{:S(2)}) collective-permute-start(bf16[2,32,4096]{2,1,0:T(8,128)(2,1)S(1)} %pad_maximum_fusion.6), channel_id=1, source_target_pairs={{0,12},{1,17},{4,8},{5,21},{8,4},{9,25},{12,0},{13,29},{16,28},{17... | collective-permute-start | bytes 1572872 | tf_op jit(solution)/shard_map/ppermute | solution.py:38
  64.9 17.4 %collective-permute-start.6 = (bf16[2,64,4096]{2,1,0:T(8,128)(2,1)S(1)}, bf16[2,64,4096]{2,1,0:T(8,128)(2,1)S(1)}, u32[]{:S(2)}, u32[]{:S(2)}) collective-permute-start(bf16[2,64,4096]{2,1,0:T(8,128)(2,1)S(1)} %pad_maximum_fusion.2), channel_id=1, source_target_pairs={{0,48},{1,13},{4,52},{5,9},{8,56},{9,5},{12,60},{13,1},{16,32},{17... | collective-permute-start | bytes 3145736 | tf_op jit(solution)/shard_map/ppermute | solution.py:38
  71.7 14.5 %copy-start.1 = (bf16[512,4096]{1,0:T(8,128)(2,1)}, bf16[512,4096]{1,0:T(8,128)(2,1)S(1)}, u32[]{:S(2)}) copy-start(bf16[512,4096]{1,0:T(8,128)(2,1)S(1)} %broadcast_select_fusion) | copy-start | bytes 12582916
  71.8 14.4 %copy-start.3 = (bf16[1,512,4096]{2,1,0:T(8,128)(2,1)S(1)}, bf16[1,512,4096]{2,1,0:T(8,128)(2,1)}, u32[]{:S(2)}) copy-start(bf16[1,512,4096]{2,1,0:T(8,128)(2,1)} %param.6) | copy-start | bytes 12582916
  71.8 16.1 %collective-permute-start.11 = (bf16[2,64,4096]{2,1,0:T(8,128)(2,1)S(1)}, bf16[2,64,4096]{2,1,0:T(8,128)(2,1)S(1)}, u32[]{:S(2)}, u32[]{:S(2)}) collective-permute-start(bf16[2,64,4096]{2,1,0:T(8,128)(2,1)S(1)} %pad_maximum_fusion.3), channel_id=1, source_target_pairs={{0,16},{1,5},{4,20},{5,1},{8,24},{9,13},{12,28},{13,9},{16,0},{17,... | collective-permute-start | bytes 3145736 | tf_op jit(solution)/shard_map/ppermute | solution.py:38
  82.5 53.5 %collective-permute-start.13 = (bf16[2,128,4096]{2,1,0:T(8,128)(2,1)S(1)}, bf16[2,128,4096]{2,1,0:T(8,128)(2,1)}, u32[]{:S(2)}, u32[]{:S(2)}) collective-permute-start(bf16[2,128,4096]{2,1,0:T(8,128)(2,1)S(1)} %pad_maximum_fusion), channel_id=1, source_target_pairs={{0,12},{1,17},{4,8},{5,21},{8,4},{9,25},{12,0},{13,29},{16,28},{17... | collective-permute-start | bytes 6291464 | tf_op jit(solution)/shard_map/ppermute | solution.py:38
  89.5 52.2 %collective-permute-start.14 = (bf16[2,128,4096]{2,1,0:T(8,128)(2,1)}, bf16[2,128,4096]{2,1,0:T(8,128)(2,1)}, u32[]{:S(2)}, u32[]{:S(2)}) collective-permute-start(bf16[2,128,4096]{2,1,0:T(8,128)(2,1)} %pad_maximum_fusion.1), channel_id=1, source_target_pairs={{0,4},{1,49},{4,0},{5,53},{8,12},{9,57},{12,8},{13,61},{16,20},{17... | collective-permute-start | bytes 6291464 | tf_op jit(solution)/shard_map/ppermute | solution.py:38
  93.1 4.4 %collective-permute-start.7 = (f32[128,256]{1,0:T(8,128)S(1)}, f32[128,256]{1,0:T(8,128)S(1)}, u32[]{:S(2)}, u32[]{:S(2)}) collective-permute-start(f32[128,256]{1,0:T(8,128)S(1)} %pad_maximum_fusion.12), channel_id=1, source_target_pairs={{0,1},{1,0},{2,3},{3,2},{4,5},{5,4},{6,7},{7,6},{8,9},{9,8},{10,11... | collective-permute-start | bytes 393224 | tf_op jit(solution)/shard_map/ppermute | solution.py:125
  96.5 36.6 %copy-start.4 = (bf16[1,512,4096]{2,1,0:T(8,128)(2,1)S(1)}, bf16[1,512,4096]{2,1,0:T(8,128)(2,1)}, u32[]{:S(2)}) copy-start(bf16[1,512,4096]{2,1,0:T(8,128)(2,1)} %param.6) | copy-start | bytes 12582916
  97.5 38.4 %collective-permute-start.12 = (bf16[256,128]{1,0:T(8,128)(2,1)S(1)}, bf16[256,128]{1,0:T(8,128)(2,1)S(1)}, u32[]{:S(2)}, u32[]{:S(2)}) collective-permute-start(bf16[256,128]{1,0:T(8,128)(2,1)S(1)} %select_convert_fusion.1), channel_id=1, source_target_pairs={{0,2},{2,0},{1,3},{3,1},{4,6},{6,4},{5,7},{7,5},{8,10},{10,8},{9,1... | collective-permute-start | bytes 196616 | tf_op jit(solution)/shard_map/ppermute | solution.py:129
  135.9 2.9 %copy-start.2 = (bf16[512,4096]{1,0:T(8,128)(2,1)S(1)}, bf16[512,4096]{1,0:T(8,128)(2,1)}, u32[]{:S(2)}) copy-start(bf16[512,4096]{1,0:T(8,128)(2,1)} %copy-done.1) | copy-start | bytes 12582916
  144.4 5.4 %copy-start.5 = (s32[128,3]{0,1:T(4,128)S(1)}, s32[128,3]{0,1:T(4,128)}, u32[]{:S(2)}) copy-start(s32[128,3]{0,1:T(4,128)} %constant.34.clone) | copy-start | bytes 4612
  144.4 5.4 %copy-start.6 = (s32[128,3]{0,1:T(4,128)S(1)}, s32[128,3]{0,1:T(4,128)}, u32[]{:S(2)}) copy-start(s32[128,3]{0,1:T(4,128)} %constant.33.clone) | copy-start | bytes 4612
  147.4 3.8 %collective-permute-start.15 = (f32[384,256]{1,0:T(8,128)S(1)}, f32[384,256]{1,0:T(8,128)S(1)}, u32[]{:S(2)}, u32[]{:S(2)}) collective-permute-start(f32[384,256]{1,0:T(8,128)S(1)} %pad_maximum_fusion.7), channel_id=1, source_target_pairs={{0,1},{1,0},{2,3},{3,2},{4,5},{5,4},{6,7},{7,6},{8,9},{9,8},{10,11... | collective-permute-start | bytes 1179656 | tf_op jit(solution)/shard_map/ppermute | solution.py:125
  151.2 26.9 %collective-permute-start.16 = (bf16[768,128]{1,0:T(8,128)(2,1)S(1)}, bf16[768,128]{1,0:T(8,128)(2,1)S(1)}, u32[]{:S(2)}, u32[]{:S(2)}) collective-permute-start(bf16[768,128]{1,0:T(8,128)(2,1)S(1)} %select_convert_fusion), channel_id=1, source_target_pairs={{0,2},{2,0},{1,3},{3,1},{4,6},{6,4},{5,7},{7,5},{8,10},{10,8},{9,1... | collective-permute-start | bytes 589832 | tf_op jit(solution)/shard_map/ppermute | solution.py:129

commit v6 on v3

--- a/solution.py
+++ b/solution.py
@@ -80,8 +80,10 @@
         if step < len(TURNS) - 1:
             held = [joined(pieces) for pieces in zip(held, came)]
 
+    ready = lax.optimization_barrier(tuple(rows for rows, _ in held))
+    held = [(rows, piece[1]) for rows, piece in zip(ready, held)]
     kept, arrived, owners = [], [], []
-    for pieces in (held[:2], held[2:] + came[:1], came[1:]):
+    for pieces in (held[:2], held[2:] + came):
         partial_scores = jnp.concatenate(
             [
                 lax.dot_general(rows, resident, (((1,), (1,)), ((), ())), preferred_element_type=jnp.float32)
@@ -92,7 +94,10 @@
         shares = [partial_scores[:, k * width : (k + 1) * width] for k in range(4)]
         away = [jnp.where(core == 0, shares[2 * k + 1], shares[2 * k]) for k in range(2)]
         here = [jnp.where(core == 0, shares[2 * k], shares[2 * k + 1]) for k in range(2)]
-        other = lax.ppermute(jnp.concatenate(away, 1), "core", [(0, 1), (1, 0)])
+        away = jnp.concatenate(away, 1)
+        if arrived:
+            away, arrived[0] = lax.optimization_barrier((away, arrived[0]))
+        other = lax.ppermute(away, "core", [(0, 1), (1, 0)])
         both = [here[k] + other[:, k * width : (k + 1) * width] for k in range(2)]
         kept.append(jnp.where(half == 0, both[0], both[1]))
         cross = jnp.where(half == 0, both[1], both[0]).astype(jnp.bfloat16)

time: 162 us -> 155 us (0.957)
  the two profiles are of different devices: /device:TPU:1 before, /device:TPU:41 now
where the time goes in v6:
time: 155 us
  starting transfers between devices  111 us (72%)
  waiting for transfers between devices  25.3 us (16%)
  matrix products  13.6 us (9%)
  Pallas kernels  1.59 us (1%)
    ppermute x20, starting transfers between devices, partner(): lax.ppermute(rows, axis, [(i, i ^ bits) for i in range(SIZES[AXES.index(a...  73.1 us
    ppermute x2, starting transfers between devices, on_device(): arrived.append(lax.ppermute(cross, 'half', [(0, 1), (1, 0)]))  26 us
    ppermute x2, waiting for transfers between devices, on_device(): arrived.append(lax.ppermute(cross, 'half', [(0, 1), (1, 0)]))  17.9 us
    dot_general x8, matrix products, on_device(): lax.dot_general(rows, resident, (((1,), (1,)), ((), ())), preferred_eleme...  12.2 us
    ppermute x2, starting transfers between devices, on_device(): other = lax.ppermute(away, 'core', [(0, 1), (1, 0)])  12 us
    ppermute x20, waiting for transfers between devices, partner(): lax.ppermute(rows, axis, [(i, i ^ bits) for i in range(SIZES[AXES.index(a...  5.49 us
  transfers between devices with their start and end apart: 24, of which 6 were waited for; matrix products, arithmetic and copies ran while one was open for 8% of the time, Pallas kernels for 0%

profile of v6, /device:TPU:41, one launch (start us, length us, event | category | flops | bytes accessed | tf_op | source)
XLA Modules:
  0.0 154.6 jit_solution(18178136943871262469)
XLA Ops:
  0.0 1.0 reshape.6
  1.1 0.2 convolution_bitcast_fusion
  1.3 1.1 convolution_convert_fusion
  2.4 0.2 convert_element_type.14
  2.6 8.8 %collective-permute-start = (bf16[8,4096]{1,0:T(8,128)(2,1)S(1)}, bf16[8,4096]{1,0:T(8,128)(2,1)S(1)}, u32[]{:S(2)}, u32[]{:S(2)}) collective-permute-start(bf16[8,4096]{1,0:T(8,128)(2,1)S(1)} %convert_element_type.14), channel_id=1, source_target_pairs={{0,256},{64,320},{128,384},{192,448},{256,0},{320,64},{384,128},{4... | collective-permute-start | bytes 196616 | tf_op jit(solution)/shard_map/ppermute | solution.py:30
  11.4 2.2 %collective-permute-done = bf16[8,4096]{1,0:T(8,128)(2,1)S(1)} collective-permute-done((bf16[8,4096]{1,0:T(8,128)(2,1)S(1)}, bf16[8,4096]{1,0:T(8,128)(2,1)S(1)}, u32[]{:S(2)}, u32[]{:S(2)}) %collective-permute-start) | collective-permute-done | bytes 65568 | tf_op jit(solution)/shard_map/ppermute | solution.py:30
  13.7 7.1 %collective-permute-start.4 = (bf16[16,4096]{1,0:T(8,128)(2,1)S(1)}, bf16[16,4096]{1,0:T(8,128)(2,1)S(1)}, u32[]{:S(2)}, u32[]{:S(2)}) collective-permute-start(bf16[16,4096]{1,0:T(8,128)(2,1)S(1)} %pad_maximum_fusion.15), channel_id=1, source_target_pairs={{0,128},{64,192},{128,0},{192,64},{256,384},{320,448},{384,256},{4... | collective-permute-start | bytes 393224 | tf_op jit(solution)/shard_map/ppermute | solution.py:30
  20.9 3.1 %collective-permute-start.1 = (bf16[16,4096]{1,0:T(8,128)(2,1)S(1)}, bf16[16,4096]{1,0:T(8,128)(2,1)S(1)}, u32[]{:S(2)}, u32[]{:S(2)}) collective-permute-start(bf16[16,4096]{1,0:T(8,128)(2,1)S(1)} %pad_maximum_fusion.15), channel_id=1, source_target_pairs={{0,16},{16,0},{32,48},{48,32},{1,17},{17,1},{33,49},{49,33},{2,18}... | collective-permute-start | bytes 393224 | tf_op jit(solution)/shard_map/ppermute | solution.py:30
  24.0 1.9 %collective-permute-start.8 = (bf16[16,4096]{1,0:T(8,128)(2,1)S(1)}, bf16[16,4096]{1,0:T(8,128)(2,1)S(1)}, u32[]{:S(2)}, u32[]{:S(2)}) collective-permute-start(bf16[16,4096]{1,0:T(8,128)(2,1)S(1)} %pad_maximum_fusion.15), channel_id=1, source_target_pairs={{0,64},{64,0},{128,192},{192,128},{256,320},{320,256},{384,448},{4... | collective-permute-start | bytes 393224 | tf_op jit(solution)/shard_map/ppermute | solution.py:30
  25.9 2.1 %collective-permute-start.5 = (bf16[16,4096]{1,0:T(8,128)(2,1)S(1)}, bf16[16,4096]{1,0:T(8,128)(2,1)S(1)}, u32[]{:S(2)}, u32[]{:S(2)}) collective-permute-start(bf16[16,4096]{1,0:T(8,128)(2,1)S(1)} %collective-permute-done.4), channel_id=1, source_target_pairs={{0,4},{4,0},{8,12},{12,8},{1,5},{5,1},{9,13},{13,9},{2,6},{6,2},{1... | collective-permute-start | bytes 393224 | tf_op jit(solution)/shard_map/ppermute | solution.py:30
  28.1 3.2 %collective-permute-start.2 = (bf16[32,4096]{1,0:T(8,128)(2,1)S(1)}, bf16[32,4096]{1,0:T(8,128)(2,1)S(1)}, u32[]{:S(2)}, u32[]{:S(2)}) collective-permute-start(bf16[32,4096]{1,0:T(8,128)(2,1)S(1)} %pad_maximum_fusion.9), channel_id=1, source_target_pairs={{0,4},{4,0},{8,12},{12,8},{1,5},{5,1},{9,13},{13,9},{2,6},{6,2},{1... | collective-permute-start | bytes 786440 | tf_op jit(solution)/shard_map/ppermute | solution.py:30
  31.3 3.4 %collective-permute-start.12 = (bf16[16,4096]{1,0:T(8,128)(2,1)S(1)}, bf16[16,4096]{1,0:T(8,128)(2,1)S(1)}, u32[]{:S(2)}, u32[]{:S(2)}) collective-permute-start(bf16[16,4096]{1,0:T(8,128)(2,1)S(1)} %collective-permute-done.4), channel_id=1, source_target_pairs={{0,64},{64,0},{128,192},{192,128},{256,320},{320,256},{384,448},{4... | collective-permute-start | bytes 393224 | tf_op jit(solution)/shard_map/ppermute | solution.py:30
  34.6 3.7 %collective-permute-start.9 = (bf16[16,4096]{1,0:T(8,128)(2,1)S(1)}, bf16[16,4096]{1,0:T(8,128)(2,1)S(1)}, u32[]{:S(2)}, u32[]{:S(2)}) collective-permute-start(bf16[16,4096]{1,0:T(8,128)(2,1)S(1)} %collective-permute-done.8), channel_id=1, source_target_pairs={{0,48},{16,32},{32,16},{48,0},{1,49},{17,33},{33,17},{49,1},{2,50}... | collective-permute-start | bytes 393224 | tf_op jit(solution)/shard_map/ppermute | solution.py:30
  38.4 2.8 %collective-permute-start.6 = (bf16[32,4096]{1,0:T(8,128)(2,1)S(1)}, bf16[32,4096]{1,0:T(8,128)(2,1)S(1)}, u32[]{:S(2)}, u32[]{:S(2)}) collective-permute-start(bf16[32,4096]{1,0:T(8,128)(2,1)S(1)} %pad_maximum_fusion.10), channel_id=1, source_target_pairs={{0,48},{16,32},{32,16},{48,0},{1,49},{17,33},{33,17},{49,1},{2,50}... | collective-permute-start | bytes 786440 | tf_op jit(solution)/shard_map/ppermute | solution.py:30
  41.2 0.4 collective-permute-done.9
  41.6 3.2 %collective-permute-start.10 = (bf16[32,4096]{1,0:T(8,128)(2,1)S(1)}, bf16[32,4096]{1,0:T(8,128)(2,1)S(1)}, u32[]{:S(2)}, u32[]{:S(2)}) collective-permute-start(bf16[32,4096]{1,0:T(8,128)(2,1)S(1)} %pad_maximum_fusion.11), channel_id=1, source_target_pairs={{0,12},{4,8},{8,4},{12,0},{1,13},{5,9},{9,5},{13,1},{2,14},{6,10},... | collective-permute-start | bytes 786440 | tf_op jit(solution)/shard_map/ppermute | solution.py:30
  44.8 2.1 %collective-permute-start.13 = (bf16[16,4096]{1,0:T(8,128)(2,1)S(1)}, bf16[16,4096]{1,0:T(8,128)(2,1)S(1)}, u32[]{:S(2)}, u32[]{:S(2)}) collective-permute-start(bf16[16,4096]{1,0:T(8,128)(2,1)S(1)} %collective-permute-done.12), channel_id=1, source_target_pairs={{0,12},{4,8},{8,4},{12,0},{1,13},{5,9},{9,5},{13,1},{2,14},{6,10},... | collective-permute-start | bytes 393224 | tf_op jit(solution)/shard_map/ppermute | solution.py:30
  47.0 3.7 %collective-permute-start.3 = (bf16[64,4096]{1,0:T(8,128)(2,1)S(1)}, bf16[64,4096]{1,0:T(8,128)(2,1)S(1)}, u32[]{:S(2)}, u32[]{:S(2)}) collective-permute-start(bf16[64,4096]{1,0:T(8,128)(2,1)S(1)} %pad_maximum_fusion.5), channel_id=1, source_target_pairs={{0,48},{16,32},{32,16},{48,0},{1,49},{17,33},{33,17},{49,1},{2,50}... | collective-permute-start | bytes 1572872 | tf_op jit(solution)/shard_map/ppermute | solution.py:30
  50.7 0.4 collective-permute-done.13
  51.1 1.9 %collective-permute-start.14 = (bf16[32,4096]{1,0:T(8,128)(2,1)S(1)}, bf16[32,4096]{1,0:T(8,128)(2,1)S(1)}, u32[]{:S(2)}, u32[]{:S(2)}) collective-permute-start(bf16[32,4096]{1,0:T(8,128)(2,1)S(1)} %pad_maximum_fusion.12), channel_id=1, source_target_pairs={{0,16},{16,0},{32,48},{48,32},{1,17},{17,1},{33,49},{49,33},{2,18}... | collective-permute-start | bytes 786440 | tf_op jit(solution)/shard_map/ppermute | solution.py:30
  53.1 2.8 %collective-permute-start.7 = (bf16[64,4096]{1,0:T(8,128)(2,1)S(1)}, bf16[64,4096]{1,0:T(8,128)(2,1)S(1)}, u32[]{:S(2)}, u32[]{:S(2)}) collective-permute-start(bf16[64,4096]{1,0:T(8,128)(2,1)S(1)} %pad_maximum_fusion.6), channel_id=1, source_target_pairs={{0,12},{4,8},{8,4},{12,0},{1,13},{5,9},{9,5},{13,1},{2,14},{6,10},... | collective-permute-start | bytes 1572872 | tf_op jit(solution)/shard_map/ppermute | solution.py:30
  56.0 3.4 %collective-permute-start.11 = (bf16[64,4096]{1,0:T(8,128)(2,1)S(1)}, bf16[64,4096]{1,0:T(8,128)(2,1)S(1)}, u32[]{:S(2)}, u32[]{:S(2)}) collective-permute-start(bf16[64,4096]{1,0:T(8,128)(2,1)S(1)} %pad_maximum_fusion.7), channel_id=1, source_target_pairs={{0,16},{16,0},{32,48},{48,32},{1,17},{17,1},{33,49},{49,33},{2,18}... | collective-permute-start | bytes 1572872 | tf_op jit(solution)/shard_map/ppermute | solution.py:30
  59.4 5.0 %collective-permute-start.15 = (bf16[64,4096]{1,0:T(8,128)(2,1)S(1)}, bf16[64,4096]{1,0:T(8,128)(2,1)S(1)}, u32[]{:S(2)}, u32[]{:S(2)}) collective-permute-start(bf16[64,4096]{1,0:T(8,128)(2,1)S(1)} %pad_maximum_fusion.8), channel_id=1, source_target_pairs={{0,4},{4,0},{8,12},{12,8},{1,5},{5,1},{9,13},{13,9},{2,6},{6,2},{1... | collective-permute-start | bytes 1572872 | tf_op jit(solution)/shard_map/ppermute | solution.py:30
  64.5 3.9 %collective-permute-start.17 = (bf16[128,4096]{1,0:T(8,128)(2,1)S(1)}, bf16[128,4096]{1,0:T(8,128)(2,1)S(1)}, u32[]{:S(2)}, u32[]{:S(2)}) collective-permute-start(bf16[128,4096]{1,0:T(8,128)(2,1)S(1)} %pad_maximum_fusion), channel_id=1, source_target_pairs={{0,12},{4,8},{8,4},{12,0},{1,13},{5,9},{9,5},{13,1},{2,14},{6,10},... | collective-permute-start | bytes 3145736 | tf_op jit(solution)/shard_map/ppermute | solution.py:30
  68.5 0.1 pad_maximum_fusion.1
  68.6 2.4 %collective-permute-done.11 = bf16[64,4096]{1,0:T(8,128)(2,1)S(1)} collective-permute-done((bf16[64,4096]{1,0:T(8,128)(2,1)S(1)}, bf16[64,4096]{1,0:T(8,128)(2,1)S(1)}, u32[]{:S(2)}, u32[]{:S(2)}) %collective-permute-start.11) | collective-permute-done | bytes 524320 | tf_op jit(solution)/shard_map/ppermute | solution.py:30
  71.0 0.1 pad_maximum_fusion.2
  71.1 1.9 %collective-permute-start.18 = (bf16[128,4096]{1,0:T(8,128)(2,1)S(1)}, bf16[128,4096]{1,0:T(8,128)(2,1)S(1)}, u32[]{:S(2)}, u32[]{:S(2)}) collective-permute-start(bf16[128,4096]{1,0:T(8,128)(2,1)S(1)} %pad_maximum_fusion.1), channel_id=1, source_target_pairs={{0,16},{16,0},{32,48},{48,32},{1,17},{17,1},{33,49},{49,33},{2,18}... | collective-permute-start | bytes 3145736 | tf_op jit(solution)/shard_map/ppermute | solution.py:30
  73.0 5.2 %collective-permute-start.19 = (bf16[128,4096]{1,0:T(8,128)(2,1)S(1)}, bf16[128,4096]{1,0:T(8,128)(2,1)S(1)}, u32[]{:S(2)}, u32[]{:S(2)}) collective-permute-start(bf16[128,4096]{1,0:T(8,128)(2,1)S(1)} %pad_maximum_fusion.2), channel_id=1, source_target_pairs={{0,4},{4,0},{8,12},{12,8},{1,5},{5,1},{9,13},{13,9},{2,6},{6,2},{1... | collective-permute-start | bytes 3145736 | tf_op jit(solution)/shard_map/ppermute | solution.py:30
  78.2 0.1 pad_maximum_fusion.3
  78.3 3.8 %collective-permute-start.20 = (bf16[128,4096]{1,0:T(8,128)(2,1)S(1)}, bf16[128,4096]{1,0:T(8,128)(2,1)S(1)}, u32[]{:S(2)}, u32[]{:S(2)}) collective-permute-start(bf16[128,4096]{1,0:T(8,128)(2,1)S(1)} %pad_maximum_fusion.3), channel_id=1, source_target_pairs={{0,48},{16,32},{32,16},{48,0},{1,49},{17,33},{33,17},{49,1},{2,50}... | collective-permute-start | bytes 3145736 | tf_op jit(solution)/shard_map/ppermute | solution.py:30
  82.1 1.5 fusion.12
  83.7 1.5 fusion.14
  85.3 9.8 %collective-permute-start.16 = (f32[256,256]{1,0:T(8,128)S(1)}, f32[256,256]{1,0:T(8,128)S(1)}, u32[]{:S(2)}, u32[]{:S(2)}) collective-permute-start(f32[256,256]{1,0:T(8,128)S(1)} %pad_maximum_fusion.13), channel_id=1, source_target_pairs={{0,1},{1,0},{2,3},{3,2},{4,5},{5,4},{6,7},{7,6},{8,9},{9,8},{10,11... | collective-permute-start | bytes 786440 | tf_op jit(solution)/shard_map/ppermute | solution.py:100
  95.1 1.5 fusion.16
  96.7 1.5 fusion.19
  98.3 14.1 %collective-permute-start.21 = (bf16[256,128]{1,0:T(8,128)(2,1)S(1)}, bf16[256,128]{1,0:T(8,128)(2,1)S(1)}, u32[]{:S(2)}, u32[]{:S(2)}) collective-permute-start(bf16[256,128]{1,0:T(8,128)(2,1)S(1)} %get-tuple-element.20), channel_id=1, source_target_pairs={{0,2},{2,0},{1,3},{3,1},{4,6},{6,4},{5,7},{7,5},{8,10},{10,8},{9,1... | collective-permute-start | bytes 196616 | tf_op jit(solution)/shard_map/ppermute | solution.py:104
  112.4 1.5 fusion.22
  114.0 1.5 fusion.25
  115.5 1.5 fusion.28
  117.1 1.5 fusion.31
  118.6 0.1 slice_select_fusion.1
  118.8 2.2 %collective-permute-start.22 = (f32[768,256]{1,0:T(8,128)S(1)}, f32[768,256]{1,0:T(8,128)S(1)}, u32[]{:S(2)}, u32[]{:S(2)}) collective-permute-start(f32[768,256]{1,0:T(8,128)S(1)} %pad_maximum_fusion.4), channel_id=1, source_target_pairs={{0,1},{1,0},{2,3},{3,2},{4,5},{5,4},{6,7},{7,6},{8,9},{9,8},{10,11... | collective-permute-start | bytes 2359304 | tf_op jit(solution)/shard_map/ppermute | solution.py:100
  121.1 1.9 %collective-permute-done.22 = f32[768,256]{1,0:T(8,128)S(1)} collective-permute-done((f32[768,256]{1,0:T(8,128)S(1)}, f32[768,256]{1,0:T(8,128)S(1)}, u32[]{:S(2)}, u32[]{:S(2)}) %collective-permute-start.22) | collective-permute-done | bytes 786464 | tf_op jit(solution)/shard_map/ppermute | solution.py:100
  123.0 0.1 select_convert_fusion
  123.1 11.9 %collective-permute-start.23 = (bf16[768,128]{1,0:T(8,128)(2,1)S(1)}, bf16[768,128]{1,0:T(8,128)(2,1)S(1)}, u32[]{:S(2)}, u32[]{:S(2)}) collective-permute-start(bf16[768,128]{1,0:T(8,128)(2,1)S(1)} %get-tuple-element.17), channel_id=1, source_target_pairs={{0,2},{2,0},{1,3},{3,1},{4,6},{6,4},{5,7},{7,5},{8,10},{10,8},{9,1... | collective-permute-start | bytes 589832 | tf_op jit(solution)/shard_map/ppermute | solution.py:104
  135.1 17.9 %collective-permute-done.23.refs_3_ = bf16[768,128]{1,0:T(8,128)(2,1)S(1)} collective-permute-done((bf16[768,128]{1,0:T(8,128)(2,1)S(1)}, bf16[768,128]{1,0:T(8,128)(2,1)S(1)}, u32[]{:S(2)}, u32[]{:S(2)}) %collective-permute-start.23) | collective-permute-done | bytes 196640 | tf_op jit(solution)/shard_map/ppermute | solution.py:104
  153.0 1.6 %shard_map.73 = f32[1024,128]{1,0:T(8,128)} custom-call(s32[128]{0:T(128)S(1)} %xor_add_fusion.place_ref, f32[256,128]{1,0:T(8,128)S(1)} %broadcast_select_fusion.3.refs_0_, f32[768,128]{1,0:T(8,128)S(1)} %broadcast_select_fusion.refs_1_, bf16[256,128]{1,0:T(8,128)(2,1)S(1)} %collective-permute-done.21.refs_2_, ...), custom_call_target="tpu_custom_call" | custom-call | tf_op jit(solution)/shard_map/pallas_call | solution.py:58
  (45 shorter events, 0.6 us)
Async XLA Ops:
  0.0 1.0 copy-start
  2.6 11.1 %collective-permute-start = (bf16[8,4096]{1,0:T(8,128)(2,1)S(1)}, bf16[8,4096]{1,0:T(8,128)(2,1)S(1)}, u32[]{:S(2)}, u32[]{:S(2)}) collective-permute-start(bf16[8,4096]{1,0:T(8,128)(2,1)S(1)} %convert_element_type.14), channel_id=1, source_target_pairs={{0,256},{64,320},{128,384},{192,448},{256,0},{320,64},{384,128},{4... | collective-permute-start | bytes 196616 | tf_op jit(solution)/shard_map/ppermute | solution.py:30
  13.7 12.2 %collective-permute-start.4 = (bf16[16,4096]{1,0:T(8,128)(2,1)S(1)}, bf16[16,4096]{1,0:T(8,128)(2,1)S(1)}, u32[]{:S(2)}, u32[]{:S(2)}) collective-permute-start(bf16[16,4096]{1,0:T(8,128)(2,1)S(1)} %pad_maximum_fusion.15), channel_id=1, source_target_pairs={{0,128},{64,192},{128,0},{192,64},{256,384},{320,448},{384,256},{4... | collective-permute-start | bytes 393224 | tf_op jit(solution)/shard_map/ppermute | solution.py:30
  20.9 7.2 %collective-permute-start.1 = (bf16[16,4096]{1,0:T(8,128)(2,1)S(1)}, bf16[16,4096]{1,0:T(8,128)(2,1)S(1)}, u32[]{:S(2)}, u32[]{:S(2)}) collective-permute-start(bf16[16,4096]{1,0:T(8,128)(2,1)S(1)} %pad_maximum_fusion.15), channel_id=1, source_target_pairs={{0,16},{16,0},{32,48},{48,32},{1,17},{17,1},{33,49},{49,33},{2,18}... | collective-permute-start | bytes 393224 | tf_op jit(solution)/shard_map/ppermute | solution.py:30
  24.0 10.6 %collective-permute-start.8 = (bf16[16,4096]{1,0:T(8,128)(2,1)S(1)}, bf16[16,4096]{1,0:T(8,128)(2,1)S(1)}, u32[]{:S(2)}, u32[]{:S(2)}) collective-permute-start(bf16[16,4096]{1,0:T(8,128)(2,1)S(1)} %pad_maximum_fusion.15), channel_id=1, source_target_pairs={{0,64},{64,0},{128,192},{192,128},{256,320},{320,256},{384,448},{4... | collective-permute-start | bytes 393224 | tf_op jit(solution)/shard_map/ppermute | solution.py:30
  25.9 12.4 %collective-permute-start.5 = (bf16[16,4096]{1,0:T(8,128)(2,1)S(1)}, bf16[16,4096]{1,0:T(8,128)(2,1)S(1)}, u32[]{:S(2)}, u32[]{:S(2)}) collective-permute-start(bf16[16,4096]{1,0:T(8,128)(2,1)S(1)} %collective-permute-done.4), channel_id=1, source_target_pairs={{0,4},{4,0},{8,12},{12,8},{1,5},{5,1},{9,13},{13,9},{2,6},{6,2},{1... | collective-permute-start | bytes 393224 | tf_op jit(solution)/shard_map/ppermute | solution.py:30
  28.1 18.9 %collective-permute-start.2 = (bf16[32,4096]{1,0:T(8,128)(2,1)S(1)}, bf16[32,4096]{1,0:T(8,128)(2,1)S(1)}, u32[]{:S(2)}, u32[]{:S(2)}) collective-permute-start(bf16[32,4096]{1,0:T(8,128)(2,1)S(1)} %pad_maximum_fusion.9), channel_id=1, source_target_pairs={{0,4},{4,0},{8,12},{12,8},{1,5},{5,1},{9,13},{13,9},{2,6},{6,2},{1... | collective-permute-start | bytes 786440 | tf_op jit(solution)/shard_map/ppermute | solution.py:30
  31.3 13.5 %collective-permute-start.12 = (bf16[16,4096]{1,0:T(8,128)(2,1)S(1)}, bf16[16,4096]{1,0:T(8,128)(2,1)S(1)}, u32[]{:S(2)}, u32[]{:S(2)}) collective-permute-start(bf16[16,4096]{1,0:T(8,128)(2,1)S(1)} %collective-permute-done.4), channel_id=1, source_target_pairs={{0,64},{64,0},{128,192},{192,128},{256,320},{320,256},{384,448},{4... | collective-permute-start | bytes 393224 | tf_op jit(solution)/shard_map/ppermute | solution.py:30
  34.6 6.9 %collective-permute-start.9 = (bf16[16,4096]{1,0:T(8,128)(2,1)S(1)}, bf16[16,4096]{1,0:T(8,128)(2,1)S(1)}, u32[]{:S(2)}, u32[]{:S(2)}) collective-permute-start(bf16[16,4096]{1,0:T(8,128)(2,1)S(1)} %collective-permute-done.8), channel_id=1, source_target_pairs={{0,48},{16,32},{32,16},{48,0},{1,49},{17,33},{33,17},{49,1},{2,50}... | collective-permute-start | bytes 393224 | tf_op jit(solution)/shard_map/ppermute | solution.py:30
  38.4 14.6 %collective-permute-start.6 = (bf16[32,4096]{1,0:T(8,128)(2,1)S(1)}, bf16[32,4096]{1,0:T(8,128)(2,1)S(1)}, u32[]{:S(2)}, u32[]{:S(2)}) collective-permute-start(bf16[32,4096]{1,0:T(8,128)(2,1)S(1)} %pad_maximum_fusion.10), channel_id=1, source_target_pairs={{0,48},{16,32},{32,16},{48,0},{1,49},{17,33},{33,17},{49,1},{2,50}... | collective-permute-start | bytes 786440 | tf_op jit(solution)/shard_map/ppermute | solution.py:30
  41.6 14.3 %collective-permute-start.10 = (bf16[32,4096]{1,0:T(8,128)(2,1)S(1)}, bf16[32,4096]{1,0:T(8,128)(2,1)S(1)}, u32[]{:S(2)}, u32[]{:S(2)}) collective-permute-start(bf16[32,4096]{1,0:T(8,128)(2,1)S(1)} %pad_maximum_fusion.11), channel_id=1, source_target_pairs={{0,12},{4,8},{8,4},{12,0},{1,13},{5,9},{9,5},{13,1},{2,14},{6,10},... | collective-permute-start | bytes 786440 | tf_op jit(solution)/shard_map/ppermute | solution.py:30
  44.8 6.3 %collective-permute-start.13 = (bf16[16,4096]{1,0:T(8,128)(2,1)S(1)}, bf16[16,4096]{1,0:T(8,128)(2,1)S(1)}, u32[]{:S(2)}, u32[]{:S(2)}) collective-permute-start(bf16[16,4096]{1,0:T(8,128)(2,1)S(1)} %collective-permute-done.12), channel_id=1, source_target_pairs={{0,12},{4,8},{8,4},{12,0},{1,13},{5,9},{9,5},{13,1},{2,14},{6,10},... | collective-permute-start | bytes 393224 | tf_op jit(solution)/shard_map/ppermute | solution.py:30
  47.0 17.5 %collective-permute-start.3 = (bf16[64,4096]{1,0:T(8,128)(2,1)S(1)}, bf16[64,4096]{1,0:T(8,128)(2,1)S(1)}, u32[]{:S(2)}, u32[]{:S(2)}) collective-permute-start(bf16[64,4096]{1,0:T(8,128)(2,1)S(1)} %pad_maximum_fusion.5), channel_id=1, source_target_pairs={{0,48},{16,32},{32,16},{48,0},{1,49},{17,33},{33,17},{49,1},{2,50}... | collective-permute-start | bytes 1572872 | tf_op jit(solution)/shard_map/ppermute | solution.py:30
  51.1 8.2 %collective-permute-start.14 = (bf16[32,4096]{1,0:T(8,128)(2,1)S(1)}, bf16[32,4096]{1,0:T(8,128)(2,1)S(1)}, u32[]{:S(2)}, u32[]{:S(2)}) collective-permute-start(bf16[32,4096]{1,0:T(8,128)(2,1)S(1)} %pad_maximum_fusion.12), channel_id=1, source_target_pairs={{0,16},{16,0},{32,48},{48,32},{1,17},{17,1},{33,49},{49,33},{2,18}... | collective-permute-start | bytes 786440 | tf_op jit(solution)/shard_map/ppermute | solution.py:30
  53.1 15.3 %collective-permute-start.7 = (bf16[64,4096]{1,0:T(8,128)(2,1)S(1)}, bf16[64,4096]{1,0:T(8,128)(2,1)S(1)}, u32[]{:S(2)}, u32[]{:S(2)}) collective-permute-start(bf16[64,4096]{1,0:T(8,128)(2,1)S(1)} %pad_maximum_fusion.6), channel_id=1, source_target_pairs={{0,12},{4,8},{8,4},{12,0},{1,13},{5,9},{9,5},{13,1},{2,14},{6,10},... | collective-permute-start | bytes 1572872 | tf_op jit(solution)/shard_map/ppermute | solution.py:30
  56.0 15.0 %collective-permute-start.11 = (bf16[64,4096]{1,0:T(8,128)(2,1)S(1)}, bf16[64,4096]{1,0:T(8,128)(2,1)S(1)}, u32[]{:S(2)}, u32[]{:S(2)}) collective-permute-start(bf16[64,4096]{1,0:T(8,128)(2,1)S(1)} %pad_maximum_fusion.7), channel_id=1, source_target_pairs={{0,16},{16,0},{32,48},{48,32},{1,17},{17,1},{33,49},{49,33},{2,18}... | collective-permute-start | bytes 1572872 | tf_op jit(solution)/shard_map/ppermute | solution.py:30
  59.4 18.8 %collective-permute-start.15 = (bf16[64,4096]{1,0:T(8,128)(2,1)S(1)}, bf16[64,4096]{1,0:T(8,128)(2,1)S(1)}, u32[]{:S(2)}, u32[]{:S(2)}) collective-permute-start(bf16[64,4096]{1,0:T(8,128)(2,1)S(1)} %pad_maximum_fusion.8), channel_id=1, source_target_pairs={{0,4},{4,0},{8,12},{12,8},{1,5},{5,1},{9,13},{13,9},{2,6},{6,2},{1... | collective-permute-start | bytes 1572872 | tf_op jit(solution)/shard_map/ppermute | solution.py:30
  64.5 47.9 %collective-permute-start.17 = (bf16[128,4096]{1,0:T(8,128)(2,1)S(1)}, bf16[128,4096]{1,0:T(8,128)(2,1)S(1)}, u32[]{:S(2)}, u32[]{:S(2)}) collective-permute-start(bf16[128,4096]{1,0:T(8,128)(2,1)S(1)} %pad_maximum_fusion), channel_id=1, source_target_pairs={{0,12},{4,8},{8,4},{12,0},{1,13},{5,9},{9,5},{13,1},{2,14},{6,10},... | collective-permute-start | bytes 3145736 | tf_op jit(solution)/shard_map/ppermute | solution.py:30
  68.4 13.7 %copy-start.1 = (bf16[1,512,4096]{2,1,0:T(8,128)(2,1)S(1)}, bf16[1,512,4096]{2,1,0:T(8,128)(2,1)}, u32[]{:S(2)}) copy-start(bf16[1,512,4096]{2,1,0:T(8,128)(2,1)} %param.7) | copy-start | bytes 12582916
  71.1 42.9 %collective-permute-start.18 = (bf16[128,4096]{1,0:T(8,128)(2,1)S(1)}, bf16[128,4096]{1,0:T(8,128)(2,1)S(1)}, u32[]{:S(2)}, u32[]{:S(2)}) collective-permute-start(bf16[128,4096]{1,0:T(8,128)(2,1)S(1)} %pad_maximum_fusion.1), channel_id=1, source_target_pairs={{0,16},{16,0},{32,48},{48,32},{1,17},{17,1},{33,49},{49,33},{2,18}... | collective-permute-start | bytes 3145736 | tf_op jit(solution)/shard_map/ppermute | solution.py:30
  73.0 42.5 %collective-permute-start.19 = (bf16[128,4096]{1,0:T(8,128)(2,1)S(1)}, bf16[128,4096]{1,0:T(8,128)(2,1)S(1)}, u32[]{:S(2)}, u32[]{:S(2)}) collective-permute-start(bf16[128,4096]{1,0:T(8,128)(2,1)S(1)} %pad_maximum_fusion.2), channel_id=1, source_target_pairs={{0,4},{4,0},{8,12},{12,8},{1,5},{5,1},{9,13},{13,9},{2,6},{6,2},{1... | collective-permute-start | bytes 3145736 | tf_op jit(solution)/shard_map/ppermute | solution.py:30
  78.3 38.8 %collective-permute-start.20 = (bf16[128,4096]{1,0:T(8,128)(2,1)S(1)}, bf16[128,4096]{1,0:T(8,128)(2,1)S(1)}, u32[]{:S(2)}, u32[]{:S(2)}) collective-permute-start(bf16[128,4096]{1,0:T(8,128)(2,1)S(1)} %pad_maximum_fusion.3), channel_id=1, source_target_pairs={{0,48},{16,32},{32,16},{48,0},{1,49},{17,33},{33,17},{49,1},{2,50}... | collective-permute-start | bytes 3145736 | tf_op jit(solution)/shard_map/ppermute | solution.py:30
  85.3 12.9 %collective-permute-start.16 = (f32[256,256]{1,0:T(8,128)S(1)}, f32[256,256]{1,0:T(8,128)S(1)}, u32[]{:S(2)}, u32[]{:S(2)}) collective-permute-start(f32[256,256]{1,0:T(8,128)S(1)} %pad_maximum_fusion.13), channel_id=1, source_target_pairs={{0,1},{1,0},{2,3},{3,2},{4,5},{5,4},{6,7},{7,6},{8,9},{9,8},{10,11... | collective-permute-start | bytes 786440 | tf_op jit(solution)/shard_map/ppermute | solution.py:100
  98.3 20.5 %collective-permute-start.21 = (bf16[256,128]{1,0:T(8,128)(2,1)S(1)}, bf16[256,128]{1,0:T(8,128)(2,1)S(1)}, u32[]{:S(2)}, u32[]{:S(2)}) collective-permute-start(bf16[256,128]{1,0:T(8,128)(2,1)S(1)} %get-tuple-element.20), channel_id=1, source_target_pairs={{0,2},{2,0},{1,3},{3,1},{4,6},{6,4},{5,7},{7,5},{8,10},{10,8},{9,1... | collective-permute-start | bytes 196616 | tf_op jit(solution)/shard_map/ppermute | solution.py:104
  118.6 2.4 %copy-start.2 = (s32[128]{0:T(128)S(1)}, s32[128]{0:T(128)}, u32[]{:S(2)}) copy-start(s32[128]{0:T(128)} %constant.33.clone) | copy-start | bytes 1540
  118.6 2.4 %copy-start.3 = (s32[128]{0:T(128)S(1)}, s32[128]{0:T(128)}, u32[]{:S(2)}) copy-start(s32[128]{0:T(128)} %constant.32.clone) | copy-start | bytes 1540
  118.6 2.4 %copy-start.4 = (s32[128]{0:T(128)S(1)}, s32[128]{0:T(128)}, u32[]{:S(2)}) copy-start(s32[128]{0:T(128)} %constant.31.clone) | copy-start | bytes 1540
  118.8 4.2 %collective-permute-start.22 = (f32[768,256]{1,0:T(8,128)S(1)}, f32[768,256]{1,0:T(8,128)S(1)}, u32[]{:S(2)}, u32[]{:S(2)}) collective-permute-start(f32[768,256]{1,0:T(8,128)S(1)} %pad_maximum_fusion.4), channel_id=1, source_target_pairs={{0,1},{1,0},{2,3},{3,2},{4,5},{5,4},{6,7},{7,6},{8,9},{9,8},{10,11... | collective-permute-start | bytes 2359304 | tf_op jit(solution)/shard_map/ppermute | solution.py:100
  123.1 29.9 %collective-permute-start.23 = (bf16[768,128]{1,0:T(8,128)(2,1)S(1)}, bf16[768,128]{1,0:T(8,128)(2,1)S(1)}, u32[]{:S(2)}, u32[]{:S(2)}) collective-permute-start(bf16[768,128]{1,0:T(8,128)(2,1)S(1)} %get-tuple-element.17), channel_id=1, source_target_pairs={{0,2},{2,0},{1,3},{3,1},{4,6},{6,4},{5,7},{7,5},{8,10},{10,8},{9,1... | collective-permute-start | bytes 589832 | tf_op jit(solution)/shard_map/ppermute | solution.py:104

commit v7 on v6

--- a/solution.py
+++ b/solution.py
@@ -71,10 +71,11 @@
     resident = train_grads[0]
 
     own = condition(query_grads[0], left_factor[0], right_factor[0]), [(0, 0, 0)]
-    pair = joined([own, partner(own, "z", 4)])
-    two = partner(pair, "z", 2)
-    one = partner(pair, "z", 1)
-    held = [pair, two, one, partner(two, "z", 1)]
+    four, two, one = (partner(own, "z", bits) for bits in (4, 2, 1))
+    count = own[0].shape[0]
+    rows, owners = partner(joined([two, one]), "z", 4)
+    pairs = [joined([p, (rows[k * count : (k + 1) * count], owners[k : k + 1])]) for k, p in enumerate((two, one))]
+    held = [joined([own, four])] + pairs + [partner(pairs[0], "z", 1)]
     for step in range(len(TURNS)):
         came = [partner(p, *TURNS[(k + step) % len(TURNS)]) for k, p in enumerate(held)]
         if step < len(TURNS) - 1:

time: 155 us -> 163 us (1.052)
  the two profiles are of different devices: /device:TPU:41 before, /device:TPU:1 now
where the time goes in v7:
time: 163 us
  starting transfers between devices  102 us (63%)
  waiting for transfers between devices  42.4 us (26%)
  matrix products  13.6 us (8%)
    ppermute x21, starting transfers between devices, partner(): lax.ppermute(rows, axis, [(i, i ^ bits) for i in range(SIZES[AXES.index(a...  71.4 us
    ppermute x2, waiting for transfers between devices, on_device(): arrived.append(lax.ppermute(cross, 'half', [(0, 1), (1, 0)]))  20.5 us
    ppermute x2, starting transfers between devices, on_device(): arrived.append(lax.ppermute(cross, 'half', [(0, 1), (1, 0)]))  20.3 us
    ppermute x21, waiting for transfers between devices, partner(): lax.ppermute(rows, axis, [(i, i ^ bits) for i in range(SIZES[AXES.index(a...  20 us
    dot_general x8, matrix products, on_device(): lax.dot_general(rows, resident, (((1,), (1,)), ((), ())), preferred_eleme...  12.2 us
    ppermute x2, starting transfers between devices, on_device(): other = lax.ppermute(away, 'core', [(0, 1), (1, 0)])  10.4 us
  transfers between devices with their start and end apart: 25, of which 8 were waited for; matrix products, arithmetic and copies ran while one was open for 8% of the time, Pallas kernels for 0%

profile of v7, /device:TPU:1, one launch (start us, length us, event | category | flops | bytes accessed | tf_op | source)
XLA Modules:
  0.0 162.6 jit_solution(11585603267000593763)
XLA Ops:
  0.0 1.0 reshape.6
  1.1 0.2 convolution_bitcast_fusion
  1.3 1.1 convolution_convert_fusion
  2.4 0.2 convert_element_type.14
  2.6 5.7 %collective-permute-start.4 = (bf16[8,4096]{1,0:T(8,128)(2,1)S(1)}, bf16[8,4096]{1,0:T(8,128)(2,1)S(1)}, u32[]{:S(2)}, u32[]{:S(2)}) collective-permute-start(bf16[8,4096]{1,0:T(8,128)(2,1)S(1)} %convert_element_type.14), channel_id=1, source_target_pairs={{0,128},{64,192},{128,0},{192,64},{256,384},{320,448},{384,256},{4... | collective-permute-start | bytes 196616 | tf_op jit(solution)/shard_map/ppermute | solution.py:30
  8.3 3.5 %collective-permute-start.5 = (bf16[8,4096]{1,0:T(8,128)(2,1)S(1)}, bf16[8,4096]{1,0:T(8,128)(2,1)S(1)}, u32[]{:S(2)}, u32[]{:S(2)}) collective-permute-start(bf16[8,4096]{1,0:T(8,128)(2,1)S(1)} %convert_element_type.14), channel_id=1, source_target_pairs={{0,64},{64,0},{128,192},{192,128},{256,320},{320,256},{384,448},{4... | collective-permute-start | bytes 196616 | tf_op jit(solution)/shard_map/ppermute | solution.py:30
  11.9 8.8 %collective-permute-start = (bf16[8,4096]{1,0:T(8,128)(2,1)S(1)}, bf16[8,4096]{1,0:T(8,128)(2,1)S(1)}, u32[]{:S(2)}, u32[]{:S(2)}) collective-permute-start(bf16[8,4096]{1,0:T(8,128)(2,1)S(1)} %convert_element_type.14), channel_id=1, source_target_pairs={{0,256},{64,320},{128,384},{192,448},{256,0},{320,64},{384,128},{4... | collective-permute-start | bytes 196616 | tf_op jit(solution)/shard_map/ppermute | solution.py:30
  20.8 1.9 %collective-permute-start.6 = (bf16[16,4096]{1,0:T(8,128)(2,1)S(1)}, bf16[16,4096]{1,0:T(8,128)(2,1)S(1)}, u32[]{:S(2)}, u32[]{:S(2)}) collective-permute-start(bf16[16,4096]{1,0:T(8,128)(2,1)S(1)} %pad_maximum_fusion.14), channel_id=1, source_target_pairs={{0,256},{64,320},{128,384},{192,448},{256,0},{320,64},{384,128},{4... | collective-permute-start | bytes 393224 | tf_op jit(solution)/shard_map/ppermute | solution.py:30
  22.7 4.3 %collective-permute-done = bf16[8,4096]{1,0:T(8,128)(2,1)S(1)} collective-permute-done((bf16[8,4096]{1,0:T(8,128)(2,1)S(1)}, bf16[8,4096]{1,0:T(8,128)(2,1)S(1)}, u32[]{:S(2)}, u32[]{:S(2)}) %collective-permute-start) | collective-permute-done | bytes 65568 | tf_op jit(solution)/shard_map/ppermute | solution.py:30
  27.0 3.2 %collective-permute-start.1 = (bf16[16,4096]{1,0:T(8,128)(2,1)S(1)}, bf16[16,4096]{1,0:T(8,128)(2,1)S(1)}, u32[]{:S(2)}, u32[]{:S(2)}) collective-permute-start(bf16[16,4096]{1,0:T(8,128)(2,1)S(1)} %pad_maximum_fusion.17), channel_id=1, source_target_pairs={{0,16},{16,0},{32,48},{48,32},{1,17},{17,1},{33,49},{49,33},{2,18}... | collective-permute-start | bytes 393224 | tf_op jit(solution)/shard_map/ppermute | solution.py:30
  30.2 9.7 %collective-permute-done.6 = bf16[16,4096]{1,0:T(8,128)(2,1)S(1)} collective-permute-done((bf16[16,4096]{1,0:T(8,128)(2,1)S(1)}, bf16[16,4096]{1,0:T(8,128)(2,1)S(1)}, u32[]{:S(2)}, u32[]{:S(2)}) %collective-permute-start.6) | collective-permute-done | bytes 131104 | tf_op jit(solution)/shard_map/ppermute | solution.py:30
  39.9 3.2 %collective-permute-start.7 = (bf16[16,4096]{1,0:T(8,128)(2,1)S(1)}, bf16[16,4096]{1,0:T(8,128)(2,1)S(1)}, u32[]{:S(2)}, u32[]{:S(2)}) collective-permute-start(bf16[16,4096]{1,0:T(8,128)(2,1)S(1)} %pad_maximum_fusion.15), channel_id=1, source_target_pairs={{0,4},{4,0},{8,12},{12,8},{1,5},{5,1},{9,13},{13,9},{2,6},{6,2},{1... | collective-permute-start | bytes 393224 | tf_op jit(solution)/shard_map/ppermute | solution.py:30
  43.1 1.9 %collective-permute-start.13 = (bf16[16,4096]{1,0:T(8,128)(2,1)S(1)}, bf16[16,4096]{1,0:T(8,128)(2,1)S(1)}, u32[]{:S(2)}, u32[]{:S(2)}) collective-permute-start(bf16[16,4096]{1,0:T(8,128)(2,1)S(1)} %pad_maximum_fusion.15), channel_id=1, source_target_pairs={{0,64},{64,0},{128,192},{192,128},{256,320},{320,256},{384,448},{4... | collective-permute-start | bytes 393224 | tf_op jit(solution)/shard_map/ppermute | solution.py:30
  45.1 2.1 %collective-permute-start.2 = (bf16[32,4096]{1,0:T(8,128)(2,1)S(1)}, bf16[32,4096]{1,0:T(8,128)(2,1)S(1)}, u32[]{:S(2)}, u32[]{:S(2)}) collective-permute-start(bf16[32,4096]{1,0:T(8,128)(2,1)S(1)} %pad_maximum_fusion.9), channel_id=1, source_target_pairs={{0,4},{4,0},{8,12},{12,8},{1,5},{5,1},{9,13},{13,9},{2,6},{6,2},{1... | collective-permute-start | bytes 786440 | tf_op jit(solution)/shard_map/ppermute | solution.py:30
  47.2 4.4 %collective-permute-start.10 = (bf16[16,4096]{1,0:T(8,128)(2,1)S(1)}, bf16[16,4096]{1,0:T(8,128)(2,1)S(1)}, u32[]{:S(2)}, u32[]{:S(2)}) collective-permute-start(bf16[16,4096]{1,0:T(8,128)(2,1)S(1)} %pad_maximum_fusion.18), channel_id=1, source_target_pairs={{0,48},{16,32},{32,16},{48,0},{1,49},{17,33},{33,17},{49,1},{2,50}... | collective-permute-start | bytes 393224 | tf_op jit(solution)/shard_map/ppermute | solution.py:30
  51.6 2.1 %collective-permute-start.8 = (bf16[32,4096]{1,0:T(8,128)(2,1)S(1)}, bf16[32,4096]{1,0:T(8,128)(2,1)S(1)}, u32[]{:S(2)}, u32[]{:S(2)}) collective-permute-start(bf16[32,4096]{1,0:T(8,128)(2,1)S(1)} %pad_maximum_fusion.10), channel_id=1, source_target_pairs={{0,48},{16,32},{32,16},{48,0},{1,49},{17,33},{33,17},{49,1},{2,50}... | collective-permute-start | bytes 786440 | tf_op jit(solution)/shard_map/ppermute | solution.py:30
  53.7 0.4 collective-permute-done.10
  54.1 4.6 %collective-permute-start.11 = (bf16[32,4096]{1,0:T(8,128)(2,1)S(1)}, bf16[32,4096]{1,0:T(8,128)(2,1)S(1)}, u32[]{:S(2)}, u32[]{:S(2)}) collective-permute-start(bf16[32,4096]{1,0:T(8,128)(2,1)S(1)} %pad_maximum_fusion.11), channel_id=1, source_target_pairs={{0,12},{4,8},{8,4},{12,0},{1,13},{5,9},{9,5},{13,1},{2,14},{6,10},... | collective-permute-start | bytes 786440 | tf_op jit(solution)/shard_map/ppermute | solution.py:30
  58.8 1.9 %collective-permute-start.14 = (bf16[16,4096]{1,0:T(8,128)(2,1)S(1)}, bf16[16,4096]{1,0:T(8,128)(2,1)S(1)}, u32[]{:S(2)}, u32[]{:S(2)}) collective-permute-start(bf16[16,4096]{1,0:T(8,128)(2,1)S(1)} %collective-permute-done.13), channel_id=1, source_target_pairs={{0,12},{4,8},{8,4},{12,0},{1,13},{5,9},{9,5},{13,1},{2,14},{6,10},... | collective-permute-start | bytes 393224 | tf_op jit(solution)/shard_map/ppermute | solution.py:30
  60.8 4.4 %collective-permute-start.3 = (bf16[64,4096]{1,0:T(8,128)(2,1)S(1)}, bf16[64,4096]{1,0:T(8,128)(2,1)S(1)}, u32[]{:S(2)}, u32[]{:S(2)}) collective-permute-start(bf16[64,4096]{1,0:T(8,128)(2,1)S(1)} %pad_maximum_fusion.5), channel_id=1, source_target_pairs={{0,48},{16,32},{32,16},{48,0},{1,49},{17,33},{33,17},{49,1},{2,50}... | collective-permute-start | bytes 1572872 | tf_op jit(solution)/shard_map/ppermute | solution.py:30
  65.2 1.6 collective-permute-done.14
  66.8 2.2 %collective-permute-start.15 = (bf16[32,4096]{1,0:T(8,128)(2,1)S(1)}, bf16[32,4096]{1,0:T(8,128)(2,1)S(1)}, u32[]{:S(2)}, u32[]{:S(2)}) collective-permute-start(bf16[32,4096]{1,0:T(8,128)(2,1)S(1)} %pad_maximum_fusion.12), channel_id=1, source_target_pairs={{0,16},{16,0},{32,48},{48,32},{1,17},{17,1},{33,49},{49,33},{2,18}... | collective-permute-start | bytes 786440 | tf_op jit(solution)/shard_map/ppermute | solution.py:30
  69.0 3.8 %collective-permute-start.9 = (bf16[64,4096]{1,0:T(8,128)(2,1)S(1)}, bf16[64,4096]{1,0:T(8,128)(2,1)S(1)}, u32[]{:S(2)}, u32[]{:S(2)}) collective-permute-start(bf16[64,4096]{1,0:T(8,128)(2,1)S(1)} %pad_maximum_fusion.6), channel_id=1, source_target_pairs={{0,12},{4,8},{8,4},{12,0},{1,13},{5,9},{9,5},{13,1},{2,14},{6,10},... | collective-permute-start | bytes 1572872 | tf_op jit(solution)/shard_map/ppermute | solution.py:30
  72.9 2.8 %collective-permute-start.12 = (bf16[64,4096]{1,0:T(8,128)(2,1)S(1)}, bf16[64,4096]{1,0:T(8,128)(2,1)S(1)}, u32[]{:S(2)}, u32[]{:S(2)}) collective-permute-start(bf16[64,4096]{1,0:T(8,128)(2,1)S(1)} %pad_maximum_fusion.7), channel_id=1, source_target_pairs={{0,16},{16,0},{32,48},{48,32},{1,17},{17,1},{33,49},{49,33},{2,18}... | collective-permute-start | bytes 1572872 | tf_op jit(solution)/shard_map/ppermute | solution.py:30
  75.8 1.9 %collective-permute-start.16 = (bf16[64,4096]{1,0:T(8,128)(2,1)S(1)}, bf16[64,4096]{1,0:T(8,128)(2,1)S(1)}, u32[]{:S(2)}, u32[]{:S(2)}) collective-permute-start(bf16[64,4096]{1,0:T(8,128)(2,1)S(1)} %pad_maximum_fusion.8), channel_id=1, source_target_pairs={{0,4},{4,0},{8,12},{12,8},{1,5},{5,1},{9,13},{13,9},{2,6},{6,2},{1... | collective-permute-start | bytes 1572872 | tf_op jit(solution)/shard_map/ppermute | solution.py:30
  77.8 3.0 %collective-permute-start.18 = (bf16[128,4096]{1,0:T(8,128)(2,1)S(1)}, bf16[128,4096]{1,0:T(8,128)(2,1)S(1)}, u32[]{:S(2)}, u32[]{:S(2)}) collective-permute-start(bf16[128,4096]{1,0:T(8,128)(2,1)S(1)} %pad_maximum_fusion), channel_id=1, source_target_pairs={{0,12},{4,8},{8,4},{12,0},{1,13},{5,9},{9,5},{13,1},{2,14},{6,10},... | collective-permute-start | bytes 3145736 | tf_op jit(solution)/shard_map/ppermute | solution.py:30
  80.8 2.2 %collective-permute-done.9 = bf16[64,4096]{1,0:T(8,128)(2,1)S(1)} collective-permute-done((bf16[64,4096]{1,0:T(8,128)(2,1)S(1)}, bf16[64,4096]{1,0:T(8,128)(2,1)S(1)}, u32[]{:S(2)}, u32[]{:S(2)}) %collective-permute-start.9) | collective-permute-done | bytes 524320 | tf_op jit(solution)/shard_map/ppermute | solution.py:30
  83.1 1.8 %collective-permute-done.12 = bf16[64,4096]{1,0:T(8,128)(2,1)S(1)} collective-permute-done((bf16[64,4096]{1,0:T(8,128)(2,1)S(1)}, bf16[64,4096]{1,0:T(8,128)(2,1)S(1)}, u32[]{:S(2)}, u32[]{:S(2)}) %collective-permute-start.12) | collective-permute-done | bytes 524320 | tf_op jit(solution)/shard_map/ppermute | solution.py:30
  85.0 2.3 %collective-permute-start.19 = (bf16[128,4096]{1,0:T(8,128)(2,1)S(1)}, bf16[128,4096]{1,0:T(8,128)(2,1)S(1)}, u32[]{:S(2)}, u32[]{:S(2)}) collective-permute-start(bf16[128,4096]{1,0:T(8,128)(2,1)S(1)} %pad_maximum_fusion.1), channel_id=1, source_target_pairs={{0,16},{16,0},{32,48},{48,32},{1,17},{17,1},{33,49},{49,33},{2,18}... | collective-permute-start | bytes 3145736 | tf_op jit(solution)/shard_map/ppermute | solution.py:30
  87.2 1.9 %collective-permute-start.20 = (bf16[128,4096]{1,0:T(8,128)(2,1)S(1)}, bf16[128,4096]{1,0:T(8,128)(2,1)S(1)}, u32[]{:S(2)}, u32[]{:S(2)}) collective-permute-start(bf16[128,4096]{1,0:T(8,128)(2,1)S(1)} %pad_maximum_fusion.2), channel_id=1, source_target_pairs={{0,4},{4,0},{8,12},{12,8},{1,5},{5,1},{9,13},{13,9},{2,6},{6,2},{1... | collective-permute-start | bytes 3145736 | tf_op jit(solution)/shard_map/ppermute | solution.py:30
  89.2 0.1 pad_maximum_fusion.3
  89.3 5.6 %collective-permute-start.21 = (bf16[128,4096]{1,0:T(8,128)(2,1)S(1)}, bf16[128,4096]{1,0:T(8,128)(2,1)S(1)}, u32[]{:S(2)}, u32[]{:S(2)}) collective-permute-start(bf16[128,4096]{1,0:T(8,128)(2,1)S(1)} %pad_maximum_fusion.3), channel_id=1, source_target_pairs={{0,48},{16,32},{32,16},{48,0},{1,49},{17,33},{33,17},{49,1},{2,50}... | collective-permute-start | bytes 3145736 | tf_op jit(solution)/shard_map/ppermute | solution.py:30
  94.9 1.5 fusion.12
  96.5 1.5 fusion.14
  98.1 8.2 %collective-permute-start.17 = (f32[256,256]{1,0:T(8,128)S(1)}, f32[256,256]{1,0:T(8,128)S(1)}, u32[]{:S(2)}, u32[]{:S(2)}) collective-permute-start(f32[256,256]{1,0:T(8,128)S(1)} %pad_maximum_fusion.13), channel_id=1, source_target_pairs={{0,1},{1,0},{2,3},{3,2},{4,5},{5,4},{6,7},{7,6},{8,9},{9,8},{10,11... | collective-permute-start | bytes 786440 | tf_op jit(solution)/shard_map/ppermute | solution.py:101
  106.3 1.5 fusion.16
  107.8 1.5 fusion.19
  109.5 11.0 %collective-permute-start.22 = (bf16[256,128]{1,0:T(8,128)(2,1)S(1)}, bf16[256,128]{1,0:T(8,128)(2,1)S(1)}, u32[]{:S(2)}, u32[]{:S(2)}) collective-permute-start(bf16[256,128]{1,0:T(8,128)(2,1)S(1)} %get-tuple-element.20), channel_id=1, source_target_pairs={{0,2},{2,0},{1,3},{3,1},{4,6},{6,4},{5,7},{7,5},{8,10},{10,8},{9,1... | collective-permute-start | bytes 196616 | tf_op jit(solution)/shard_map/ppermute | solution.py:105
  120.5 1.5 fusion.22
  122.0 1.5 fusion.25
  123.6 1.5 fusion.28
  125.1 1.5 fusion.31
  126.8 2.2 %collective-permute-start.23 = (f32[768,256]{1,0:T(8,128)S(1)}, f32[768,256]{1,0:T(8,128)S(1)}, u32[]{:S(2)}, u32[]{:S(2)}) collective-permute-start(f32[768,256]{1,0:T(8,128)S(1)} %pad_maximum_fusion.4), channel_id=1, source_target_pairs={{0,1},{1,0},{2,3},{3,2},{4,5},{5,4},{6,7},{7,6},{8,9},{9,8},{10,11... | collective-permute-start | bytes 2359304 | tf_op jit(solution)/shard_map/ppermute | solution.py:101
  129.1 1.9 %collective-permute-done.23 = f32[768,256]{1,0:T(8,128)S(1)} collective-permute-done((f32[768,256]{1,0:T(8,128)S(1)}, f32[768,256]{1,0:T(8,128)S(1)}, u32[]{:S(2)}, u32[]{:S(2)}) %collective-permute-start.23) | collective-permute-done | bytes 786464 | tf_op jit(solution)/shard_map/ppermute | solution.py:101
  131.0 0.1 select_convert_fusion
  131.2 9.2 %collective-permute-start.24 = (bf16[768,128]{1,0:T(8,128)(2,1)S(1)}, bf16[768,128]{1,0:T(8,128)(2,1)S(1)}, u32[]{:S(2)}, u32[]{:S(2)}) collective-permute-start(bf16[768,128]{1,0:T(8,128)(2,1)S(1)} %get-tuple-element.17), channel_id=1, source_target_pairs={{0,2},{2,0},{1,3},{3,1},{4,6},{6,4},{5,7},{7,5},{8,10},{10,8},{9,1... | collective-permute-start | bytes 589832 | tf_op jit(solution)/shard_map/ppermute | solution.py:105
  140.5 20.5 %collective-permute-done.24.refs_3_ = bf16[768,128]{1,0:T(8,128)(2,1)S(1)} collective-permute-done((bf16[768,128]{1,0:T(8,128)(2,1)S(1)}, bf16[768,128]{1,0:T(8,128)(2,1)S(1)}, u32[]{:S(2)}, u32[]{:S(2)}) %collective-permute-start.24) | collective-permute-done | bytes 196640 | tf_op jit(solution)/shard_map/ppermute | solution.py:105
  161.0 1.6 shard_map.73
  (51 shorter events, 0.9 us)
Async XLA Ops:
  0.0 1.0 copy-start
  2.6 18.1 %collective-permute-start.4 = (bf16[8,4096]{1,0:T(8,128)(2,1)S(1)}, bf16[8,4096]{1,0:T(8,128)(2,1)S(1)}, u32[]{:S(2)}, u32[]{:S(2)}) collective-permute-start(bf16[8,4096]{1,0:T(8,128)(2,1)S(1)} %convert_element_type.14), channel_id=1, source_target_pairs={{0,128},{64,192},{128,0},{192,64},{256,384},{320,448},{384,256},{4... | collective-permute-start | bytes 196616 | tf_op jit(solution)/shard_map/ppermute | solution.py:30
  8.3 12.4 %collective-permute-start.5 = (bf16[8,4096]{1,0:T(8,128)(2,1)S(1)}, bf16[8,4096]{1,0:T(8,128)(2,1)S(1)}, u32[]{:S(2)}, u32[]{:S(2)}) collective-permute-start(bf16[8,4096]{1,0:T(8,128)(2,1)S(1)} %convert_element_type.14), channel_id=1, source_target_pairs={{0,64},{64,0},{128,192},{192,128},{256,320},{320,256},{384,448},{4... | collective-permute-start | bytes 196616 | tf_op jit(solution)/shard_map/ppermute | solution.py:30
  11.9 15.1 %collective-permute-start = (bf16[8,4096]{1,0:T(8,128)(2,1)S(1)}, bf16[8,4096]{1,0:T(8,128)(2,1)S(1)}, u32[]{:S(2)}, u32[]{:S(2)}) collective-permute-start(bf16[8,4096]{1,0:T(8,128)(2,1)S(1)} %convert_element_type.14), channel_id=1, source_target_pairs={{0,256},{64,320},{128,384},{192,448},{256,0},{320,64},{384,128},{4... | collective-permute-start | bytes 196616 | tf_op jit(solution)/shard_map/ppermute | solution.py:30
  20.8 19.1 %collective-permute-start.6 = (bf16[16,4096]{1,0:T(8,128)(2,1)S(1)}, bf16[16,4096]{1,0:T(8,128)(2,1)S(1)}, u32[]{:S(2)}, u32[]{:S(2)}) collective-permute-start(bf16[16,4096]{1,0:T(8,128)(2,1)S(1)} %pad_maximum_fusion.14), channel_id=1, source_target_pairs={{0,256},{64,320},{128,384},{192,448},{256,0},{320,64},{384,128},{4... | collective-permute-start | bytes 393224 | tf_op jit(solution)/shard_map/ppermute | solution.py:30
  27.0 18.1 %collective-permute-start.1 = (bf16[16,4096]{1,0:T(8,128)(2,1)S(1)}, bf16[16,4096]{1,0:T(8,128)(2,1)S(1)}, u32[]{:S(2)}, u32[]{:S(2)}) collective-permute-start(bf16[16,4096]{1,0:T(8,128)(2,1)S(1)} %pad_maximum_fusion.17), channel_id=1, source_target_pairs={{0,16},{16,0},{32,48},{48,32},{1,17},{17,1},{33,49},{49,33},{2,18}... | collective-permute-start | bytes 393224 | tf_op jit(solution)/shard_map/ppermute | solution.py:30
  39.9 11.7 %collective-permute-start.7 = (bf16[16,4096]{1,0:T(8,128)(2,1)S(1)}, bf16[16,4096]{1,0:T(8,128)(2,1)S(1)}, u32[]{:S(2)}, u32[]{:S(2)}) collective-permute-start(bf16[16,4096]{1,0:T(8,128)(2,1)S(1)} %pad_maximum_fusion.15), channel_id=1, source_target_pairs={{0,4},{4,0},{8,12},{12,8},{1,5},{5,1},{9,13},{13,9},{2,6},{6,2},{1... | collective-permute-start | bytes 393224 | tf_op jit(solution)/shard_map/ppermute | solution.py:30
  43.1 15.7 %collective-permute-start.13 = (bf16[16,4096]{1,0:T(8,128)(2,1)S(1)}, bf16[16,4096]{1,0:T(8,128)(2,1)S(1)}, u32[]{:S(2)}, u32[]{:S(2)}) collective-permute-start(bf16[16,4096]{1,0:T(8,128)(2,1)S(1)} %pad_maximum_fusion.15), channel_id=1, source_target_pairs={{0,64},{64,0},{128,192},{192,128},{256,320},{320,256},{384,448},{4... | collective-permute-start | bytes 393224 | tf_op jit(solution)/shard_map/ppermute | solution.py:30
  45.1 15.6 %collective-permute-start.2 = (bf16[32,4096]{1,0:T(8,128)(2,1)S(1)}, bf16[32,4096]{1,0:T(8,128)(2,1)S(1)}, u32[]{:S(2)}, u32[]{:S(2)}) collective-permute-start(bf16[32,4096]{1,0:T(8,128)(2,1)S(1)} %pad_maximum_fusion.9), channel_id=1, source_target_pairs={{0,4},{4,0},{8,12},{12,8},{1,5},{5,1},{9,13},{13,9},{2,6},{6,2},{1... | collective-permute-start | bytes 786440 | tf_op jit(solution)/shard_map/ppermute | solution.py:30
  47.2 6.9 %collective-permute-start.10 = (bf16[16,4096]{1,0:T(8,128)(2,1)S(1)}, bf16[16,4096]{1,0:T(8,128)(2,1)S(1)}, u32[]{:S(2)}, u32[]{:S(2)}) collective-permute-start(bf16[16,4096]{1,0:T(8,128)(2,1)S(1)} %pad_maximum_fusion.18), channel_id=1, source_target_pairs={{0,48},{16,32},{32,16},{48,0},{1,49},{17,33},{33,17},{49,1},{2,50}... | collective-permute-start | bytes 393224 | tf_op jit(solution)/shard_map/ppermute | solution.py:30
  51.6 17.4 %collective-permute-start.8 = (bf16[32,4096]{1,0:T(8,128)(2,1)S(1)}, bf16[32,4096]{1,0:T(8,128)(2,1)S(1)}, u32[]{:S(2)}, u32[]{:S(2)}) collective-permute-start(bf16[32,4096]{1,0:T(8,128)(2,1)S(1)} %pad_maximum_fusion.10), channel_id=1, source_target_pairs={{0,48},{16,32},{32,16},{48,0},{1,49},{17,33},{33,17},{49,1},{2,50}... | collective-permute-start | bytes 786440 | tf_op jit(solution)/shard_map/ppermute | solution.py:30
  54.1 18.7 %collective-permute-start.11 = (bf16[32,4096]{1,0:T(8,128)(2,1)S(1)}, bf16[32,4096]{1,0:T(8,128)(2,1)S(1)}, u32[]{:S(2)}, u32[]{:S(2)}) collective-permute-start(bf16[32,4096]{1,0:T(8,128)(2,1)S(1)} %pad_maximum_fusion.11), channel_id=1, source_target_pairs={{0,12},{4,8},{8,4},{12,0},{1,13},{5,9},{9,5},{13,1},{2,14},{6,10},... | collective-permute-start | bytes 786440 | tf_op jit(solution)/shard_map/ppermute | solution.py:30
  58.8 7.9 %collective-permute-start.14 = (bf16[16,4096]{1,0:T(8,128)(2,1)S(1)}, bf16[16,4096]{1,0:T(8,128)(2,1)S(1)}, u32[]{:S(2)}, u32[]{:S(2)}) collective-permute-start(bf16[16,4096]{1,0:T(8,128)(2,1)S(1)} %collective-permute-done.13), channel_id=1, source_target_pairs={{0,12},{4,8},{8,4},{12,0},{1,13},{5,9},{9,5},{13,1},{2,14},{6,10},... | collective-permute-start | bytes 393224 | tf_op jit(solution)/shard_map/ppermute | solution.py:30
  60.8 16.9 %collective-permute-start.3 = (bf16[64,4096]{1,0:T(8,128)(2,1)S(1)}, bf16[64,4096]{1,0:T(8,128)(2,1)S(1)}, u32[]{:S(2)}, u32[]{:S(2)}) collective-permute-start(bf16[64,4096]{1,0:T(8,128)(2,1)S(1)} %pad_maximum_fusion.5), channel_id=1, source_target_pairs={{0,48},{16,32},{32,16},{48,0},{1,49},{17,33},{33,17},{49,1},{2,50}... | collective-permute-start | bytes 1572872 | tf_op jit(solution)/shard_map/ppermute | solution.py:30
  66.8 9.0 %collective-permute-start.15 = (bf16[32,4096]{1,0:T(8,128)(2,1)S(1)}, bf16[32,4096]{1,0:T(8,128)(2,1)S(1)}, u32[]{:S(2)}, u32[]{:S(2)}) collective-permute-start(bf16[32,4096]{1,0:T(8,128)(2,1)S(1)} %pad_maximum_fusion.12), channel_id=1, source_target_pairs={{0,16},{16,0},{32,48},{48,32},{1,17},{17,1},{33,49},{49,33},{2,18}... | collective-permute-start | bytes 786440 | tf_op jit(solution)/shard_map/ppermute | solution.py:30
  69.0 13.9 %collective-permute-start.9 = (bf16[64,4096]{1,0:T(8,128)(2,1)S(1)}, bf16[64,4096]{1,0:T(8,128)(2,1)S(1)}, u32[]{:S(2)}, u32[]{:S(2)}) collective-permute-start(bf16[64,4096]{1,0:T(8,128)(2,1)S(1)} %pad_maximum_fusion.6), channel_id=1, source_target_pairs={{0,12},{4,8},{8,4},{12,0},{1,13},{5,9},{9,5},{13,1},{2,14},{6,10},... | collective-permute-start | bytes 1572872 | tf_op jit(solution)/shard_map/ppermute | solution.py:30
  72.9 11.9 %collective-permute-start.12 = (bf16[64,4096]{1,0:T(8,128)(2,1)S(1)}, bf16[64,4096]{1,0:T(8,128)(2,1)S(1)}, u32[]{:S(2)}, u32[]{:S(2)}) collective-permute-start(bf16[64,4096]{1,0:T(8,128)(2,1)S(1)} %pad_maximum_fusion.7), channel_id=1, source_target_pairs={{0,16},{16,0},{32,48},{48,32},{1,17},{17,1},{33,49},{49,33},{2,18}... | collective-permute-start | bytes 1572872 | tf_op jit(solution)/shard_map/ppermute | solution.py:30
  75.8 13.4 %collective-permute-start.16 = (bf16[64,4096]{1,0:T(8,128)(2,1)S(1)}, bf16[64,4096]{1,0:T(8,128)(2,1)S(1)}, u32[]{:S(2)}, u32[]{:S(2)}) collective-permute-start(bf16[64,4096]{1,0:T(8,128)(2,1)S(1)} %pad_maximum_fusion.8), channel_id=1, source_target_pairs={{0,4},{4,0},{8,12},{12,8},{1,5},{5,1},{9,13},{13,9},{2,6},{6,2},{1... | collective-permute-start | bytes 1572872 | tf_op jit(solution)/shard_map/ppermute | solution.py:30
  77.8 42.7 %collective-permute-start.18 = (bf16[128,4096]{1,0:T(8,128)(2,1)S(1)}, bf16[128,4096]{1,0:T(8,128)(2,1)S(1)}, u32[]{:S(2)}, u32[]{:S(2)}) collective-permute-start(bf16[128,4096]{1,0:T(8,128)(2,1)S(1)} %pad_maximum_fusion), channel_id=1, source_target_pairs={{0,12},{4,8},{8,4},{12,0},{1,13},{5,9},{9,5},{13,1},{2,14},{6,10},... | collective-permute-start | bytes 3145736 | tf_op jit(solution)/shard_map/ppermute | solution.py:30
  83.0 11.9 %copy-start.1 = (bf16[1,512,4096]{2,1,0:T(8,128)(2,1)S(1)}, bf16[1,512,4096]{2,1,0:T(8,128)(2,1)}, u32[]{:S(2)}) copy-start(bf16[1,512,4096]{2,1,0:T(8,128)(2,1)} %param.7) | copy-start | bytes 12582916
  85.0 37.1 %collective-permute-start.19 = (bf16[128,4096]{1,0:T(8,128)(2,1)S(1)}, bf16[128,4096]{1,0:T(8,128)(2,1)S(1)}, u32[]{:S(2)}, u32[]{:S(2)}) collective-permute-start(bf16[128,4096]{1,0:T(8,128)(2,1)S(1)} %pad_maximum_fusion.1), channel_id=1, source_target_pairs={{0,16},{16,0},{32,48},{48,32},{1,17},{17,1},{33,49},{49,33},{2,18}... | collective-permute-start | bytes 3145736 | tf_op jit(solution)/shard_map/ppermute | solution.py:30
  87.2 36.3 %collective-permute-start.20 = (bf16[128,4096]{1,0:T(8,128)(2,1)S(1)}, bf16[128,4096]{1,0:T(8,128)(2,1)S(1)}, u32[]{:S(2)}, u32[]{:S(2)}) collective-permute-start(bf16[128,4096]{1,0:T(8,128)(2,1)S(1)} %pad_maximum_fusion.2), channel_id=1, source_target_pairs={{0,4},{4,0},{8,12},{12,8},{1,5},{5,1},{9,13},{13,9},{2,6},{6,2},{1... | collective-permute-start | bytes 3145736 | tf_op jit(solution)/shard_map/ppermute | solution.py:30
  89.3 35.8 %collective-permute-start.21 = (bf16[128,4096]{1,0:T(8,128)(2,1)S(1)}, bf16[128,4096]{1,0:T(8,128)(2,1)S(1)}, u32[]{:S(2)}, u32[]{:S(2)}) collective-permute-start(bf16[128,4096]{1,0:T(8,128)(2,1)S(1)} %pad_maximum_fusion.3), channel_id=1, source_target_pairs={{0,48},{16,32},{32,16},{48,0},{1,49},{17,33},{33,17},{49,1},{2,50}... | collective-permute-start | bytes 3145736 | tf_op jit(solution)/shard_map/ppermute | solution.py:30
  98.1 11.3 %collective-permute-start.17 = (f32[256,256]{1,0:T(8,128)S(1)}, f32[256,256]{1,0:T(8,128)S(1)}, u32[]{:S(2)}, u32[]{:S(2)}) collective-permute-start(f32[256,256]{1,0:T(8,128)S(1)} %pad_maximum_fusion.13), channel_id=1, source_target_pairs={{0,1},{1,0},{2,3},{3,2},{4,5},{5,4},{6,7},{7,6},{8,9},{9,8},{10,11... | collective-permute-start | bytes 786440 | tf_op jit(solution)/shard_map/ppermute | solution.py:101
  109.5 17.4 %collective-permute-start.22 = (bf16[256,128]{1,0:T(8,128)(2,1)S(1)}, bf16[256,128]{1,0:T(8,128)(2,1)S(1)}, u32[]{:S(2)}, u32[]{:S(2)}) collective-permute-start(bf16[256,128]{1,0:T(8,128)(2,1)S(1)} %get-tuple-element.20), channel_id=1, source_target_pairs={{0,2},{2,0},{1,3},{3,1},{4,6},{6,4},{5,7},{7,5},{8,10},{10,8},{9,1... | collective-permute-start | bytes 196616 | tf_op jit(solution)/shard_map/ppermute | solution.py:105
  126.7 2.4 %copy-start.2 = (s32[128]{0:T(128)S(1)}, s32[128]{0:T(128)}, u32[]{:S(2)}) copy-start(s32[128]{0:T(128)} %constant.33.clone) | copy-start | bytes 1540
  126.7 2.4 %copy-start.3 = (s32[128]{0:T(128)S(1)}, s32[128]{0:T(128)}, u32[]{:S(2)}) copy-start(s32[128]{0:T(128)} %constant.32.clone) | copy-start | bytes 1540
  126.7 2.4 %copy-start.4 = (s32[128]{0:T(128)S(1)}, s32[128]{0:T(128)}, u32[]{:S(2)}) copy-start(s32[128]{0:T(128)} %constant.31.clone) | copy-start | bytes 1540
  126.8 4.2 %collective-permute-start.23 = (f32[768,256]{1,0:T(8,128)S(1)}, f32[768,256]{1,0:T(8,128)S(1)}, u32[]{:S(2)}, u32[]{:S(2)}) collective-permute-start(f32[768,256]{1,0:T(8,128)S(1)} %pad_maximum_fusion.4), channel_id=1, source_target_pairs={{0,1},{1,0},{2,3},{3,2},{4,5},{5,4},{6,7},{7,6},{8,9},{9,8},{10,11... | collective-permute-start | bytes 2359304 | tf_op jit(solution)/shard_map/ppermute | solution.py:101
  131.2 29.8 %collective-permute-start.24 = (bf16[768,128]{1,0:T(8,128)(2,1)S(1)}, bf16[768,128]{1,0:T(8,128)(2,1)S(1)}, u32[]{:S(2)}, u32[]{:S(2)}) collective-permute-start(bf16[768,128]{1,0:T(8,128)(2,1)S(1)} %get-tuple-element.17), channel_id=1, source_target_pairs={{0,2},{2,0},{1,3},{3,1},{4,6},{6,4},{5,7},{7,5},{8,10},{10,8},{9,1... | collective-permute-start | bytes 589832 | tf_op jit(solution)/shard_map/ppermute | solution.py:105
